TPU v7x, 256 devices: a whole 4x4x8 slice. The times are simulated.
256 devices in a mesh: grp: 8 (over y, z_hi), dev: 32 (over x, z_lo, core).
Axes of the slice: x: 4, y: 4, z: 8 (z_hi: 2, z_lo: 4; z = z_hi * 4 + z_lo), core: 2. Of those that a mesh axis runs over, the one named last changes fastest.
Arguments:
- doc_states: bfloat16 [2048, 128, 768], P(('grp', 'dev')), parts along dimension 0
- context_embeds: bfloat16 [4096, 768], P(('grp', 'dev')), parts along dimension 0
- w_qkv: bfloat16 [768, 2304], P('dev'), may hold values from -0.21875 to 0.21875
- w_out: bfloat16 [768, 768], P('dev'), may hold values from -0.21875 to 0.21875
- ln_gain: float32 [768], replicated, may hold values from 0.1 to 1.9
- queries: bfloat16 [2048, 768], P(('grp', 'dev')), parts along dimension 0
- positive: int32 [2048], P(('grp', 'dev')), parts along dimension 0, may hold values from 0 to 255, each once
- lengths: int32 [2048], P(('grp', 'dev')), parts along dimension 0, may hold values from 32 to 128, as said below
Outputs:
- doc_embed: bfloat16 [2048, 768], P(('grp', 'dev')), parts along dimension 0
- doc_grad: float32 [2048, 768], P(('grp', 'dev')), parts along dimension 0
- query_grad: float32 [2048, 768], P(('grp', 'dev')), parts along dimension 0
- query_loss: float32 [2048], P(('grp', 'dev')), parts along dimension 0
There are 8 independent parts, one for each index of `grp`. A program takes and returns all parts, laid end to end along the dimension named above; an argument that names none is the same for every part. Nothing has to cross between parts.
Inputs may be any that keep to these rules, and one draw needn't show every extreme that they name: `lengths`: every document has at least 32 valid tokens; the first document of the group has all 128.
All inputs are finite; a program needn't handle non-finite values.
Results may differ from a plain program's by a relative error of at most 0.0084.
Values may be sent and summed in bfloat16 or wider, within the bound.
No kernel may reach another device: no remote copies, remote signals or barrier semaphores. Data moves between devices by JAX's collectives and lax.ppermute only.
A program may use at most 64 MiB of HBM per device.

v0:
```python
import math

import jax
import jax.numpy as jnp
from jax import lax
from jax.sharding import PartitionSpec as P

HEADS = 12


contrastive_sharpness = 0.25
epsilon = 1e-05


def attend_token_block(inputs, ctx_keys, ctx_values, representation_matrix):
    block_qkv, block_lengths = inputs
    count, seq = (block_qkv.shape[0], block_qkv.shape[1])
    head_size = representation_matrix // HEADS
    multiplier = 1.0 / head_size**0.5
    query_part = block_qkv[..., :representation_matrix].reshape(count, seq, HEADS, head_size)
    key_part = block_qkv[..., representation_matrix : 2 * representation_matrix].reshape(
        count, seq, HEADS, head_size
    )
    value_part = block_qkv[..., 2 * representation_matrix :].reshape(count, seq, HEADS, head_size)
    score_ctx = (
        jnp.einsum("bshd,chd->bhsc", query_part, ctx_keys, preferred_element_type=jnp.float32)
        * multiplier
    )
    score_own = (
        jnp.einsum("bshd,bthd->bhst", query_part, key_part, preferred_element_type=jnp.float32)
        * multiplier
    )
    valid = jnp.arange(seq)[None, :] < block_lengths[:, None]
    score_own = jnp.where(valid[:, None, None, :], score_own, -jnp.inf)
    highest = jnp.maximum(
        jnp.max(score_ctx, axis=-1, keepdims=True), jnp.max(score_own, axis=-1, keepdims=True)
    )
    expo_ctx = jnp.exp(score_ctx - highest)
    expo_own = jnp.exp(score_own - highest)
    totals = jnp.sum(expo_ctx, axis=-1, keepdims=True) + jnp.sum(expo_own, axis=-1, keepdims=True)
    probs_ctx = (expo_ctx / totals).astype(jnp.bfloat16)
    probs_own = (expo_own / totals).astype(jnp.bfloat16)
    mixed = jnp.einsum("bhsc,chd->bshd", probs_ctx, ctx_values, preferred_element_type=jnp.float32)
    mixed = mixed + jnp.einsum(
        "bhst,bthd->bshd", probs_own, value_part, preferred_element_type=jnp.float32
    )
    return mixed.reshape(count, seq, representation_matrix).astype(jnp.bfloat16)


def local(doc_states, context_embeds, w_qkv, w_out, ln_gain, queries, positive, lengths):
    docs_local, seq, representation_matrix = doc_states.shape
    token_rows = doc_states.reshape(docs_local * seq, representation_matrix)
    prefix_rows = lax.all_gather(context_embeds, "dev", axis=0, tiled=True)
    piece = lax.all_gather(w_qkv, "dev", axis=0, tiled=True)
    column_indices = token_rows
    qkv_sum = jnp.dot(column_indices, piece, preferred_element_type=jnp.float32)
    prefix_sum = jnp.dot(
        prefix_rows, piece[:, representation_matrix:], preferred_element_type=jnp.float32
    )
    qkv = qkv_sum.astype(jnp.bfloat16)
    context_kv = prefix_sum.astype(jnp.bfloat16)
    ctx_count = context_kv.shape[0]
    head_size = representation_matrix // HEADS
    ctx_keys = context_kv[:, :representation_matrix].reshape(ctx_count, HEADS, head_size)
    ctx_values = context_kv[:, representation_matrix:].reshape(ctx_count, HEADS, head_size)
    block = math.gcd(docs_local, max(1, 512 // seq))
    grouped_qkv = qkv.reshape(docs_local // block, block, seq, 3 * representation_matrix)
    bucketed_durations = lengths.reshape(docs_local // block, block)
    attn = lax.map(
        lambda inputs: attend_token_block(inputs, ctx_keys, ctx_values, representation_matrix),
        (grouped_qkv, bucketed_durations),
    )
    attn = attn.reshape(docs_local * seq, representation_matrix)
    column_indices = attn
    projected = jnp.dot(
        column_indices,
        lax.all_gather(w_out, "dev", axis=0, tiled=True),
        preferred_element_type=jnp.float32,
    )
    hidden = token_rows.astype(jnp.float32) + projected
    center = jnp.mean(hidden, axis=-1, keepdims=True)
    spread = jnp.mean((hidden - center) ** 2, axis=-1, keepdims=True)
    normed = ((hidden - center) / jnp.sqrt(spread + epsilon) * ln_gain).reshape(
        docs_local, seq, representation_matrix
    )
    valid = jnp.arange(seq)[None, :] < lengths[:, None]
    pooled = (
        jnp.sum(jnp.where(valid[:, :, None], normed, 0.0), axis=1)
        / lengths.astype(jnp.float32)[:, None]
    )
    doc_embed = pooled.astype(jnp.bfloat16)
    logit_divisor = 1.0 / (representation_matrix**0.5 * contrastive_sharpness)
    batch_neighbour_encoding = lax.all_gather(doc_embed, "dev", axis=0, tiled=True)
    group_docs = batch_neighbour_encoding.shape[0]
    scores = (
        jnp.einsum(
            "qd,kd->qk", queries, batch_neighbour_encoding, preferred_element_type=jnp.float32
        )
        * logit_divisor
    )
    highest = jnp.max(scores, axis=1, keepdims=True)
    lse = highest[:, 0] + jnp.log(jnp.sum(jnp.exp(scores - highest), axis=1))
    is_positive = jnp.arange(group_docs, dtype=jnp.int32)[None, :] == positive[:, None]
    query_loss = lse - jnp.sum(jnp.where(is_positive, scores, 0.0), axis=1)
    coeff = jnp.exp(scores - lse[:, None]) - is_positive.astype(jnp.float32)
    query_grad = (
        jnp.dot(
            coeff, batch_neighbour_encoding.astype(jnp.float32), precision=lax.Precision.HIGHEST
        )
        * logit_divisor
    )
    query_float = queries.astype(jnp.float32)
    doc_grad = lax.psum_scatter(
        jnp.dot(coeff.T, query_float, precision=lax.Precision.HIGHEST) * logit_divisor,
        "dev",
        scatter_dimension=0,
        tiled=True,
    )
    return (doc_embed, doc_grad, query_grad, query_loss)


def solution(mesh):
    placed = (
        P(("grp", "dev"), None, None),
        P(("grp", "dev"), None),
        P("dev", None),
        P("dev", None),
        P(),
        P(("grp", "dev"), None),
        P(("grp", "dev")),
        P(("grp", "dev")),
    )
    return jax.shard_map(
        local,
        mesh=mesh,
        in_specs=placed,
        out_specs=(
            P(("grp", "dev"), None),
            P(("grp", "dev"), None),
            P(("grp", "dev"), None),
            P(("grp", "dev")),
        ),
        check_vma=False,
    )
```

profile of v0, /device:TPU:1, one launch (start us, length us, event | category | flops | bytes accessed | tf_op | source)
XLA Modules:
  0.0 331.6 jit_solution(12043486239860311103)
XLA Ops:
  7.2 0.7 all-gather.3.cloned.1.call-update
  8.0 0.7 all-gather.5.cloned.1.call-update
  8.7 0.7 reshape.129
  9.5 1.3 iota_compare_fusion.2
  10.7 1.2 convert_element_type.42
  11.9 50.6 %all_gather.13 = bf16[512,768]{1,0:T(8,128)(2,1)S(1)} all-gather(bf16[16,768]{1,0:T(8,128)(2,1)} %param.11), channel_id=1, replica_groups=mesh['grp'=8,'dev'=32] {'dev'}, dimensions={0}, use_global_device_ids=true | all-gather | bytes 811008 | tf_op jit(solution)/shard_map/all_gather | solution.py:53
  62.5 14.4 %all-gather.3.cloned.1.call-done = bf16[768,2304]{1,0:T(8,128)(2,1)} async-done(((bf16[24,2304]{1,0:T(8,128)(2,1)}), bf16[768,2304]{1,0:T(8,128)(2,1)}) %all-gather.3.cloned.1.call-update) | async-done | bytes 3538960 | tf_op jit(solution)/shard_map/all_gather | solution.py:54
  76.9 3.0 convolution_convert_fusion.1
  80.0 0.1 fusion.29
  80.1 0.3 copy.66
  80.4 1.2 copy.67
  81.6 8.4 %convolution_convert_fusion = bf16[1024,2304]{1,0:T(8,128)(2,1)} fusion(bf16[1024,768]{1,0:T(8,128)(2,1)} %bitcast.110, bf16[768,2304]{1,0:T(8,128)(2,1)} %all-gather.3.cloned.1.call-done), kind=kOutput, calls=%fused_computation.28 | convolution fusion | flops 3626237952 | bytes 9830400 | tf_op jit(solution)/shard_map/dot_general | solution.py:56
  90.0 41.2 %while.10 = (s32[]{:T(128)}, bf16[2,4,128,768]{3,2,1,0:T(8,128)(2,1)}, bf16[2,4,128,2304]{3,2,1,0:T(8,128)(2,1)}, bf16[512,12,64]{0,2,1:T(8,128)(2,1)S(1)}, s32[...) while((s32[]{:T(128)}, bf16[2,4,128,768]{3,2,1,0:T(8,128)(2,1)}, ...), condition=%wide.region_5.6_spmd, body=%wide.region_0.5_spmd.sunk | while | flops 1045156352 | bytes 78351008 | solution.py:69
  90.0 3.3 constant_dynamic-slice_fusion.3
  93.3 3.0 copy.102
  96.3 0.2 fusion.60
  96.6 1.0 fusion.62
  97.5 2.0 bitcast_reduce_fusion.2
  99.5 0.9 fusion.64
  100.4 2.9 fusion.63
  103.3 1.3 fusion.65
  104.6 4.6 %fusion.66 = bf16[4,128,12,64]{1,3,0,2:T(8,128)(2,1)S(1)} fusion(f32[4,12,64,128]{3,2,0,1:T(8,128)S(1)} %fusion.65, f32[12,4,128,512]{3,2,1,0:T(8,128)S(1)} %get-tuple-element.150, f32[4,12,128]{2,0,1:T(4,128)S(1)} %copy_add_fusion.2, f32[4,12,128]{2,0,1:T(4,128)S(1)} %copy_maximum_fusion.2, bf16[512,12,64]{0,2,1:T(8,128)(2,1)S(1)} %copy-done.1), kind=kOutput, calls=%fused_computation.12.clone.1 | convolution fusion | flops 416022528 | bytes 15777792 | tf_op jit(solution)/shard_map/while/body/eval_jaxpr/bhsc,chd->bshd/dot_general | solution.py:43
  109.3 0.3 copy.106
  109.6 1.0 constant_dynamic-update-slice_fusion.2
  110.6 3.3 constant_dynamic-slice_fusion.3
  113.9 3.0 copy.102
  116.9 0.2 fusion.60
  117.2 1.0 fusion.62
  118.1 2.0 bitcast_reduce_fusion.2
  120.1 0.8 fusion.64
  121.0 2.9 fusion.63
  123.9 1.3 fusion.65
  125.3 4.6 %fusion.66 = bf16[4,128,12,64]{1,3,0,2:T(8,128)(2,1)S(1)} fusion(f32[4,12,64,128]{3,2,0,1:T(8,128)S(1)} %fusion.65, f32[12,4,128,512]{3,2,1,0:T(8,128)S(1)} %get-tuple-element.150, f32[4,12,128]{2,0,1:T(4,128)S(1)} %copy_add_fusion.2, f32[4,12,128]{2,0,1:T(4,128)S(1)} %copy_maximum_fusion.2, bf16[512,12,64]{0,2,1:T(8,128)(2,1)S(1)} %copy-done.1), kind=kOutput, calls=%fused_computation.12.clone.1 | convolution fusion | flops 416022528 | bytes 15777792 | tf_op jit(solution)/shard_map/while/body/eval_jaxpr/bhsc,chd->bshd/dot_general | solution.py:43
  129.9 0.3 copy.106
  130.2 1.0 constant_dynamic-update-slice_fusion.2
  131.2 6.7 %all-gather.5.cloned.1.call-done = bf16[768,768]{1,0:T(8,128)(2,1)} async-done(((bf16[24,768]{1,0:T(8,128)(2,1)}), bf16[768,768]{1,0:T(8,128)(2,1)}) %all-gather.5.cloned.1.call-update) | async-done | bytes 1179664 | tf_op jit(solution)/shard_map/all_gather | solution.py:77
  137.9 3.8 %fusion.30 = (f32[1024]{0:T(1024)S(1)}, f32[1024,768]{1,0:T(8,128)S(1)}) fusion(bf16[1024,768]{1,0:T(8,128)(2,1)} %bitcast.112, bf16[768,768]{1,0:T(8,128)(2,1)} %all-gather.5.cloned.1.call-done, bf16[1024,768]{1,0:T(8,128)(2,1)} %bitcast.111), kind=kOutput, calls=%fused_computation.59 | convolution fusion | flops 1210317824 | bytes 7475200 | tf_op jit(solution)/shard_map/dot_general | solution.py:75
  141.7 0.5 multiply_reduce_fusion
  142.3 0.1 copy-done.3
  142.4 0.8 select_reduce_fusion
  143.2 0.1 divide_convert_fusion.5
  143.3 42.2 %all_gather.15 = bf16[256,768]{1,0:T(8,128)(2,1)S(1)} all-gather(bf16[8,768]{1,0:T(8,128)(2,1)S(1)} %divide_convert_fusion.5), channel_id=1, replica_groups=mesh['grp'=8,'dev'=32] {'dev'}, dimensions={0}, use_global_device_ids=true | all-gather | bytes 405504 | tf_op jit(solution)/shard_map/all_gather | solution.py:93
  185.5 0.4 fusion.31
  185.9 0.2 fusion.20
  186.1 0.5 fusion.27
  186.6 1.5 convolution_multiply_fusion
  188.1 0.9 convolution_multiply_fusion.1
  189.1 135.9 %reduce-scatter.2.cloned.1.call-done = f32[8,768]{1,0:T(8,128)} async-done(((f32[256,768]{1,0:T(8,128)}), f32[8,768]{1,0:T(8,128)}) %reduce-scatter.2.cloned.1.call-update) | async-done | bytes 24592 | tf_op jit(solution)/shard_map/reduce_scatter | solution.py:113
  (36 shorter events, 0.6 us)
Async XLA Ops:
  7.2 178.4 %copy-start = (bf16[8,768]{1,0:T(8,128)(2,1)S(1)}, bf16[8,768]{1,0:T(8,128)(2,1)}, u32[]{:S(2)}) copy-start(bf16[8,768]{1,0:T(8,128)(2,1)} %param.15) | copy-start | bytes 36868
  7.2 69.8 %all-gather.3.cloned.1.call-start = ((), (), s32[]{:S(2)}) async-start(), calls=%async_computation.1 | async-start | bytes 3649536 | tf_op jit(solution)/shard_map/all_gather | solution.py:54
  7.9 130.0 %all-gather.5.cloned.1.call-start = ((), (), s32[]{:S(2)}) async-start(), calls=%async_computation.2 | async-start | bytes 1216512 | tf_op jit(solution)/shard_map/all_gather | solution.py:77
  8.7 316.4 %reduce-scatter.2.cloned.1.call-start = ((), (), s32[]{:S(2)}) async-start(), calls=%async_computation.3 | async-start | bytes 811008 | tf_op jit(solution)/shard_map/reduce_scatter | solution.py:113
  103.3 1.3 copy-start.1
  123.9 1.3 copy-start.1
  141.7 0.7 copy-start.3
  141.7 0.7 copy-start.5
  141.7 1.5 copy-start.6
  141.7 44.1 %copy-start.4 = (s32[8]{0:T(128)S(1)}, s32[8]{0:T(128)}, u32[]{:S(2)}) copy-start(s32[8]{0:T(128)} %param.16) | copy-start | bytes 100
  143.3 181.7 %copy-start.2 = (bf16[8,768]{1,0:T(8,128)(2,1)}, bf16[8,768]{1,0:T(8,128)(2,1)S(1)}, u32[]{:S(2)}) copy-start(bf16[8,768]{1,0:T(8,128)(2,1)S(1)} %divide_convert_fusion.5) | copy-start | bytes 36868
Sparse Core Ops, SparseCore 0:
  9.9 67.0 all-gather.2
  78.8 59.0 all-gather.4
  188.3 136.7 reduce-scatter.1
where the time goes:
time: 336 us; the launch traced here: 332 us
  waiting for transfers between devices  158 us (47%)
  blocking collectives  92.8 us (28%)
  matrix products  35.7 us (11%)
  local copies, waits for them, and re-layouts  18.1 us (5%)
  between operations  13.9 us (4%)
  other arithmetic  12.3 us (4%)
    reduce_scatter x1, waiting for transfers between devices, local(): lax.psum_scatter(jnp.dot(coeff.T, query_float, precision=lax.Precision.HI...  136 us
    all_gather x1, blocking collectives, local(): prefix_rows = lax.all_gather(context_embeds, 'dev', axis=0, tiled=True)  50.6 us
    all_gather x1, blocking collectives, local(): lax.all_gather(doc_embed, 'dev', axis=0, tiled=True)  42.2 us
    all_gather x1, waiting for transfers between devices, local(): piece = lax.all_gather(w_qkv, 'dev', axis=0, tiled=True)  14.4 us
    dynamic_slice x4, local copies, waits for them, and re-layouts, local(): lax.map(lambda inputs: attend_token_block(inputs, ctx_keys, ctx_values, r...  12.6 us
    dot_general x2, matrix products, attend_token_block(): jnp.einsum('bhsc,chd->bshd', probs_ctx, ctx_values, preferred_element_typ...  9.15 us
    dot_general x1, matrix products, local(): qkv_sum = jnp.dot(column_indices, piece, preferred_element_type=jnp.float32)  8.43 us
  transfers between devices with their start and end apart: 3, of which 3 were waited for; matrix products, arithmetic and copies ran while one was open for 18% of the time, Pallas kernels for 0%

commit v1 on v0

v1 whole, which is shorter than its diff:
```python
import functools

import jax
import jax.numpy as jnp
from jax import lax
from jax.experimental import pallas as pl
from jax.experimental.pallas import tpu as pltpu
from jax.sharding import PartitionSpec as P

HEAD = 64
PAIR = 128
SHARPNESS = 0.25
EPSILON = 1e-5
LOG2E = 1.4426950408889634
F32 = jnp.float32
BF16 = jnp.bfloat16
VMEM_LIMIT = 56 * 2**20
NT = (((1,), (1,)), ((), ()))


def halves(tile):
    low = lax.broadcasted_iota(jnp.int32, (1, PAIR), 1) < HEAD
    zero = jnp.zeros_like(tile)
    return jnp.where(low, tile, zero).astype(BF16), jnp.where(low, zero, tile).astype(BF16)


def ones_beside(rows):
    low = lax.broadcasted_iota(jnp.int32, (1, PAIR), 1) < HEAD
    first = lax.broadcasted_iota(jnp.int32, (2 * rows, 1), 0) < rows
    return jnp.where(jnp.logical_xor(first, low), 0.0, 1.0).astype(BF16)


def attend_kernel(rows, unroll, len_ref, x_ref, ctx_ref, w_ref, o_ref, q_s, k_s, v_s, kc_s, vc_s):
    pairs, docs, two_seq, _ = k_s.shape
    seq = two_seq // 2
    width = pairs * PAIR
    blocks, ctx_rows, hidden = ctx_ref.shape
    nctx = blocks * 16
    scale = LOG2E / HEAD**0.5

    def project(i, _):
        r = pl.ds(pl.multiple_of(i * rows, rows), rows)
        states = x_ref[r, :]
        q = jnp.dot(states, w_ref[:, :width], preferred_element_type=F32)
        q_s[r, :] = (q * scale).astype(BF16)
        for begin, out in ((width, k_s), (2 * width, v_s)):
            t = jnp.dot(states, w_ref[:, begin : begin + width], preferred_element_type=F32)
            for j in range(pairs):
                even, odd = halves(t[:, j * PAIR : (j + 1) * PAIR])
                for e in range(rows // seq):
                    d = i * (rows // seq) + e
                    out[j, d, :seq] = even[e * seq : (e + 1) * seq]
                    out[j, d, seq:] = odd[e * seq : (e + 1) * seq]
        return 0

    lax.fori_loop(0, docs * seq // rows, project, 0)
    ctx = ctx_ref[:, :16, :].reshape(nctx, hidden)
    for begin, out in ((width, kc_s), (2 * width, vc_s)):
        t = jnp.dot(ctx, w_ref[:, begin : begin + width], preferred_element_type=F32)
        for j in range(pairs):
            even, odd = halves(t[:, j * PAIR : (j + 1) * PAIR])
            out[j, :nctx] = even
            out[j, nctx:] = odd
    ones_ctx = ones_beside(nctx)
    ones_own = ones_beside(seq)
    slot = lax.broadcasted_iota(jnp.int32, (1, 2 * seq), 1)
    slot = jnp.where(slot < seq, slot, slot - seq)
    for j in range(pairs):

        def doc(d, _):
            r = pl.ds(pl.multiple_of(d * seq, seq), seq)
            q = q_s[r, j * PAIR : (j + 1) * PAIR]
            bias = jnp.where(slot < len_ref[d], 0.0, -jnp.inf).astype(F32)
            score_ctx = lax.dot_general(q, kc_s[j], NT, preferred_element_type=F32)
            score_own = lax.dot_general(q, k_s[j, d], NT, preferred_element_type=F32) + bias
            p_ctx, p_own = [], []
            for e in range(2):
                c = score_ctx[:, e * nctx : (e + 1) * nctx]
                o = score_own[:, e * seq : (e + 1) * seq]
                top = jnp.maximum(jnp.max(c, axis=1, keepdims=True), jnp.max(o, axis=1, keepdims=True))
                p_ctx.append(jnp.exp2(c - top).astype(BF16))
                p_own.append(jnp.exp2(o - top).astype(BF16))
            mixed = jnp.dot(
                jnp.concatenate(p_ctx, axis=1),
                jnp.concatenate([vc_s[j], ones_ctx], axis=1),
                preferred_element_type=F32,
            ) + jnp.dot(
                jnp.concatenate(p_own, axis=1),
                jnp.concatenate([v_s[j, d], ones_own], axis=1),
                preferred_element_type=F32,
            )
            o_ref[r, j * PAIR : (j + 1) * PAIR] = (mixed[:, :PAIR] / mixed[:, PAIR:]).astype(BF16)
            return 0

        lax.fori_loop(0, docs, doc, 0, unroll=unroll)


def attend(lengths, x, ctx, w, seq):
    tokens, hidden = x.shape
    docs = tokens // seq
    width = w.shape[1] // 3
    pairs = width // PAIR
    nctx = ctx.shape[0] * 16
    vmem = pl.BlockSpec(memory_space=pltpu.VMEM)
    flops = 2 * tokens * hidden * 3 * width + 2 * nctx * hidden * 2 * width + 4 * tokens * (nctx + seq) * width
    return pl.pallas_call(
        functools.partial(attend_kernel, 2 * seq, docs),
        out_shape=jax.ShapeDtypeStruct((tokens, width), BF16),
        in_specs=[pl.BlockSpec(memory_space=pltpu.SMEM), vmem, vmem, vmem],
        out_specs=vmem,
        scratch_shapes=[
            pltpu.VMEM((tokens, width), BF16),
            pltpu.VMEM((pairs, docs, 2 * seq, PAIR), BF16),
            pltpu.VMEM((pairs, docs, 2 * seq, PAIR), BF16),
            pltpu.VMEM((pairs, 2 * nctx, PAIR), BF16),
            pltpu.VMEM((pairs, 2 * nctx, PAIR), BF16),
        ],
        compiler_params=pltpu.CompilerParams(vmem_limit_bytes=VMEM_LIMIT),
        cost_estimate=pl.CostEstimate(flops=flops, bytes_accessed=8 * 2**20, transcendentals=tokens * (nctx + seq) * 2 * pairs),
        name="attend",
    )(lengths, x, ctx, w)


def pool_kernel(seq, len_ref, x_ref, attn_ref, w_ref, gain_ref, o_ref):
    docs = o_ref.shape[0]
    hidden = x_ref.shape[1]
    position = lax.broadcasted_iota(jnp.int32, (seq, 1), 0)
    pooled = []
    for d in range(docs):
        r = slice(d * seq, (d + 1) * seq)
        h = x_ref[r, :].astype(F32) + jnp.dot(attn_ref[r, :], w_ref[...], preferred_element_type=F32)
        center = jnp.mean(h, axis=1, keepdims=True)
        off = h - center
        spread = jnp.mean(off * off, axis=1, keepdims=True)
        length = len_ref[d]
        weight = jnp.where(position < length, lax.rsqrt(spread + EPSILON), 0.0)
        pooled.append(jnp.sum(off * weight, axis=0, keepdims=True) / length.astype(F32))
    o_ref[...] = (jnp.concatenate(pooled, axis=0) * gain_ref[...]).astype(BF16)


def pool(lengths, x, attn, w_out, gain, seq):
    tokens, hidden = x.shape
    vmem = pl.BlockSpec(memory_space=pltpu.VMEM)
    return pl.pallas_call(
        functools.partial(pool_kernel, seq),
        out_shape=jax.ShapeDtypeStruct((tokens // seq, hidden), BF16),
        in_specs=[pl.BlockSpec(memory_space=pltpu.SMEM), vmem, vmem, vmem, vmem],
        out_specs=vmem,
        compiler_params=pltpu.CompilerParams(vmem_limit_bytes=VMEM_LIMIT),
        cost_estimate=pl.CostEstimate(flops=2 * tokens * hidden * hidden, bytes_accessed=5 * 2**20, transcendentals=0),
        name="pool",
    )(lengths, x, attn, w_out, gain.reshape(1, hidden))


def exact_dot(a, b):
    a1 = a.astype(BF16)
    rest = a - a1.astype(F32)
    a2 = rest.astype(BF16)
    a3 = (rest - a2.astype(F32)).astype(BF16)
    n = a.shape[0]
    out = jnp.dot(jnp.concatenate([a1, a2, a3], axis=0), b, preferred_element_type=F32)
    return out[:n] + out[n : 2 * n] + out[2 * n :]


def contrast_kernel(me_ref, pack_ref, embed_ref, dgrad_ref, qgrad_ref, loss_ref, coeff_s):
    blocks, rows, hidden = pack_ref.shape
    docs = embed_ref.shape[0]
    mine = docs // blocks
    cols = blocks * 16
    me = me_ref[0]
    divisor = 1.0 / (hidden**0.5 * SHARPNESS)
    packed = pack_ref[:, 16:, :].reshape(cols, hidden)
    embed = embed_ref[...]
    lane = lax.broadcasted_iota(jnp.int32, (1, cols), 1)
    picker = jnp.where(lane % 16 == mine, 1.0, 0.0) * jnp.ones((16, 1), F32)
    positive = jnp.dot(picker.astype(BF16), packed[:, :cols], preferred_element_type=F32)[:1]
    scores_t = lax.dot_general(embed, packed, NT, preferred_element_type=F32) * divisor
    top = jnp.max(scores_t, axis=0, keepdims=True)
    lse_t = top + jnp.log(jnp.sum(jnp.exp(scores_t - top), axis=0, keepdims=True))
    doc_id = lax.broadcasted_iota(jnp.int32, (docs, 1), 0).astype(F32)
    coeff_t = jnp.exp(scores_t - lse_t) - jnp.where(doc_id == positive, 1.0, 0.0)
    coeff_s[...] = jnp.where(lane % 16 < mine, coeff_t, 0.0)
    own_t = coeff_s[pl.ds(pl.multiple_of(me * mine, mine), mine), :]
    dgrad_ref[...] = exact_dot(own_t, packed) * divisor
    queries = pack_ref[pl.ds(me, 1), 16:, :].reshape(16, hidden)
    scores = lax.dot_general(queries, embed, NT, preferred_element_type=F32) * divisor
    top = jnp.max(scores, axis=1, keepdims=True)
    lse = top + jnp.log(jnp.sum(jnp.exp(scores - top), axis=1, keepdims=True))
    row = lax.broadcasted_iota(jnp.int32, (16, 1), 0)
    own_positive = jnp.sum(jnp.where(lane == me * 16 + row, positive, 0.0), axis=1, keepdims=True)
    is_positive = lax.broadcasted_iota(jnp.int32, (1, docs), 1).astype(F32) == own_positive
    loss = lse - jnp.sum(jnp.where(is_positive, scores, 0.0), axis=1, keepdims=True)
    coeff = jnp.exp(scores - lse) - jnp.where(is_positive, 1.0, 0.0)
    qgrad_ref[...] = exact_dot(coeff, embed)[:mine] * divisor
    spot = lax.broadcasted_iota(jnp.int32, (1, PAIR), 1)
    loss_ref[...] = jnp.sum(jnp.where(spot == row, loss, 0.0), axis=0, keepdims=True)[:, :mine]


def contrast(me, pack, embed):
    blocks, rows, hidden = pack.shape
    docs = embed.shape[0]
    mine = docs // blocks
    vmem = pl.BlockSpec(memory_space=pltpu.VMEM)
    return pl.pallas_call(
        contrast_kernel,
        out_shape=(
            jax.ShapeDtypeStruct((mine, hidden), F32),
            jax.ShapeDtypeStruct((mine, hidden), F32),
            jax.ShapeDtypeStruct((1, mine), F32),
        ),
        in_specs=[pl.BlockSpec(memory_space=pltpu.SMEM), vmem, vmem],
        out_specs=(vmem, vmem, vmem),
        scratch_shapes=[pltpu.VMEM((docs, blocks * 16), F32)],
        compiler_params=pltpu.CompilerParams(vmem_limit_bytes=VMEM_LIMIT),
        name="contrast",
    )(me, pack, embed)


def spread_all(block, axis, size):
    return lax.all_to_all(jnp.broadcast_to(block[None], (size,) + block.shape), axis, 0, 0)


def pack_kernel(me_ref, positive_ref, context_ref, query_ref, o_ref):
    mine, hidden = query_ref.shape
    spot = lax.broadcasted_iota(jnp.int32, (8, hidden), 1) - 16 * me_ref[0]
    first = lax.broadcasted_iota(jnp.int32, (8, hidden), 0) == 0
    rows = jnp.zeros((8, hidden), F32)
    for i in range(mine):
        rows = jnp.where(jnp.logical_and(spot == i, first), positive_ref[i].astype(F32), rows)
    o_ref[:16] = context_ref[...]
    o_ref[16:] = jnp.concatenate([query_ref[...].astype(F32), rows], axis=0).astype(BF16)


def pack_rows(me, context, queries, positive):
    hidden = queries.shape[1]
    smem = pl.BlockSpec(memory_space=pltpu.SMEM)
    vmem = pl.BlockSpec(memory_space=pltpu.VMEM)
    return pl.pallas_call(
        pack_kernel,
        out_shape=jax.ShapeDtypeStruct((32, hidden), BF16),
        in_specs=[smem, smem, vmem, vmem],
        out_specs=vmem,
        name="pack",
    )(me, positive, context, queries)


def local(doc_states, context_embeds, w_qkv, w_out, ln_gain, queries, positive, lengths):
    docs, seq, hidden = doc_states.shape
    size = lax.axis_size("dev")
    me = lax.axis_index("dev")
    x = doc_states.reshape(docs * seq, hidden)
    pack = spread_all(pack_rows(me.reshape(1), context_embeds, queries, positive), "dev", size)
    weights = lax.all_gather(jnp.concatenate([w_qkv, w_out], axis=1), "dev", axis=0, tiled=True)
    attn = attend(lengths, x, pack, weights[:, : 3 * hidden], seq)
    embed = pool(lengths, x, attn, weights[:, 3 * hidden :], ln_gain, seq)
    embeds = spread_all(embed, "dev", size).reshape(size * docs, hidden)
    dgrad, qgrad, loss = contrast(me.reshape(1), pack, embeds)
    return embed, dgrad, qgrad, loss.reshape(docs)


def solution(mesh):
    both = ("grp", "dev")
    return jax.shard_map(
        local,
        mesh=mesh,
        in_specs=(
            P(both, None, None),
            P(both, None),
            P("dev", None),
            P("dev", None),
            P(),
            P(both, None),
            P(both),
            P(both),
        ),
        out_specs=(P(both, None), P(both, None), P(both, None), P(both)),
        check_vma=False,
    )
```

time: 336 us -> 157 us (0.47); the launches traced: 332 us -> 156 us
  waiting for transfers between devices: 158 us -> 71.7 us
  blocking collectives: 92.8 us -> 19 us
  matrix products: 35.7 us -> 0 us
  Pallas kernels: 0 us -> 28.5 us
  other arithmetic: 12.3 us -> 1.59 us
  starting transfers between devices: 0.11 us -> 10.2 us
  local copies, waits for them, and re-layouts: 18.1 us -> 11.1 us
    reduce_scatter x1 -> x0, waiting for transfers between devices: 136 us -> none  [local(): lax.psum_scatter(jnp.dot(coeff.T, query_float, precision=lax.Precision.HI...]
    all_gather x2 -> x0, blocking collectives: 92.8 us -> none  [the longest x1 50.6 us: local(): prefix_rows = lax.all_gather(context_embeds, 'dev', axis=0, tiled=True)]
    all_gather x2 -> x1, waiting for transfers between devices: 21.2 us -> 71.7 us  [local(): lax.all_gather(jnp.concatenate([w_qkv, w_out], axis=1), 'dev', axis=0, ti...]
    dot_general x14 -> x0, matrix products: 35.7 us -> none  [the longest x2 9.15 us: attend_token_block(): jnp.einsum('bhsc,chd->bshd', probs_ctx, ctx_values, preferred_element_typ...]
    pallas_call x0 -> x4, Pallas kernels: none -> 28.5 us  [the longest x1 18.9 us: attend(): pl.pallas_call(functools.partial(attend_kernel, 2 * seq, docs), out_shape...]
    all_to_all x0 -> x1, blocking collectives: none -> 19 us  [spread_all(): lax.all_to_all(jnp.broadcast_to(block[None], (size,) + block.shape), axis...]
    dynamic_slice x4 -> x0, local copies, waits for them, and re-layouts: 12.6 us -> none  [local(): lax.map(lambda inputs: attend_token_block(inputs, ctx_keys, ctx_values, r...]
    all_to_all x0 -> x1, starting transfers between devices: none -> 10.2 us  [spread_all(): lax.all_to_all(jnp.broadcast_to(block[None], (size,) + block.shape), axis...]
  transfers between devices with their start and end apart: 3 -> 2, of which waited for: 3 -> 1; matrix products, arithmetic and copies ran while one was open for 18% -> 6% of each run, Pallas kernels for 0% -> 1%
where the time goes in v1:
time: 157 us; the launch traced here: 156 us
  waiting for transfers between devices  71.7 us (46%)
  Pallas kernels  28.5 us (18%)
  blocking collectives  19 us (12%)
  between operations  14.1 us (9%)
  local copies, waits for them, and re-layouts  11.1 us (7%)
  starting transfers between devices  10.2 us (6%)
  other arithmetic  1.59 us (1%)
    all_gather x1, waiting for transfers between devices, local(): lax.all_gather(jnp.concatenate([w_qkv, w_out], axis=1), 'dev', axis=0, ti...  71.7 us
    all_to_all x1, blocking collectives, spread_all(): lax.all_to_all(jnp.broadcast_to(block[None], (size,) + block.shape), axis...  19 us
    pallas_call x1, Pallas kernels, attend(): pl.pallas_call(functools.partial(attend_kernel, 2 * seq, docs), out_shape...  18.9 us
    all_to_all x1, starting transfers between devices, spread_all(): lax.all_to_all(jnp.broadcast_to(block[None], (size,) + block.shape), axis...  10.2 us
    pallas_call x1, Pallas kernels, pool(): pl.pallas_call(functools.partial(pool_kernel, seq), out_shape=jax.ShapeDt...  4.65 us
    slice x1, local copies, waits for them, and re-layouts, local(): attn = attend(lengths, x, pack, weights[:, :3 * hidden], seq)  4 us
    pallas_call x1, Pallas kernels, contrast(): pl.pallas_call(contrast_kernel, out_shape=(jax.ShapeDtypeStruct((mine, hi...  3.55 us
  transfers between devices with their start and end apart: 2, of which 1 were waited for; matrix products, arithmetic and copies ran while one was open for 6% of the time, Pallas kernels for 1%

profile of v1, /device:TPU:1, one launch (start us, length us, event | category | flops | bytes accessed | tf_op | source)
XLA Modules:
  0.0 156.1 jit_solution(14505135632498095232)
XLA Ops:
  7.2 0.0 all-gather.2.cloned.1.call-start
  7.2 1.6 %pad_maximum_fusion = bf16[24,3072]{1,0:T(8,128)(2,1)} fusion(bf16[24,768]{1,0:T(8,128)(2,1)} %param.11, bf16[24,2304]{1,0:T(8,128)(2,1)} %param.10), kind=kLoop, calls=%fused_computation | loop fusion | flops 294912 | bytes 294912 | tf_op jit(solution)/shard_map/concatenate | solution.py:253
  8.8 0.0 all-gather.2.cloned.1.call-update
  8.8 1.4 pack.1
  10.2 2.2 %broadcast_in_dim.4 = bf16[32,32,768]{2,1,0:T(8,128)(2,1)} broadcast(bf16[32,768]{1,0:T(8,128)(2,1)} %pack.1), dimensions={1,2} | broadcast | bytes 1622016 | tf_op jit(solution)/shard_map/broadcast_in_dim | solution.py:220
  12.4 0.0 copy-start.1
  12.4 10.2 %all-to-all-start = ((bf16[32,32,768]{2,1,0:T(8,128)(2,1)}), bf16[32,32,768]{2,1,0:T(8,128)(2,1)S(1)}, u32[]{:S(2)}, u32[]{:S(2)}) async-start(bf16[32,32,768]{2,1,0:T(8,128)(2,1)} %broadcast_in_dim.4), calls=%async_computation | async-start | bytes 3145728 | tf_op jit(solution)/shard_map/all_to_all | solution.py:220
  22.6 0.0 copy-done.1
  22.6 0.6 reshape.28.gain_ref
  23.2 71.7 %all-gather.2.cloned.1.call-done = bf16[768,3072]{1,0:T(8,128)(2,1)} async-done(((bf16[24,3072]{1,0:T(8,128)(2,1)}), bf16[768,3072]{1,0:T(8,128)(2,1)}) %all-gather.2.cloned.1.call-update) | async-done | bytes 4718608 | tf_op jit(solution)/shard_map/all_gather | solution.py:253
  94.9 2.4 %slice.9.w_ref = bf16[768,768]{1,0:T(8,128)(2,1)} slice(bf16[768,3072]{1,0:T(8,128)(2,1)} %all-gather.2.cloned.1.call-done), slice={[0:768], [2304:3072]} | slice | bytes 2359296 | tf_op jit(solution)/shard_map/slice | solution.py:255
  97.3 4.0 %slice.8.w_ref = bf16[768,2304]{1,0:T(8,128)(2,1)} slice(bf16[768,3072]{1,0:T(8,128)(2,1)} %all-gather.2.cloned.1.call-done), slice={[0:768], [0:2304]} | slice | bytes 7077888 | tf_op jit(solution)/shard_map/slice | solution.py:254
  101.3 0.0 all-to-all-done.ctx_ref.pack_ref
  101.3 0.0 copy-start
  101.3 1.1 copy-done
  102.4 18.9 %attend.1.attn_ref = bf16[1024,768]{1,0:T(8,128)(2,1)} custom-call(s32[8]{0:T(128)} %len_ref.3, bf16[1024,768]{1,0:T(8,128)(2,1)} %bitcast.5, bf16[32,32,768]{2,1,0:T(8,128)(2,1)} %copy-done, bf16[768,2304]{1,0:T(8,128)(2,1)} %slice.8.w_ref), custom_call_target="tpu_custom_call" | custom-call | flops 6845104128 | bytes 8388608 | tf_op jit(solution)/shard_map/attend/pallas_call | solution.py:106
  121.3 4.6 %pool.1 = bf16[8,768]{1,0:T(8,128)(2,1)} custom-call(s32[8]{0:T(128)} %len_ref.3, bf16[1024,768]{1,0:T(8,128)(2,1)} %bitcast.6, bf16[1024,768]{1,0:T(8,128)(2,1)} %attend.1.attn_ref, bf16[768,768]{1,0:T(8,128)(2,1)} %slice.9.w_ref, f32[1,768]{1,0:T(1,128)} %reshape.28.gain_ref), custom_call_target="tpu_custom_call" | custom-call | flops 1207959552 | bytes 5242880 | tf_op jit(solution)/shard_map/pool/pallas_call | solution.py:144
  126.0 0.7 broadcast_in_dim.5
  126.7 19.0 %all_to_all.10 = bf16[32,8,768]{2,1,0:T(8,128)(2,1)} all-to-all(bf16[32,8,768]{2,1,0:T(8,128)(2,1)S(1)} %broadcast_in_dim.5), channel_id=1, replica_groups=mesh['grp'=8,'dev'=32] {'dev'}, dimensions={0} | all-to-all | bytes 786432 | tf_op jit(solution)/shard_map/all_to_all | solution.py:220
  145.7 3.6 %contrast.1 = (f32[8,768]{1,0:T(8,128)}, f32[8,768]{1,0:T(8,128)}, f32[1,8]{1,0:T(1,128)}) custom-call(s32[1]{0:T(128)} %bitcast.1.me_ref, bf16[32,32,768]{2,1,0:T(8,128)(2,1)} %copy-done, bf16[256,768]{1,0:T(8,128)(2,1)} %bitcast.4), custom_call_target="tpu_custom_call" | custom-call | tf_op jit(solution)/shard_map/contrast/pallas_call | solution.py:204
Async XLA Ops:
  7.2 87.7 %all-gather.2.cloned.1.call-start = ((), (), s32[]{:S(2)}) async-start(), calls=%async_computation.2 | async-start | bytes 4866048 | tf_op jit(solution)/shard_map/all_gather | solution.py:253
  12.4 10.2 %copy-start.1 = (f32[768]{0:T(1024)S(1)}, f32[768]{0:T(1024)}, u32[]{:S(2)}) copy-start(f32[768]{0:T(1024)} %param.12) | copy-start | bytes 9220
  12.4 88.9 %all-to-all-start = ((bf16[32,32,768]{2,1,0:T(8,128)(2,1)}), bf16[32,32,768]{2,1,0:T(8,128)(2,1)S(1)}, u32[]{:S(2)}, u32[]{:S(2)}) async-start(bf16[32,32,768]{2,1,0:T(8,128)(2,1)} %broadcast_in_dim.4), calls=%async_computation | async-start | bytes 3145728 | tf_op jit(solution)/shard_map/all_to_all | solution.py:220
  101.3 1.1 copy-start
Sparse Core Ops, SparseCore 0:
  9.9 85.0 all-gather.1

commit v2 on v1

v2 whole, which is shorter than its diff:
```python
import functools

import jax
import jax.numpy as jnp
from jax import lax
from jax.experimental import pallas as pl
from jax.experimental.pallas import tpu as pltpu
from jax.sharding import PartitionSpec as P

HEAD = 64
PAIR = 128
SHARPNESS = 0.25
EPSILON = 1e-5
LOG2E = 1.4426950408889634
F32 = jnp.float32
BF16 = jnp.bfloat16
VMEM_LIMIT = 56 * 2**20
NT = (((1,), (1,)), ((), ()))


def halves(tile):
    low = lax.broadcasted_iota(jnp.int32, (1, PAIR), 1) < HEAD
    zero = jnp.zeros_like(tile)
    return jnp.where(low, tile, zero).astype(BF16), jnp.where(low, zero, tile).astype(BF16)


def ones_beside(rows):
    low = lax.broadcasted_iota(jnp.int32, (1, PAIR), 1) < HEAD
    first = lax.broadcasted_iota(jnp.int32, (2 * rows, 1), 0) < rows
    return jnp.where(jnp.logical_xor(first, low), 0.0, 1.0).astype(BF16)


HALF = 384
WEIGHTS = 3 * HALF
PROJECT = 4 * HALF
ROWS = 5 * HALF
BLOCK = ROWS + 128
SMALL = ((0, 0), (2, 1), (0, 2), (2, 3))
LARGE = ((0, 0), (1, 0), (3, 0), (0, 1))


def half_block(half, positive_ref, context_ref, query_ref, wqkv_ref, wout_ref):
    mine, hidden = query_ref.shape
    first = half == 0
    parts = [wqkv_ref[:, b * hidden : (b + 1) * hidden].astype(F32) for b in range(3)] + [wout_ref[...].astype(F32)]
    parts.append(jnp.concatenate([context_ref[...].astype(F32), query_ref[...].astype(F32)], axis=0))
    parts = [jnp.where(first, p[:, :HALF], p[:, HALF:]) for p in parts]
    row = lax.broadcasted_iota(jnp.int32, (24, 128), 0)
    spot = jnp.zeros((24, 128), F32)
    for i in range(mine):
        spot = jnp.where(row == 16 + i, positive_ref[i].astype(F32), spot)
    return jnp.concatenate(parts + [spot], axis=1)


def give_kernel(spot_ref, positive_ref, context_ref, query_ref, wqkv_ref, wout_ref, o_ref):
    block = half_block(1 - spot_ref[1], positive_ref, context_ref, query_ref, wqkv_ref, wout_ref)
    o_ref[...] = block.astype(BF16)


def chip_kernel(spot_ref, positive_ref, context_ref, query_ref, wqkv_ref, wout_ref, got_ref, o_ref):
    own = half_block(spot_ref[1], positive_ref, context_ref, query_ref, wqkv_ref, wout_ref)
    got = got_ref[...].astype(F32)
    first = spot_ref[1] == 0
    low = jnp.where(first, own, got)
    high = jnp.where(first, got, own)
    o_ref[:, :PROJECT] = jnp.concatenate([low[:, :PROJECT], high[:, :PROJECT]], axis=0).astype(BF16)
    rows = [low[:16, PROJECT:], high[:16, PROJECT:], low[16:, PROJECT:], high[16:, PROJECT:]]
    o_ref[:, PROJECT:] = jnp.concatenate(rows, axis=0).astype(BF16)


def build(kernel, rows, name, spot, positive, *arrays):
    smem = pl.BlockSpec(memory_space=pltpu.SMEM)
    vmem = pl.BlockSpec(memory_space=pltpu.VMEM)
    return pl.pallas_call(
        kernel,
        out_shape=jax.ShapeDtypeStruct((rows, BLOCK), BF16),
        in_specs=[smem, smem] + [vmem] * len(arrays),
        out_specs=vmem,
        name=name,
    )(spot, positive, *arrays)


def layer_kernel(rows, unroll, len_ref, spot_ref, x_ref, gain_ref, *refs):
    pieces, refs = refs[:8], refs[8:]
    o_ref, told_ref, w_s, wo_s, ctx_s, query_s, spot_s, q_s, k_s, v_s, kc_s, vc_s, attn_s, sems = refs
    tokens, hidden = x_ref.shape
    docs = o_ref.shape[0]
    seq = tokens // docs
    pairs = hidden // PAIR
    per = HALF // PAIR
    nctx = ctx_s.shape[1] * ctx_s.shape[2]
    scale = LOG2E / HEAD**0.5
    x, core, z = spot_ref[0], spot_ref[1], spot_ref[2]
    weights, others, last = [], [], []
    for side in range(2):
        for p, (ax, az) in enumerate(LARGE):
            piece = pieces[side * 4 + p]
            n = side * 4 + p
            for k, (bx, bz) in enumerate(SMALL):
                at = pl.multiple_of((((x + ax + bx) & 3) * 4 + ((z + az + bz) & 3)) * 48, 48)
                here = (core + side) & 1
                lanes = pl.ds(pl.multiple_of(here * HALF, HALF), HALF)
                weights.append(
                    pltpu.make_async_copy(
                        piece.at[k, :, pl.ds(0, WEIGHTS)], w_s.at[side, pl.ds(at, 48)], sems.at[0, n * 4 + k]
                    )
                )
                last.append(
                    pltpu.make_async_copy(
                        piece.at[k, :, pl.ds(WEIGHTS, HALF)], wo_s.at[pl.ds(at, 48), lanes], sems.at[1, n * 4 + k]
                    )
                )
            others.append(
                pltpu.make_async_copy(
                    piece.at[:, pl.ds(0, 32), pl.ds(PROJECT, HALF)], ctx_s.at[side, pl.ds(4 * p, 4)], sems.at[2, n]
                )
            )
            last.append(
                pltpu.make_async_copy(
                    piece.at[:, pl.ds(32, 16), pl.ds(PROJECT, HALF)], query_s.at[side, pl.ds(4 * p, 4)], sems.at[2, 8 + n]
                )
            )
            if side == 0:
                last.append(
                    pltpu.make_async_copy(
                        piece.at[:, pl.ds(32, 16), pl.ds(ROWS, 128)], spot_s.at[pl.ds(4 * p, 4)], sems.at[2, 16 + n]
                    )
                )
    for copy in weights + others + last:
        copy.start()
    for copy in weights:
        copy.wait()

    def project(i, _):
        r = pl.ds(pl.multiple_of(i * rows, rows), rows)
        states = x_ref[r, :]
        for side in range(2):
            q = jnp.dot(states, w_s[side, :, :HALF], preferred_element_type=F32)
            q_s[r, side * HALF : (side + 1) * HALF] = (q * scale).astype(BF16)
            for begin, out in ((HALF, k_s), (2 * HALF, v_s)):
                t = jnp.dot(states, w_s[side, :, begin : begin + HALF], preferred_element_type=F32)
                for j in range(per):
                    even, odd = halves(t[:, j * PAIR : (j + 1) * PAIR])
                    for e in range(rows // seq):
                        d = i * (rows // seq) + e
                        out[side * per + j, d, :seq] = even[e * seq : (e + 1) * seq]
                        out[side * per + j, d, seq:] = odd[e * seq : (e + 1) * seq]
        return 0

    lax.fori_loop(0, tokens // rows, project, 0)
    for copy in others:
        copy.wait()
    near = ctx_s[0].reshape(nctx, HALF)
    far = ctx_s[1].reshape(nctx, HALF)
    first = core == 0
    ctx = jnp.concatenate([jnp.where(first, near, far), jnp.where(first, far, near)], axis=1)
    for side in range(2):
        for begin, out in ((HALF, kc_s), (2 * HALF, vc_s)):
            t = jnp.dot(ctx, w_s[side, :, begin : begin + HALF], preferred_element_type=F32)
            for j in range(per):
                even, odd = halves(t[:, j * PAIR : (j + 1) * PAIR])
                out[side * per + j, :nctx] = even
                out[side * per + j, nctx:] = odd
    ones_ctx = ones_beside(nctx)
    ones_own = ones_beside(seq)
    slot = lax.broadcasted_iota(jnp.int32, (1, 2 * seq), 1)
    slot = jnp.where(slot < seq, slot, slot - seq)
    for j in range(pairs):

        def doc(d, _):
            r = pl.ds(pl.multiple_of(d * seq, seq), seq)
            q = q_s[r, j * PAIR : (j + 1) * PAIR]
            bias = jnp.where(slot < len_ref[d], 0.0, -jnp.inf).astype(F32)
            score_ctx = lax.dot_general(q, kc_s[j], NT, preferred_element_type=F32)
            score_own = lax.dot_general(q, k_s[j, d], NT, preferred_element_type=F32) + bias
            p_ctx, p_own = [], []
            for e in range(2):
                c = score_ctx[:, e * nctx : (e + 1) * nctx]
                o = score_own[:, e * seq : (e + 1) * seq]
                top = jnp.maximum(jnp.max(c, axis=1, keepdims=True), jnp.max(o, axis=1, keepdims=True))
                p_ctx.append(jnp.exp2(c - top).astype(BF16))
                p_own.append(jnp.exp2(o - top).astype(BF16))
            mixed = jnp.dot(
                jnp.concatenate(p_ctx, axis=1),
                jnp.concatenate([vc_s[j], ones_ctx], axis=1),
                preferred_element_type=F32,
            ) + jnp.dot(
                jnp.concatenate(p_own, axis=1),
                jnp.concatenate([v_s[j, d], ones_own], axis=1),
                preferred_element_type=F32,
            )
            attn_s[r, j * PAIR : (j + 1) * PAIR] = (mixed[:, :PAIR] / mixed[:, PAIR:]).astype(BF16)
            return 0

        lax.fori_loop(0, docs, doc, 0, unroll=unroll)
    for copy in last:
        copy.wait()
    w_near = wo_s[pl.ds(pl.multiple_of(core * HALF, HALF), HALF), :]
    w_far = wo_s[pl.ds(pl.multiple_of((1 - core) * HALF, HALF), HALF), :]
    position = lax.broadcasted_iota(jnp.int32, (seq, 1), 0)
    pooled = []
    for d in range(docs):
        r = slice(d * seq, (d + 1) * seq)
        h = x_ref[r, :].astype(F32) + jnp.dot(attn_s[r, :HALF], w_near, preferred_element_type=F32)
        h = h + jnp.dot(attn_s[r, HALF:], w_far, preferred_element_type=F32)
        center = jnp.mean(h, axis=1, keepdims=True)
        off = h - center
        spread = jnp.mean(off * off, axis=1, keepdims=True)
        length = len_ref[d]
        weight = jnp.where(position < length, lax.rsqrt(spread + EPSILON), 0.0)
        pooled.append(jnp.sum(off * weight, axis=0, keepdims=True) / length.astype(F32))
    o_ref[...] = (jnp.concatenate(pooled, axis=0) * gain_ref[...]).astype(BF16)
    count = told_ref.shape[0]
    near = query_s[0].reshape(count, HALF)
    far = query_s[1].reshape(count, HALF)
    told_ref[:, :HALF] = jnp.where(first, near, far)
    told_ref[:, HALF:hidden] = jnp.where(first, far, near)
    told_ref[:, hidden:] = spot_s[...].reshape(count, 128)


def layer(lengths, spot, x, gain, pieces, seq):
    tokens, hidden = x.shape
    docs = tokens // seq
    pairs = hidden // PAIR
    chips = 16
    nctx = chips * 32
    vmem = pl.BlockSpec(memory_space=pltpu.VMEM)
    smem = pl.BlockSpec(memory_space=pltpu.SMEM)
    hbm = pl.BlockSpec(memory_space=pl.ANY)
    return pl.pallas_call(
        functools.partial(layer_kernel, 2 * seq, docs),
        out_shape=(
            jax.ShapeDtypeStruct((docs, hidden), BF16),
            jax.ShapeDtypeStruct((chips * 16, hidden + 128), BF16),
        ),
        in_specs=[smem, smem, vmem, vmem] + [hbm] * 8,
        out_specs=(vmem, vmem),
        scratch_shapes=[
            pltpu.VMEM((2, hidden, WEIGHTS), BF16),
            pltpu.VMEM((hidden, hidden), BF16),
            pltpu.VMEM((2, chips, 32, HALF), BF16),
            pltpu.VMEM((2, chips, 16, HALF), BF16),
            pltpu.VMEM((chips, 16, 128), BF16),
            pltpu.VMEM((tokens, hidden), BF16),
            pltpu.VMEM((pairs, docs, 2 * seq, PAIR), BF16),
            pltpu.VMEM((pairs, docs, 2 * seq, PAIR), BF16),
            pltpu.VMEM((pairs, 2 * nctx, PAIR), BF16),
            pltpu.VMEM((pairs, 2 * nctx, PAIR), BF16),
            pltpu.VMEM((tokens, hidden), BF16),
            pltpu.SemaphoreType.DMA((3, 32)),
        ],
        compiler_params=pltpu.CompilerParams(vmem_limit_bytes=VMEM_LIMIT),
        name="layer",
    )(lengths, spot, x, gain.reshape(1, hidden), *pieces)


def exact_dot(a, b):
    a1 = a.astype(BF16)
    rest = a - a1.astype(F32)
    a2 = rest.astype(BF16)
    a3 = (rest - a2.astype(F32)).astype(BF16)
    n = a.shape[0]
    out = jnp.dot(jnp.concatenate([a1, a2, a3], axis=0), b, preferred_element_type=F32)
    return out[:n] + out[n : 2 * n] + out[2 * n :]


def contrast_kernel(spot_ref, told_ref, embed_ref, dgrad_ref, qgrad_ref, loss_ref, coeff_s, rows_s, loss_s):
    count = told_ref.shape[0]
    docs, hidden = embed_ref.shape
    mine = dgrad_ref.shape[0]
    divisor = 1.0 / (hidden**0.5 * SHARPNESS)
    core = spot_ref[1]
    queries = told_ref[:, :hidden]
    embed = embed_ref[...]
    beside = told_ref[:, hidden:].astype(F32)
    positive = beside.T[:1]
    scores_t = lax.dot_general(embed, queries, NT, preferred_element_type=F32) * divisor
    top = jnp.max(scores_t, axis=0, keepdims=True)
    lse_t = top + jnp.log(jnp.sum(jnp.exp(scores_t - top), axis=0, keepdims=True))
    doc_id = lax.broadcasted_iota(jnp.int32, (docs, 1), 0).astype(F32)
    coeff_s[...] = jnp.exp(scores_t - lse_t) - jnp.where(doc_id == positive, 1.0, 0.0)
    own = pl.multiple_of(((spot_ref[0] * 4 + spot_ref[2]) * 2 + core) * mine, mine)
    dgrad_ref[...] = exact_dot(coeff_s[pl.ds(own, mine), :], queries) * divisor
    scores = lax.dot_general(queries[:16], embed, NT, preferred_element_type=F32) * divisor
    top = jnp.max(scores, axis=1, keepdims=True)
    lse = top + jnp.log(jnp.sum(jnp.exp(scores - top), axis=1, keepdims=True))
    is_positive = lax.broadcasted_iota(jnp.int32, (1, docs), 1).astype(F32) == beside[:16, :1]
    loss = lse - jnp.sum(jnp.where(is_positive, scores, 0.0), axis=1, keepdims=True)
    rows_s[...] = jnp.exp(scores - lse) - jnp.where(is_positive, 1.0, 0.0)
    half = pl.ds(pl.multiple_of(core * mine, mine), mine)
    qgrad_ref[...] = exact_dot(rows_s[half, :], embed) * divisor
    loss_s[...] = jnp.broadcast_to(loss, loss_s.shape)
    spot = lax.broadcasted_iota(jnp.int32, (mine, 128), 1)
    row = lax.broadcasted_iota(jnp.int32, (mine, 128), 0)
    loss_ref[...] = jnp.sum(jnp.where(spot == row, loss_s[half, :], 0.0), axis=0, keepdims=True)[:, :mine]


def contrast(spot, told, embed, mine):
    count = told.shape[0]
    docs, hidden = embed.shape
    vmem = pl.BlockSpec(memory_space=pltpu.VMEM)
    return pl.pallas_call(
        contrast_kernel,
        out_shape=(
            jax.ShapeDtypeStruct((mine, hidden), F32),
            jax.ShapeDtypeStruct((mine, hidden), F32),
            jax.ShapeDtypeStruct((1, mine), F32),
        ),
        in_specs=[pl.BlockSpec(memory_space=pltpu.SMEM), vmem, vmem],
        out_specs=(vmem, vmem, vmem),
        scratch_shapes=[
            pltpu.VMEM((docs, count), F32),
            pltpu.VMEM((16, docs), F32),
            pltpu.VMEM((16, 128), F32),
        ],
        compiler_params=pltpu.CompilerParams(vmem_limit_bytes=VMEM_LIMIT),
        name="contrast",
    )(spot, told, embed)


def spread_all(block, axis, size):
    return lax.all_to_all(jnp.broadcast_to(block[None], (size,) + block.shape), axis, 0, 0)


def fetch(value, dx=0, dz=0, dcore=0):
    moves = [
        ((x + dx) % 4 * 8 + (z + dz) % 4 * 2 + (core ^ dcore), x * 8 + z * 2 + core)
        for x in range(4)
        for z in range(4)
        for core in range(2)
    ]
    return lax.ppermute(value, "dev", moves)


def local(doc_states, context_embeds, w_qkv, w_out, ln_gain, queries, positive, lengths):
    docs, seq, hidden = doc_states.shape
    size = lax.axis_size("dev")
    me = lax.axis_index("dev")
    spot = jnp.stack([me >> 3, me & 1, (me >> 1) & 3])
    x = doc_states.reshape(docs * seq, hidden)
    arrays = (context_embeds, queries, w_qkv, w_out)
    got = fetch(build(give_kernel, 24, "give", spot, positive, *arrays), dcore=1)
    block = build(chip_kernel, 48, "chip", spot, positive, *arrays, got)
    four = jnp.stack([block] + [fetch(block, dx, dz) for dx, dz in SMALL[1:]])
    near = [four] + [fetch(four, dx, dz) for dx, dz in LARGE[1:]]
    far = [fetch(piece, dcore=1) for piece in near]
    embed, told = layer(lengths, spot, x, ln_gain, near + far, seq)
    embeds = spread_all(embed, "dev", size).reshape(size * docs, hidden)
    dgrad, qgrad, loss = contrast(spot, told, embeds, docs)
    return embed, dgrad, qgrad, loss.reshape(docs)


def solution(mesh):
    both = ("grp", "dev")
    return jax.shard_map(
        local,
        mesh=mesh,
        in_specs=(
            P(both, None, None),
            P(both, None),
            P("dev", None),
            P("dev", None),
            P(),
            P(both, None),
            P(both),
            P(both),
        ),
        out_specs=(P(both, None), P(both, None), P(both, None), P(both)),
        check_vma=False,
    )
```

time: 157 us -> 106 us (0.68)
  waiting for transfers between devices: 71.7 us -> 28 us
  between operations: 14.1 us -> 0.73 us
  starting transfers between devices: 10.2 us -> 23.5 us
  local copies, waits for them, and re-layouts: 11.1 us -> 2.94 us
  Pallas kernels: 28.5 us -> 30.5 us
    all_gather x1 -> x0, waiting for transfers between devices: 71.7 us -> none  [local(): lax.all_gather(jnp.concatenate([w_qkv, w_out], axis=1), 'dev', axis=0, ti...]
    ppermute x0 -> x11, waiting for transfers between devices: none -> 28 us  [fetch(): return lax.ppermute(value, 'dev', moves)]
    ppermute x0 -> x11, starting transfers between devices: none -> 23.5 us  [fetch(): return lax.ppermute(value, 'dev', moves)]
    all_to_all x1 -> x0, starting transfers between devices: 10.2 us -> none  [spread_all(): lax.all_to_all(jnp.broadcast_to(block[None], (size,) + block.shape), axis...]
    slice x2 -> x0, local copies, waits for them, and re-layouts: 6.38 us -> none  [the longest x1 4 us: local(): attn = attend(lengths, x, pack, weights[:, :3 * hidden], seq)]
    pallas_call x3, Pallas kernels: 24.9 us -> 27.4 us  [the longest x1 24.1 us: layer(): pl.pallas_call(functools.partial(layer_kernel, 2 * seq, docs), out_shape=...]
    broadcast_in_dim x2 -> x1, local copies, waits for them, and re-layouts: 2.94 us -> 0.74 us  [spread_all(): jnp.broadcast_to(block[None], (size,) + block.shape)]
    another operation x0 -> x2, other arithmetic: none -> 1.7 us  [the longest x1 1.03 us: local(): four = jnp.stack([block] + [fetch(block, dx, dz) for dx, dz in SMALL[1:]])]
  transfers between devices with their start and end apart: 2 -> 11, of which waited for: 1 -> 7; matrix products, arithmetic and copies ran while one was open for 6% -> 1% of each run, Pallas kernels for 1% -> 0%
where the time goes in v2:
time: 106 us
  Pallas kernels  30.5 us (29%)
  waiting for transfers between devices  28 us (26%)
  starting transfers between devices  23.5 us (22%)
  blocking collectives  18.4 us (17%)
  local copies, waits for them, and re-layouts  2.94 us (3%)
  other arithmetic  1.7 us (2%)
    ppermute x11, waiting for transfers between devices, fetch(): return lax.ppermute(value, 'dev', moves)  28 us
    pallas_call x1, Pallas kernels, layer(): pl.pallas_call(functools.partial(layer_kernel, 2 * seq, docs), out_shape=...  24.1 us
    ppermute x11, starting transfers between devices, fetch(): return lax.ppermute(value, 'dev', moves)  23.5 us
    all_to_all x1, blocking collectives, spread_all(): lax.all_to_all(jnp.broadcast_to(block[None], (size,) + block.shape), axis...  18.4 us
    pallas_call x2, Pallas kernels, build(): pl.pallas_call(kernel, out_shape=jax.ShapeDtypeStruct((rows, BLOCK), BF16...  3.35 us
    pallas_call x1, Pallas kernels, contrast(): pl.pallas_call(contrast_kernel, out_shape=(jax.ShapeDtypeStruct((mine, hi...  3.05 us
  transfers between devices with their start and end apart: 11, of which 7 were waited for; matrix products, arithmetic and copies ran while one was open for 1% of the time, Pallas kernels for 0%

profile of v2, /device:TPU:1, one launch (start us, length us, event | category | flops | bytes accessed | tf_op | source)
XLA Modules:
  0.0 105.8 jit_solution(12052368362621025559)
XLA Ops:
  0.6 0.0 copy-start.9
  0.6 0.7 pad_add_fusion.spot_ref
  1.3 1.6 %give.1 = bf16[24,2048]{1,0:T(8,128)(2,1)} custom-call(s32[3]{0:T(128)} %pad_add_fusion.spot_ref, s32[8]{0:T(128)} %positive_ref.3, bf16[16,768]{1,0:T(8,128)(2,1)} %context_ref.3, bf16[8,768]{1,0:T(8,128)(2,1)} %query_ref.3, bf16[24,2304]{1,0:T(8,128)(2,1)} %wqkv_ref.3, bf16[24,768]{1,0:T(8,128)(2,1)} %wout_ref.3), custom_call_target="tpu_custom_call" | custom-call | tf_op jit(solution)/shard_map/give/pallas_call | solution.py:74
  2.9 3.2 %collective-permute-start = (bf16[24,2048]{1,0:T(8,128)(2,1)}, bf16[24,2048]{1,0:T(8,128)(2,1)S(1)}, u32[]{:S(2)}, u32[]{:S(2)}) collective-permute-start(bf16[24,2048]{1,0:T(8,128)(2,1)} %give.1), channel_id=1, source_target_pairs={{1,0},{0,1},{3,2},{2,3},{5,4},{4,5},{7,6},{6,7},{9,8},{8,9},{11,10... | collective-permute-start | bytes 294920 | tf_op jit(solution)/shard_map/ppermute | solution.py:332
  6.2 1.2 %collective-permute-done.got_ref = bf16[24,2048]{1,0:T(8,128)(2,1)S(1)} collective-permute-done((bf16[24,2048]{1,0:T(8,128)(2,1)}, bf16[24,2048]{1,0:T(8,128)(2,1)S(1)}, u32[]{:S(2)}, u32[]{:S(2)}) %collective-permute-start) | collective-permute-done | bytes 98336 | tf_op jit(solution)/shard_map/ppermute | solution.py:332
  7.3 0.0 copy-start.8
  7.3 0.6 copy-done.8
  8.0 1.7 %chip.1 = bf16[48,2048]{1,0:T(8,128)(2,1)} custom-call(s32[3]{0:T(128)} %pad_add_fusion.spot_ref, s32[8]{0:T(128)} %positive_ref.3, bf16[16,768]{1,0:T(8,128)(2,1)} %context_ref.3, bf16[8,768]{1,0:T(8,128)(2,1)} %query_ref.3, bf16[24,2304]{1,0:T(8,128)(2,1)} %wqkv_ref.3, bf16[24,768]{1,0:T(8,128)(2,1)} %wout_ref.3, bf16[24,2048]{1,0:T(8,128)(2,1)} %copy-done.8), custom_call_target="tpu_custom_call" | custom-call | tf_op jit(solution)/shard_map/chip/pallas_call | solution.py:74
  9.7 2.4 %collective-permute-start.3 = (bf16[48,2048]{1,0:T(8,128)(2,1)}, bf16[48,2048]{1,0:T(8,128)(2,1)S(1)}, u32[]{:S(2)}, u32[]{:S(2)}) collective-permute-start(bf16[48,2048]{1,0:T(8,128)(2,1)} %chip.1), channel_id=1, source_target_pairs={{22,0},{23,1},{16,2},{17,3},{18,4},{19,5},{20,6},{21,7},{30,8},{31... | collective-permute-start | bytes 589832 | tf_op jit(solution)/shard_map/ppermute | solution.py:332
  12.1 3.0 %collective-permute-start.2 = (bf16[48,2048]{1,0:T(8,128)(2,1)}, bf16[48,2048]{1,0:T(8,128)(2,1)S(1)}, u32[]{:S(2)}, u32[]{:S(2)}) collective-permute-start(bf16[48,2048]{1,0:T(8,128)(2,1)} %chip.1), channel_id=1, source_target_pairs={{4,0},{5,1},{6,2},{7,3},{0,4},{1,5},{2,6},{3,7},{12,8},{13,9},{14,... | collective-permute-start | bytes 589832 | tf_op jit(solution)/shard_map/ppermute | solution.py:332
  15.1 0.7 collective-permute-start.1
  15.7 4.6 %collective-permute-done.3 = bf16[48,2048]{1,0:T(8,128)(2,1)S(1)} collective-permute-done((bf16[48,2048]{1,0:T(8,128)(2,1)}, bf16[48,2048]{1,0:T(8,128)(2,1)S(1)}, u32[]{:S(2)}, u32[]{:S(2)}) %collective-permute-start.3) | collective-permute-done | bytes 196640 | tf_op jit(solution)/shard_map/ppermute | solution.py:332
  20.3 7.4 %collective-permute-done.2 = bf16[48,2048]{1,0:T(8,128)(2,1)S(1)} collective-permute-done((bf16[48,2048]{1,0:T(8,128)(2,1)}, bf16[48,2048]{1,0:T(8,128)(2,1)S(1)}, u32[]{:S(2)}, u32[]{:S(2)}) %collective-permute-start.2) | collective-permute-done | bytes 196640 | tf_op jit(solution)/shard_map/ppermute | solution.py:332
  27.7 0.0 collective-permute-done.1
  27.7 1.0 pad_maximum_fusion.refs_0_
  28.7 0.0 copy-start
  28.8 5.7 %collective-permute-start.6 = (bf16[4,48,2048]{2,1,0:T(8,128)(2,1)S(1)}, bf16[4,48,2048]{2,1,0:T(8,128)(2,1)S(1)}, u32[]{:S(2)}, u32[]{:S(2)}) collective-permute-start(bf16[4,48,2048]{2,1,0:T(8,128)(2,1)S(1)} %pad_maximum_fusion.refs_0_), channel_id=1, source_target_pairs={{2,0},{3,1},{4,2},{5,3},{6,4},{7,5},{0,6},{1,7},{10,8},{11,9},{12,... | collective-permute-start | bytes 2359304 | tf_op jit(solution)/shard_map/ppermute | solution.py:332
  34.4 0.3 collective-permute-start.5
  34.7 2.4 %collective-permute-start.4 = (bf16[4,48,2048]{2,1,0:T(8,128)(2,1)S(1)}, bf16[4,48,2048]{2,1,0:T(8,128)(2,1)S(1)}, u32[]{:S(2)}, u32[]{:S(2)}) collective-permute-start(bf16[4,48,2048]{2,1,0:T(8,128)(2,1)S(1)} %pad_maximum_fusion.refs_0_), channel_id=1, source_target_pairs={{8,0},{9,1},{10,2},{11,3},{12,4},{13,5},{14,6},{15,7},{16,8},{17,9... | collective-permute-start | bytes 2359304 | tf_op jit(solution)/shard_map/ppermute | solution.py:332
  37.1 2.0 %collective-permute-start.7 = (bf16[4,48,2048]{2,1,0:T(8,128)(2,1)S(1)}, bf16[4,48,2048]{2,1,0:T(8,128)(2,1)S(1)}, u32[]{:S(2)}, u32[]{:S(2)}) collective-permute-start(bf16[4,48,2048]{2,1,0:T(8,128)(2,1)S(1)} %pad_maximum_fusion.refs_0_), channel_id=1, source_target_pairs={{1,0},{0,1},{3,2},{2,3},{5,4},{4,5},{7,6},{6,7},{9,8},{8,9},{11,10... | collective-permute-start | bytes 2359304 | tf_op jit(solution)/shard_map/ppermute | solution.py:332
  39.1 12.3 %collective-permute-done.6.refs_3_ = bf16[4,48,2048]{2,1,0:T(8,128)(2,1)S(1)} collective-permute-done((bf16[4,48,2048]{2,1,0:T(8,128)(2,1)S(1)}, bf16[4,48,2048]{2,1,0:T(8,128)(2,1)S(1)}, u32[]{:S(2)}, u32[]{:S(2)}) %collective-permute-start.6) | collective-permute-done | bytes 786464 | tf_op jit(solution)/shard_map/ppermute | solution.py:332
  51.5 0.0 copy-start.1
  51.5 1.4 %collective-permute-start.10 = (bf16[4,48,2048]{2,1,0:T(8,128)(2,1)S(1)}, bf16[4,48,2048]{2,1,0:T(8,128)(2,1)S(1)}, u32[]{:S(2)}, u32[]{:S(2)}) collective-permute-start(bf16[4,48,2048]{2,1,0:T(8,128)(2,1)S(1)} %collective-permute-done.6.refs_3_), channel_id=1, source_target_pairs={{1,0},{0,1},{3,2},{2,3},{5,4},{4,5},{7,6},{6,7},{9,8},{8,9},{11,10... | collective-permute-start | bytes 2359304 | tf_op jit(solution)/shard_map/ppermute | solution.py:332
  52.8 0.4 collective-permute-done.5.refs_2_
  53.2 2.4 %collective-permute-start.9 = (bf16[4,48,2048]{2,1,0:T(8,128)(2,1)S(1)}, bf16[4,48,2048]{2,1,0:T(8,128)(2,1)S(1)}, u32[]{:S(2)}, u32[]{:S(2)}) collective-permute-start(bf16[4,48,2048]{2,1,0:T(8,128)(2,1)S(1)} %collective-permute-done.5.refs_2_), channel_id=1, source_target_pairs={{1,0},{0,1},{3,2},{2,3},{5,4},{4,5},{7,6},{6,7},{9,8},{8,9},{11,10... | collective-permute-start | bytes 2359304 | tf_op jit(solution)/shard_map/ppermute | solution.py:332
  55.6 0.0 collective-permute-done.4.refs_1_
  55.6 0.0 copy-start.3
  55.6 0.1 collective-permute-start.8
  55.7 0.0 copy-done.9
  55.7 0.7 reshape.22.gain_ref
  56.4 0.0 collective-permute-done.7.refs_4_
  56.4 0.0 copy-start.4
  56.4 0.0 collective-permute-done.10.refs_7_
  56.4 0.0 copy-start.5
  56.4 1.1 %collective-permute-done.9.refs_6_ = bf16[4,48,2048]{2,1,0:T(8,128)(2,1)S(1)} collective-permute-done((bf16[4,48,2048]{2,1,0:T(8,128)(2,1)S(1)}, bf16[4,48,2048]{2,1,0:T(8,128)(2,1)S(1)}, u32[]{:S(2)}, u32[]{:S(2)}) %collective-permute-start.9) | collective-permute-done | bytes 786464 | tf_op jit(solution)/shard_map/ppermute | solution.py:332
  57.5 1.1 %collective-permute-done.8.refs_5_ = bf16[4,48,2048]{2,1,0:T(8,128)(2,1)S(1)} collective-permute-done((bf16[4,48,2048]{2,1,0:T(8,128)(2,1)S(1)}, bf16[4,48,2048]{2,1,0:T(8,128)(2,1)S(1)}, u32[]{:S(2)}, u32[]{:S(2)}) %collective-permute-start.8) | collective-permute-done | bytes 786464 | tf_op jit(solution)/shard_map/ppermute | solution.py:332
  58.6 0.0 copy-done
  58.6 0.0 copy-done.1
  58.6 0.0 copy-done.2
  58.6 0.0 copy-done.3
  58.7 0.0 copy-done.4
  58.7 0.0 copy-done.5
  58.7 0.0 copy-done.6
  58.7 0.8 copy-done.7
  59.5 24.1 %layer.1 = (bf16[8,768]{1,0:T(8,128)(2,1)}, bf16[256,896]{1,0:T(8,128)(2,1)}) custom-call(s32[8]{0:T(128)} %len_ref.1, s32[3]{0:T(128)} %pad_add_fusion.spot_ref, bf16[1024,768]{1,0:T(8,128)(2,1)} %bitcast.10, f32[1,768]{1,0:T(1,128)} %reshape.22.gain_ref, bf16[4,48,2048]{2,1,0:T(8,128)(2,1)} %copy-done, bf16[4,48,2048]{2,1,0:T(8,128)(2,1)} %copy-done.3, ...), custom_call_target="tpu_custom_call" | custom-call | tf_op jit(solution)/shard_map/layer/pallas_call | solution.py:230
  83.6 0.7 broadcast_in_dim.2
  84.3 18.4 %all_to_all.5 = bf16[32,8,768]{2,1,0:T(8,128)(2,1)} all-to-all(bf16[32,8,768]{2,1,0:T(8,128)(2,1)S(1)} %broadcast_in_dim.2), channel_id=1, replica_groups=mesh['grp'=8,'dev'=32] {'dev'}, dimensions={0} | all-to-all | bytes 786432 | tf_op jit(solution)/shard_map/all_to_all | solution.py:322
  102.7 3.1 %contrast.1 = (f32[8,768]{1,0:T(8,128)}, f32[8,768]{1,0:T(8,128)}, f32[1,8]{1,0:T(1,128)}) custom-call(s32[3]{0:T(128)} %pad_add_fusion.spot_ref, bf16[256,896]{1,0:T(8,128)(2,1)} %get-tuple-element.10.told_ref, bf16[256,768]{1,0:T(8,128)(2,1)} %bitcast.11), custom_call_target="tpu_custom_call" | custom-call | tf_op jit(solution)/shard_map/contrast/pallas_call | solution.py:302
  (3 shorter events, 0.0 us)
Async XLA Ops:
  0.6 55.1 %copy-start.9 = (f32[768]{0:T(1024)S(1)}, f32[768]{0:T(1024)}, u32[]{:S(2)}) copy-start(f32[768]{0:T(1024)} %param.12) | copy-start | bytes 9220
  2.9 4.4 %collective-permute-start = (bf16[24,2048]{1,0:T(8,128)(2,1)}, bf16[24,2048]{1,0:T(8,128)(2,1)S(1)}, u32[]{:S(2)}, u32[]{:S(2)}) collective-permute-start(bf16[24,2048]{1,0:T(8,128)(2,1)} %give.1), channel_id=1, source_target_pairs={{1,0},{0,1},{3,2},{2,3},{5,4},{4,5},{7,6},{6,7},{9,8},{8,9},{11,10... | collective-permute-start | bytes 294920 | tf_op jit(solution)/shard_map/ppermute | solution.py:332
  7.3 0.6 copy-start.8
  9.7 10.6 %collective-permute-start.3 = (bf16[48,2048]{1,0:T(8,128)(2,1)}, bf16[48,2048]{1,0:T(8,128)(2,1)S(1)}, u32[]{:S(2)}, u32[]{:S(2)}) collective-permute-start(bf16[48,2048]{1,0:T(8,128)(2,1)} %chip.1), channel_id=1, source_target_pairs={{22,0},{23,1},{16,2},{17,3},{18,4},{19,5},{20,6},{21,7},{30,8},{31... | collective-permute-start | bytes 589832 | tf_op jit(solution)/shard_map/ppermute | solution.py:332
  12.1 15.6 %collective-permute-start.2 = (bf16[48,2048]{1,0:T(8,128)(2,1)}, bf16[48,2048]{1,0:T(8,128)(2,1)S(1)}, u32[]{:S(2)}, u32[]{:S(2)}) collective-permute-start(bf16[48,2048]{1,0:T(8,128)(2,1)} %chip.1), channel_id=1, source_target_pairs={{4,0},{5,1},{6,2},{7,3},{0,4},{1,5},{2,6},{3,7},{12,8},{13,9},{14,... | collective-permute-start | bytes 589832 | tf_op jit(solution)/shard_map/ppermute | solution.py:332
  15.1 12.7 %collective-permute-start.1 = (bf16[48,2048]{1,0:T(8,128)(2,1)}, bf16[48,2048]{1,0:T(8,128)(2,1)S(1)}, u32[]{:S(2)}, u32[]{:S(2)}) collective-permute-start(bf16[48,2048]{1,0:T(8,128)(2,1)} %chip.1), channel_id=1, source_target_pairs={{18,0},{19,1},{20,2},{21,3},{22,4},{23,5},{16,6},{17,7},{26,8},{27... | collective-permute-start | bytes 589832 | tf_op jit(solution)/shard_map/ppermute | solution.py:332
  28.7 29.9 %copy-start = (bf16[4,48,2048]{2,1,0:T(8,128)(2,1)}, bf16[4,48,2048]{2,1,0:T(8,128)(2,1)S(1)}, u32[]{:S(2)}) copy-start(bf16[4,48,2048]{2,1,0:T(8,128)(2,1)S(1)} %pad_maximum_fusion.refs_0_) | copy-start | bytes 2359300
  28.8 22.7 %collective-permute-start.6 = (bf16[4,48,2048]{2,1,0:T(8,128)(2,1)S(1)}, bf16[4,48,2048]{2,1,0:T(8,128)(2,1)S(1)}, u32[]{:S(2)}, u32[]{:S(2)}) collective-permute-start(bf16[4,48,2048]{2,1,0:T(8,128)(2,1)S(1)} %pad_maximum_fusion.refs_0_), channel_id=1, source_target_pairs={{2,0},{3,1},{4,2},{5,3},{6,4},{7,5},{0,6},{1,7},{10,8},{11,9},{12,... | collective-permute-start | bytes 2359304 | tf_op jit(solution)/shard_map/ppermute | solution.py:332
  34.4 18.8 %collective-permute-start.5 = (bf16[4,48,2048]{2,1,0:T(8,128)(2,1)S(1)}, bf16[4,48,2048]{2,1,0:T(8,128)(2,1)S(1)}, u32[]{:S(2)}, u32[]{:S(2)}) collective-permute-start(bf16[4,48,2048]{2,1,0:T(8,128)(2,1)S(1)} %pad_maximum_fusion.refs_0_), channel_id=1, source_target_pairs={{24,0},{25,1},{26,2},{27,3},{28,4},{29,5},{30,6},{31,7},{0,8},{1,9... | collective-permute-start | bytes 2359304 | tf_op jit(solution)/shard_map/ppermute | solution.py:332
  34.7 20.9 %collective-permute-start.4 = (bf16[4,48,2048]{2,1,0:T(8,128)(2,1)S(1)}, bf16[4,48,2048]{2,1,0:T(8,128)(2,1)S(1)}, u32[]{:S(2)}, u32[]{:S(2)}) collective-permute-start(bf16[4,48,2048]{2,1,0:T(8,128)(2,1)S(1)} %pad_maximum_fusion.refs_0_), channel_id=1, source_target_pairs={{8,0},{9,1},{10,2},{11,3},{12,4},{13,5},{14,6},{15,7},{16,8},{17,9... | collective-permute-start | bytes 2359304 | tf_op jit(solution)/shard_map/ppermute | solution.py:332
  37.1 19.3 %collective-permute-start.7 = (bf16[4,48,2048]{2,1,0:T(8,128)(2,1)S(1)}, bf16[4,48,2048]{2,1,0:T(8,128)(2,1)S(1)}, u32[]{:S(2)}, u32[]{:S(2)}) collective-permute-start(bf16[4,48,2048]{2,1,0:T(8,128)(2,1)S(1)} %pad_maximum_fusion.refs_0_), channel_id=1, source_target_pairs={{1,0},{0,1},{3,2},{2,3},{5,4},{4,5},{7,6},{6,7},{9,8},{8,9},{11,10... | collective-permute-start | bytes 2359304 | tf_op jit(solution)/shard_map/ppermute | solution.py:332
  51.5 7.2 %copy-start.1 = (bf16[4,48,2048]{2,1,0:T(8,128)(2,1)}, bf16[4,48,2048]{2,1,0:T(8,128)(2,1)S(1)}, u32[]{:S(2)}) copy-start(bf16[4,48,2048]{2,1,0:T(8,128)(2,1)S(1)} %collective-permute-done.6.refs_3_) | copy-start | bytes 2359300
  51.5 5.0 %collective-permute-start.10 = (bf16[4,48,2048]{2,1,0:T(8,128)(2,1)S(1)}, bf16[4,48,2048]{2,1,0:T(8,128)(2,1)S(1)}, u32[]{:S(2)}, u32[]{:S(2)}) collective-permute-start(bf16[4,48,2048]{2,1,0:T(8,128)(2,1)S(1)} %collective-permute-done.6.refs_3_), channel_id=1, source_target_pairs={{1,0},{0,1},{3,2},{2,3},{5,4},{4,5},{7,6},{6,7},{9,8},{8,9},{11,10... | collective-permute-start | bytes 2359304 | tf_op jit(solution)/shard_map/ppermute | solution.py:332
  53.2 5.4 %copy-start.2 = (bf16[4,48,2048]{2,1,0:T(8,128)(2,1)}, bf16[4,48,2048]{2,1,0:T(8,128)(2,1)S(1)}, u32[]{:S(2)}) copy-start(bf16[4,48,2048]{2,1,0:T(8,128)(2,1)S(1)} %collective-permute-done.5.refs_2_) | copy-start | bytes 2359300
  53.2 4.3 %collective-permute-start.9 = (bf16[4,48,2048]{2,1,0:T(8,128)(2,1)S(1)}, bf16[4,48,2048]{2,1,0:T(8,128)(2,1)S(1)}, u32[]{:S(2)}, u32[]{:S(2)}) collective-permute-start(bf16[4,48,2048]{2,1,0:T(8,128)(2,1)S(1)} %collective-permute-done.5.refs_2_), channel_id=1, source_target_pairs={{1,0},{0,1},{3,2},{2,3},{5,4},{4,5},{7,6},{6,7},{9,8},{8,9},{11,10... | collective-permute-start | bytes 2359304 | tf_op jit(solution)/shard_map/ppermute | solution.py:332
  55.6 3.0 %copy-start.3 = (bf16[4,48,2048]{2,1,0:T(8,128)(2,1)}, bf16[4,48,2048]{2,1,0:T(8,128)(2,1)S(1)}, u32[]{:S(2)}) copy-start(bf16[4,48,2048]{2,1,0:T(8,128)(2,1)S(1)} %collective-permute-done.4.refs_1_) | copy-start | bytes 2359300
  55.6 3.0 %collective-permute-start.8 = (bf16[4,48,2048]{2,1,0:T(8,128)(2,1)S(1)}, bf16[4,48,2048]{2,1,0:T(8,128)(2,1)S(1)}, u32[]{:S(2)}, u32[]{:S(2)}) collective-permute-start(bf16[4,48,2048]{2,1,0:T(8,128)(2,1)S(1)} %collective-permute-done.4.refs_1_), channel_id=1, source_target_pairs={{1,0},{0,1},{3,2},{2,3},{5,4},{4,5},{7,6},{6,7},{9,8},{8,9},{11,10... | collective-permute-start | bytes 2359304 | tf_op jit(solution)/shard_map/ppermute | solution.py:332
  56.4 2.2 %copy-start.4 = (bf16[4,48,2048]{2,1,0:T(8,128)(2,1)}, bf16[4,48,2048]{2,1,0:T(8,128)(2,1)S(1)}, u32[]{:S(2)}) copy-start(bf16[4,48,2048]{2,1,0:T(8,128)(2,1)S(1)} %collective-permute-done.7.refs_4_) | copy-start | bytes 2359300
  56.4 2.3 %copy-start.5 = (bf16[4,48,2048]{2,1,0:T(8,128)(2,1)}, bf16[4,48,2048]{2,1,0:T(8,128)(2,1)S(1)}, u32[]{:S(2)}) copy-start(bf16[4,48,2048]{2,1,0:T(8,128)(2,1)S(1)} %collective-permute-done.10.refs_7_) | copy-start | bytes 2359300
  57.5 1.2 %copy-start.6 = (bf16[4,48,2048]{2,1,0:T(8,128)(2,1)}, bf16[4,48,2048]{2,1,0:T(8,128)(2,1)S(1)}, u32[]{:S(2)}) copy-start(bf16[4,48,2048]{2,1,0:T(8,128)(2,1)S(1)} %collective-permute-done.9.refs_6_) | copy-start | bytes 2359300
  58.6 0.9 copy-start.7

commit v3 on v2

v3 whole, which is shorter than its diff:
```python
import functools

import jax
import jax.numpy as jnp
from jax import lax
from jax.experimental import pallas as pl
from jax.experimental.pallas import tpu as pltpu
from jax.sharding import PartitionSpec as P

HEAD = 64
PAIR = 128
SHARPNESS = 0.25
EPSILON = 1e-5
LOG2E = 1.4426950408889634
F32 = jnp.float32
BF16 = jnp.bfloat16
VMEM_LIMIT = 56 * 2**20
NT = (((1,), (1,)), ((), ()))


def halves(tile):
    low = lax.broadcasted_iota(jnp.int32, (1, PAIR), 1) < HEAD
    zero = jnp.zeros_like(tile)
    return jnp.where(low, tile, zero).astype(BF16), jnp.where(low, zero, tile).astype(BF16)


def ones_beside(rows):
    low = lax.broadcasted_iota(jnp.int32, (1, PAIR), 1) < HEAD
    first = lax.broadcasted_iota(jnp.int32, (2 * rows, 1), 0) < rows
    return jnp.where(jnp.logical_xor(first, low), 0.0, 1.0).astype(BF16)


HALF = 384
WEIGHTS = 3 * HALF
PROJECT = 4 * HALF
BLOCK = 5 * HALF
SMALL = ((0, 0), (2, 1), (0, 2), (2, 3))
LARGE = ((0, 0), (1, 0), (3, 0), (0, 1))


def half_block(half, context_ref, query_ref, wqkv_ref, wout_ref):
    hidden = query_ref.shape[1]
    first = half == 0
    parts = [wqkv_ref[:, b * hidden : (b + 1) * hidden].astype(F32) for b in range(3)] + [wout_ref[...].astype(F32)]
    parts.append(jnp.concatenate([context_ref[...].astype(F32), query_ref[...].astype(F32)], axis=0))
    parts = [jnp.where(first, p[:, :HALF], p[:, HALF:]) for p in parts]
    return jnp.concatenate(parts, axis=1)


def place_of_device():
    me = lax.axis_index("dev")
    return me >> 3, (me >> 1) & 3, me & 1


def give_kernel(context_ref, query_ref, wqkv_ref, wout_ref, o_ref):
    core = place_of_device()[2]
    o_ref[...] = half_block(1 - core, context_ref, query_ref, wqkv_ref, wout_ref).astype(BF16)


def chip_kernel(context_ref, query_ref, wqkv_ref, wout_ref, got_ref, o_ref):
    core = place_of_device()[2]
    own = half_block(core, context_ref, query_ref, wqkv_ref, wout_ref)
    got = got_ref[...].astype(F32)
    low = jnp.where(core == 0, own, got)
    high = jnp.where(core == 0, got, own)
    o_ref[:, :PROJECT] = jnp.concatenate([low[:, :PROJECT], high[:, :PROJECT]], axis=0).astype(BF16)
    rows = [low[:16, PROJECT:], high[:16, PROJECT:], low[16:, PROJECT:], high[16:, PROJECT:]]
    o_ref[:, PROJECT:] = jnp.concatenate(rows, axis=0).astype(BF16)


def build(kernel, rows, name, *arrays):
    vmem = pl.BlockSpec(memory_space=pltpu.VMEM)
    return pl.pallas_call(
        kernel,
        out_shape=jax.ShapeDtypeStruct((rows, BLOCK), BF16),
        in_specs=[vmem] * len(arrays),
        out_specs=vmem,
        name=name,
    )(*arrays)


def layer_kernel(rows, unroll, len_ref, positive_ref, x_ref, gain_ref, *refs):
    pieces, refs = refs[:8], refs[8:]
    o_ref, tell_ref, told_ref, w_s, wo_s, ctx_s, query_s, q_s, k_s, v_s, kc_s, vc_s, attn_s, sems = refs
    tokens, hidden = x_ref.shape
    docs = o_ref.shape[0]
    seq = tokens // docs
    pairs = hidden // PAIR
    per = HALF // PAIR
    nctx = ctx_s.shape[1] * ctx_s.shape[2]
    scale = LOG2E / HEAD**0.5
    x, z, core = place_of_device()
    weights, others, last = [], [], []
    for side in range(2):
        for p, (ax, az) in enumerate(LARGE):
            piece = pieces[side * 4 + p]
            n = side * 4 + p
            for k, (bx, bz) in enumerate(SMALL):
                chip = ((x + ax + bx) & 3) * 4 + ((z + az + bz) & 3)
                at = pl.multiple_of(chip * 48, 48)
                here = (core + side) & 1
                lanes = pl.ds(pl.multiple_of(here * HALF, HALF), HALF)
                weights.append(
                    pltpu.make_async_copy(
                        piece.at[k, :, pl.ds(0, WEIGHTS)], w_s.at[side, pl.ds(at, 48)], sems.at[0, n * 4 + k]
                    )
                )
                last.append(
                    pltpu.make_async_copy(
                        piece.at[k, :, pl.ds(WEIGHTS, HALF)], wo_s.at[pl.ds(at, 48), lanes], sems.at[1, n * 4 + k]
                    )
                )
                last.append(
                    pltpu.make_async_copy(
                        piece.at[k, pl.ds(32, 16), pl.ds(PROJECT, HALF)], query_s.at[side, chip], sems.at[2, n * 4 + k]
                    )
                )
            others.append(
                pltpu.make_async_copy(
                    piece.at[:, pl.ds(0, 32), pl.ds(PROJECT, HALF)], ctx_s.at[side, pl.ds(4 * p, 4)], sems.at[3, n]
                )
            )
    for copy in weights + others + last:
        copy.start()
    for copy in weights:
        copy.wait()

    def project(i, _):
        r = pl.ds(pl.multiple_of(i * rows, rows), rows)
        states = x_ref[r, :]
        for side in range(2):
            t = jnp.dot(states, w_s[side], preferred_element_type=F32)
            q_s[r, side * HALF : (side + 1) * HALF] = (t[:, :HALF] * scale).astype(BF16)
            for begin, out in ((HALF, k_s), (2 * HALF, v_s)):
                for j in range(per):
                    even, odd = halves(t[:, begin + j * PAIR : begin + (j + 1) * PAIR])
                    for e in range(rows // seq):
                        d = i * (rows // seq) + e
                        out[side * per + j, d, :seq] = even[e * seq : (e + 1) * seq]
                        out[side * per + j, d, seq:] = odd[e * seq : (e + 1) * seq]
        return 0

    lax.fori_loop(0, tokens // rows, project, 0)
    for copy in others:
        copy.wait()
    near = ctx_s[0].reshape(nctx, HALF)
    far = ctx_s[1].reshape(nctx, HALF)
    first = core == 0
    ctx = jnp.concatenate([jnp.where(first, near, far), jnp.where(first, far, near)], axis=1)
    for side in range(2):
        t = jnp.dot(ctx, w_s[side, :, HALF:], preferred_element_type=F32)
        for begin, out in ((0, kc_s), (HALF, vc_s)):
            for j in range(per):
                even, odd = halves(t[:, begin + j * PAIR : begin + (j + 1) * PAIR])
                out[side * per + j, :nctx] = even
                out[side * per + j, nctx:] = odd
    ones_ctx = ones_beside(nctx)
    ones_own = ones_beside(seq)
    slot = lax.broadcasted_iota(jnp.int32, (1, 2 * seq), 1)
    slot = jnp.where(slot < seq, slot, slot - seq)
    for j in range(pairs):

        def doc(d, _):
            r = pl.ds(pl.multiple_of(d * seq, seq), seq)
            q = q_s[r, j * PAIR : (j + 1) * PAIR]
            bias = jnp.where(slot < len_ref[d], 0.0, -jnp.inf).astype(F32)
            score_ctx = lax.dot_general(q, kc_s[j], NT, preferred_element_type=F32)
            score_own = lax.dot_general(q, k_s[j, d], NT, preferred_element_type=F32) + bias
            p_ctx, p_own = [], []
            for e in range(2):
                c = score_ctx[:, e * nctx : (e + 1) * nctx]
                o = score_own[:, e * seq : (e + 1) * seq]
                top = jnp.maximum(jnp.max(c, axis=1, keepdims=True), jnp.max(o, axis=1, keepdims=True))
                p_ctx.append(jnp.exp2(c - top).astype(BF16))
                p_own.append(jnp.exp2(o - top).astype(BF16))
            mixed = jnp.dot(
                jnp.concatenate(p_ctx, axis=1),
                jnp.concatenate([vc_s[j], ones_ctx], axis=1),
                preferred_element_type=F32,
            ) + jnp.dot(
                jnp.concatenate(p_own, axis=1),
                jnp.concatenate([v_s[j, d], ones_own], axis=1),
                preferred_element_type=F32,
            )
            here = pl.multiple_of(((core + j // per) & 1) * HALF + j % per * PAIR, PAIR)
            attn_s[r, pl.ds(here, PAIR)] = (mixed[:, :PAIR] / mixed[:, PAIR:]).astype(BF16)
            return 0

        lax.fori_loop(0, docs, doc, 0, unroll=unroll)
    for copy in last:
        copy.wait()
    position = lax.broadcasted_iota(jnp.int32, (seq, 1), 0)
    pooled = []
    for g in range(0, docs, 2):
        both = slice(g * seq, (g + 2) * seq)
        h_both = x_ref[both, :].astype(F32) + jnp.dot(attn_s[both, :], wo_s[...], preferred_element_type=F32)
        for d in (g, g + 1):
            h = h_both[(d - g) * seq : (d - g + 1) * seq]
            center = jnp.mean(h, axis=1, keepdims=True)
            off = h - center
            spread = jnp.mean(off * off, axis=1, keepdims=True)
            length = len_ref[d]
            weight = jnp.where(position < length, lax.rsqrt(spread + EPSILON), 0.0)
            pooled.append(jnp.sum(off * weight, axis=0, keepdims=True) / length.astype(F32))
    embed = jnp.concatenate(pooled, axis=0) * gain_ref[...]
    o_ref[...] = embed.astype(BF16)
    row = lax.broadcasted_iota(jnp.int32, (docs, 128), 0)
    beside = jnp.zeros((docs, 128), F32)
    for i in range(docs):
        beside = jnp.where(row == i, positive_ref[i].astype(F32), beside)
    tell = jnp.concatenate([embed, beside], axis=1).astype(BF16)
    for i in range(tell_ref.shape[0]):
        tell_ref[i] = tell
    count = told_ref.shape[0]
    near = query_s[0].reshape(count, HALF)
    far = query_s[1].reshape(count, HALF)
    told_ref[:, :HALF] = jnp.where(first, near, far)
    told_ref[:, HALF:] = jnp.where(first, far, near)


def layer(lengths, positive, x, gain, pieces, seq):
    tokens, hidden = x.shape
    docs = tokens // seq
    pairs = hidden // PAIR
    chips = 16
    nctx = chips * 32
    rows = 2 * seq
    vmem = pl.BlockSpec(memory_space=pltpu.VMEM)
    smem = pl.BlockSpec(memory_space=pltpu.SMEM)
    hbm = pl.BlockSpec(memory_space=pl.ANY)
    return pl.pallas_call(
        functools.partial(layer_kernel, rows, docs),
        out_shape=(
            jax.ShapeDtypeStruct((docs, hidden), BF16),
            jax.ShapeDtypeStruct((chips, docs, hidden + 128), BF16),
            jax.ShapeDtypeStruct((chips * 16, hidden), BF16),
        ),
        in_specs=[smem, smem, vmem, vmem] + [hbm] * 8,
        out_specs=(vmem, vmem, vmem),
        scratch_shapes=[
            pltpu.VMEM((2, hidden, WEIGHTS), BF16),
            pltpu.VMEM((hidden, hidden), BF16),
            pltpu.VMEM((2, chips, 32, HALF), BF16),
            pltpu.VMEM((2, chips, 16, HALF), BF16),
            pltpu.VMEM((tokens, hidden), BF16),
            pltpu.VMEM((pairs, docs, 2 * seq, PAIR), BF16),
            pltpu.VMEM((pairs, docs, 2 * seq, PAIR), BF16),
            pltpu.VMEM((pairs, 2 * nctx, PAIR), BF16),
            pltpu.VMEM((pairs, 2 * nctx, PAIR), BF16),
            pltpu.VMEM((tokens, hidden), BF16),
            pltpu.SemaphoreType.DMA((4, 32)),
        ],
        compiler_params=pltpu.CompilerParams(vmem_limit_bytes=VMEM_LIMIT),
        name="layer",
    )(lengths, positive, x, gain.reshape(1, hidden), *pieces)


def exact_dot(a, b):
    a1 = a.astype(BF16)
    rest = a - a1.astype(F32)
    a2 = rest.astype(BF16)
    a3 = (rest - a2.astype(F32)).astype(BF16)
    n = a.shape[0]
    out = jnp.dot(jnp.concatenate([a1, a2, a3], axis=0), b, preferred_element_type=F32)
    return out[:n] + out[n : 2 * n] + out[2 * n :]


def contrast_kernel(told_ref, near_ref, far_ref, dgrad_ref, qgrad_ref, loss_ref, coeff_s, rows_s, loss_s):
    docs, hidden = told_ref.shape
    chips, mine, _ = near_ref.shape
    divisor = 1.0 / (hidden**0.5 * SHARPNESS)
    x, z, core = place_of_device()
    near = near_ref[...].astype(F32)
    far = far_ref[...].astype(F32)
    low = jnp.where(core == 0, near, far)
    high = jnp.where(core == 0, far, near)
    table = jnp.concatenate([t[i] for i in range(chips) for t in (low, high)], axis=0)
    embed = table[:, :hidden].astype(BF16)
    beside = table[:, hidden:]
    positive = beside.T[:1]
    queries = told_ref[...]
    scores_t = lax.dot_general(embed, queries, NT, preferred_element_type=F32) * divisor
    top = jnp.max(scores_t, axis=0, keepdims=True)
    lse_t = top + jnp.log(jnp.sum(jnp.exp(scores_t - top), axis=0, keepdims=True))
    doc_id = lax.broadcasted_iota(jnp.int32, (docs, 1), 0).astype(F32)
    coeff_s[...] = jnp.exp(scores_t - lse_t) - jnp.where(doc_id == positive, 1.0, 0.0)
    chip = x * 4 + z
    own = pl.ds(pl.multiple_of((chip * 2 + core) * mine, mine), mine)
    dgrad_ref[...] = exact_dot(coeff_s[own, :], queries) * divisor
    both = told_ref[pl.ds(pl.multiple_of(chip * 16, 16), 16), :]
    scores = lax.dot_general(both, embed, NT, preferred_element_type=F32) * divisor
    rows_s[...] = scores
    loss_s[...] = beside
    scores = rows_s[pl.ds(pl.multiple_of(core * mine, mine), mine), :]
    own_positive = loss_s[own, :1]
    top = jnp.max(scores, axis=1, keepdims=True)
    lse = top + jnp.log(jnp.sum(jnp.exp(scores - top), axis=1, keepdims=True))
    is_positive = lax.broadcasted_iota(jnp.int32, (1, docs), 1).astype(F32) == own_positive
    loss = lse - jnp.sum(jnp.where(is_positive, scores, 0.0), axis=1, keepdims=True)
    coeff = jnp.exp(scores - lse) - jnp.where(is_positive, 1.0, 0.0)
    qgrad_ref[...] = exact_dot(coeff, embed) * divisor
    spot = lax.broadcasted_iota(jnp.int32, (mine, 128), 1)
    row = lax.broadcasted_iota(jnp.int32, (mine, 128), 0)
    loss_ref[...] = jnp.sum(jnp.where(spot == row, loss, 0.0), axis=0, keepdims=True)[:, :mine]


def contrast(told, near, far):
    docs, hidden = told.shape
    mine = near.shape[1]
    vmem = pl.BlockSpec(memory_space=pltpu.VMEM)
    return pl.pallas_call(
        contrast_kernel,
        out_shape=(
            jax.ShapeDtypeStruct((mine, hidden), F32),
            jax.ShapeDtypeStruct((mine, hidden), F32),
            jax.ShapeDtypeStruct((1, mine), F32),
        ),
        in_specs=[vmem, vmem, vmem],
        out_specs=(vmem, vmem, vmem),
        scratch_shapes=[
            pltpu.VMEM((docs, docs), F32),
            pltpu.VMEM((16, docs), F32),
            pltpu.VMEM((docs, 128), F32),
        ],
        compiler_params=pltpu.CompilerParams(vmem_limit_bytes=VMEM_LIMIT),
        name="contrast",
    )(told, near, far)


def fetch(value, dx=0, dz=0, dcore=0):
    moves = [
        ((x + dx) % 4 * 8 + (z + dz) % 4 * 2 + (core ^ dcore), x * 8 + z * 2 + core)
        for x in range(4)
        for z in range(4)
        for core in range(2)
    ]
    return lax.ppermute(value, "dev", moves)


def local(doc_states, context_embeds, w_qkv, w_out, ln_gain, queries, positive, lengths):
    docs, seq, hidden = doc_states.shape
    x = doc_states.reshape(docs * seq, hidden)
    arrays = (context_embeds, queries, w_qkv, w_out)
    got = fetch(build(give_kernel, 24, "give", *arrays), dcore=1)
    block = build(chip_kernel, 48, "chip", *arrays, got)
    four = jnp.stack([block] + [fetch(block, dx, dz) for dx, dz in SMALL[1:]])
    near = [four] + [fetch(four, dx, dz) for dx, dz in LARGE[1:]]
    far = [fetch(piece, dcore=1) for piece in near]
    embed, tell, told = layer(lengths, positive, x, ln_gain, near + far, seq)
    chips = [[chip * 2 + core for chip in range(16)] for core in range(2)]
    near = lax.all_to_all(tell, "dev", 0, 0, axis_index_groups=chips)
    far = fetch(near, dcore=1)
    dgrad, qgrad, loss = contrast(told, near, far)
    return embed, dgrad, qgrad, loss.reshape(docs)


def solution(mesh):
    both = ("grp", "dev")
    return jax.shard_map(
        local,
        mesh=mesh,
        in_specs=(
            P(both, None, None),
            P(both, None),
            P("dev", None),
            P("dev", None),
            P(),
            P(both, None),
            P(both),
            P(both),
        ),
        out_specs=(P(both, None), P(both, None), P(both, None), P(both)),
        check_vma=False,
    )
```

time: 106 us -> 99.5 us (0.939)
  blocking collectives: 18.4 us -> 12.7 us
  starting transfers between devices: 23.5 us -> 25.5 us
  Pallas kernels: 30.5 us -> 29.2 us
    all_to_all x1, blocking collectives: 18.4 us -> 12.7 us  [local(): near = lax.all_to_all(tell, 'dev', 0, 0, axis_index_groups=chips)]
    ppermute x11 -> x12, starting transfers between devices: 23.5 us -> 25.5 us  [fetch(): return lax.ppermute(value, 'dev', moves)]
    pallas_call x1, Pallas kernels: 24.1 us -> 22.8 us  [layer(): pl.pallas_call(functools.partial(layer_kernel, rows, docs), out_shape=(ja...]
    ppermute x11 -> x12, waiting for transfers between devices: 28 us -> 27.2 us  [fetch(): return lax.ppermute(value, 'dev', moves)]
    unnamed x20 -> x24, local copies, waits for them, and re-layouts: 1.5 us -> 2.15 us
  transfers between devices with their start and end apart: 11 -> 12, of which waited for: 7 -> 8; matrix products, arithmetic and copies ran while one was open for 1% -> 1% of each run, Pallas kernels for 0% -> 0%
where the time goes in v3:
time: 99.5 us; the launch traced here: 99.2 us
  Pallas kernels  29.2 us (29%)
  waiting for transfers between devices  27.2 us (27%)
  starting transfers between devices  25.5 us (26%)
  blocking collectives  12.7 us (13%)
  local copies, waits for them, and re-layouts  2.86 us (3%)
  other arithmetic  1.04 us (1%)
    ppermute x12, waiting for transfers between devices, fetch(): return lax.ppermute(value, 'dev', moves)  27.2 us
    ppermute x12, starting transfers between devices, fetch(): return lax.ppermute(value, 'dev', moves)  25.5 us
    pallas_call x1, Pallas kernels, layer(): pl.pallas_call(functools.partial(layer_kernel, rows, docs), out_shape=(ja...  22.8 us
    all_to_all x1, blocking collectives, local(): near = lax.all_to_all(tell, 'dev', 0, 0, axis_index_groups=chips)  12.7 us
    pallas_call x2, Pallas kernels, build(): pl.pallas_call(kernel, out_shape=jax.ShapeDtypeStruct((rows, BLOCK), BF16...  3.32 us
    pallas_call x1, Pallas kernels, contrast(): pl.pallas_call(contrast_kernel, out_shape=(jax.ShapeDtypeStruct((mine, hi...  3.08 us
    unnamed x24, local copies, waits for them, and re-layouts  2.15 us
  transfers between devices with their start and end apart: 12, of which 8 were waited for; matrix products, arithmetic and copies ran while one was open for 1% of the time, Pallas kernels for 0%

profile of v3, /device:TPU:1, one launch (start us, length us, event | category | flops | bytes accessed | tf_op | source)
XLA Modules:
  0.0 99.2 jit_solution(18202227800962435760)
XLA Ops:
  0.6 0.0 copy-start.11
  0.6 1.6 %give.1 = bf16[24,1920]{1,0:T(8,128)(2,1)} custom-call(bf16[16,768]{1,0:T(8,128)(2,1)} %context_ref.3, bf16[8,768]{1,0:T(8,128)(2,1)} %query_ref.3, bf16[24,2304]{1,0:T(8,128)(2,1)} %wqkv_ref.3, bf16[24,768]{1,0:T(8,128)(2,1)} %wout_ref.3), custom_call_target="tpu_custom_call" | custom-call | tf_op jit(solution)/shard_map/give/pallas_call | solution.py:73
  2.2 3.2 %collective-permute-start = (bf16[24,1920]{1,0:T(8,128)(2,1)}, bf16[24,1920]{1,0:T(8,128)(2,1)S(1)}, u32[]{:S(2)}, u32[]{:S(2)}) collective-permute-start(bf16[24,1920]{1,0:T(8,128)(2,1)} %give.1), channel_id=1, source_target_pairs={{1,0},{0,1},{3,2},{2,3},{5,4},{4,5},{7,6},{6,7},{9,8},{8,9},{11,10... | collective-permute-start | bytes 276488 | tf_op jit(solution)/shard_map/ppermute | solution.py:337
  5.5 1.1 %collective-permute-done.got_ref = bf16[24,1920]{1,0:T(8,128)(2,1)S(1)} collective-permute-done((bf16[24,1920]{1,0:T(8,128)(2,1)}, bf16[24,1920]{1,0:T(8,128)(2,1)S(1)}, u32[]{:S(2)}, u32[]{:S(2)}) %collective-permute-start) | collective-permute-done | bytes 92192 | tf_op jit(solution)/shard_map/ppermute | solution.py:337
  6.6 0.0 copy-start.10
  6.6 0.6 copy-done.10
  7.3 1.7 %chip.1 = bf16[48,1920]{1,0:T(8,128)(2,1)} custom-call(bf16[16,768]{1,0:T(8,128)(2,1)} %context_ref.3, bf16[8,768]{1,0:T(8,128)(2,1)} %query_ref.3, bf16[24,2304]{1,0:T(8,128)(2,1)} %wqkv_ref.3, bf16[24,768]{1,0:T(8,128)(2,1)} %wout_ref.3, bf16[24,1920]{1,0:T(8,128)(2,1)} %copy-done.10), custom_call_target="tpu_custom_call" | custom-call | tf_op jit(solution)/shard_map/chip/pallas_call | solution.py:73
  9.0 2.4 %collective-permute-start.3 = (bf16[48,1920]{1,0:T(8,128)(2,1)}, bf16[48,1920]{1,0:T(8,128)(2,1)S(1)}, u32[]{:S(2)}, u32[]{:S(2)}) collective-permute-start(bf16[48,1920]{1,0:T(8,128)(2,1)} %chip.1), channel_id=1, source_target_pairs={{22,0},{23,1},{16,2},{17,3},{18,4},{19,5},{20,6},{21,7},{30,8},{31... | collective-permute-start | bytes 552968 | tf_op jit(solution)/shard_map/ppermute | solution.py:337
  11.3 3.0 %collective-permute-start.2 = (bf16[48,1920]{1,0:T(8,128)(2,1)}, bf16[48,1920]{1,0:T(8,128)(2,1)S(1)}, u32[]{:S(2)}, u32[]{:S(2)}) collective-permute-start(bf16[48,1920]{1,0:T(8,128)(2,1)} %chip.1), channel_id=1, source_target_pairs={{4,0},{5,1},{6,2},{7,3},{0,4},{1,5},{2,6},{3,7},{12,8},{13,9},{14,... | collective-permute-start | bytes 552968 | tf_op jit(solution)/shard_map/ppermute | solution.py:337
  14.3 0.7 collective-permute-start.1
  15.0 4.3 %collective-permute-done.3 = bf16[48,1920]{1,0:T(8,128)(2,1)S(1)} collective-permute-done((bf16[48,1920]{1,0:T(8,128)(2,1)}, bf16[48,1920]{1,0:T(8,128)(2,1)S(1)}, u32[]{:S(2)}, u32[]{:S(2)}) %collective-permute-start.3) | collective-permute-done | bytes 184352 | tf_op jit(solution)/shard_map/ppermute | solution.py:337
  19.3 6.9 %collective-permute-done.2 = bf16[48,1920]{1,0:T(8,128)(2,1)S(1)} collective-permute-done((bf16[48,1920]{1,0:T(8,128)(2,1)}, bf16[48,1920]{1,0:T(8,128)(2,1)S(1)}, u32[]{:S(2)}, u32[]{:S(2)}) %collective-permute-start.2) | collective-permute-done | bytes 184352 | tf_op jit(solution)/shard_map/ppermute | solution.py:337
  26.2 0.0 collective-permute-done.1
  26.2 1.0 %pad_maximum_fusion.refs_0_ = bf16[4,48,1920]{2,1,0:T(8,128)(2,1)S(1)} fusion(bf16[1,48,1920]{2,1,0:T(8,128)(2,1)S(1)} %bitcast.8, bf16[1,48,1920]{2,1,0:T(8,128)(2,1)S(1)} %bitcast.9, bf16[1,48,1920]{2,1,0:T(8,128)(2,1)S(1)} %bitcast.10, bf16[1,48,1920]{2,1,0:T(8,128)(2,1)} %bitcast.7), kind=kLoop, calls=%fused_computation | loop fusion | flops 1105920 | bytes 1474560 | tf_op jit(solution)/shard_map/stack | solution.py:346
  27.2 0.0 copy-start
  27.2 5.4 %collective-permute-start.6 = (bf16[4,48,1920]{2,1,0:T(8,128)(2,1)S(1)}, bf16[4,48,1920]{2,1,0:T(8,128)(2,1)S(1)}, u32[]{:S(2)}, u32[]{:S(2)}) collective-permute-start(bf16[4,48,1920]{2,1,0:T(8,128)(2,1)S(1)} %pad_maximum_fusion.refs_0_), channel_id=1, source_target_pairs={{2,0},{3,1},{4,2},{5,3},{6,4},{7,5},{0,6},{1,7},{10,8},{11,9},{12,... | collective-permute-start | bytes 2211848 | tf_op jit(solution)/shard_map/ppermute | solution.py:337
  32.7 0.3 collective-permute-start.5
  33.0 2.4 %collective-permute-start.4 = (bf16[4,48,1920]{2,1,0:T(8,128)(2,1)S(1)}, bf16[4,48,1920]{2,1,0:T(8,128)(2,1)S(1)}, u32[]{:S(2)}, u32[]{:S(2)}) collective-permute-start(bf16[4,48,1920]{2,1,0:T(8,128)(2,1)S(1)} %pad_maximum_fusion.refs_0_), channel_id=1, source_target_pairs={{8,0},{9,1},{10,2},{11,3},{12,4},{13,5},{14,6},{15,7},{16,8},{17,9... | collective-permute-start | bytes 2211848 | tf_op jit(solution)/shard_map/ppermute | solution.py:337
  35.3 2.0 %collective-permute-start.7 = (bf16[4,48,1920]{2,1,0:T(8,128)(2,1)S(1)}, bf16[4,48,1920]{2,1,0:T(8,128)(2,1)S(1)}, u32[]{:S(2)}, u32[]{:S(2)}) collective-permute-start(bf16[4,48,1920]{2,1,0:T(8,128)(2,1)S(1)} %pad_maximum_fusion.refs_0_), channel_id=1, source_target_pairs={{1,0},{0,1},{3,2},{2,3},{5,4},{4,5},{7,6},{6,7},{9,8},{8,9},{11,10... | collective-permute-start | bytes 2211848 | tf_op jit(solution)/shard_map/ppermute | solution.py:337
  37.4 11.3 %collective-permute-done.6.refs_3_ = bf16[4,48,1920]{2,1,0:T(8,128)(2,1)S(1)} collective-permute-done((bf16[4,48,1920]{2,1,0:T(8,128)(2,1)S(1)}, bf16[4,48,1920]{2,1,0:T(8,128)(2,1)S(1)}, u32[]{:S(2)}, u32[]{:S(2)}) %collective-permute-start.6) | collective-permute-done | bytes 737312 | tf_op jit(solution)/shard_map/ppermute | solution.py:337
  48.7 0.0 copy-start.2
  48.7 1.4 %collective-permute-start.10 = (bf16[4,48,1920]{2,1,0:T(8,128)(2,1)S(1)}, bf16[4,48,1920]{2,1,0:T(8,128)(2,1)S(1)}, u32[]{:S(2)}, u32[]{:S(2)}) collective-permute-start(bf16[4,48,1920]{2,1,0:T(8,128)(2,1)S(1)} %collective-permute-done.6.refs_3_), channel_id=1, source_target_pairs={{1,0},{0,1},{3,2},{2,3},{5,4},{4,5},{7,6},{6,7},{9,8},{8,9},{11,10... | collective-permute-start | bytes 2211848 | tf_op jit(solution)/shard_map/ppermute | solution.py:337
  50.1 0.3 collective-permute-done.5.refs_2_
  50.4 2.4 %collective-permute-start.9 = (bf16[4,48,1920]{2,1,0:T(8,128)(2,1)S(1)}, bf16[4,48,1920]{2,1,0:T(8,128)(2,1)S(1)}, u32[]{:S(2)}, u32[]{:S(2)}) collective-permute-start(bf16[4,48,1920]{2,1,0:T(8,128)(2,1)S(1)} %collective-permute-done.5.refs_2_), channel_id=1, source_target_pairs={{1,0},{0,1},{3,2},{2,3},{5,4},{4,5},{7,6},{6,7},{9,8},{8,9},{11,10... | collective-permute-start | bytes 2211848 | tf_op jit(solution)/shard_map/ppermute | solution.py:337
  52.8 0.0 collective-permute-done.4.refs_1_
  52.8 0.1 collective-permute-start.8
  52.9 0.0 copy-done.11
  52.9 0.7 reshape.18.gain_ref
  53.6 0.0 collective-permute-done.7.refs_4_
  53.6 0.0 collective-permute-done.10.refs_7_
  53.6 0.0 copy-start.6
  53.6 1.0 %collective-permute-done.9.refs_6_ = bf16[4,48,1920]{2,1,0:T(8,128)(2,1)S(1)} collective-permute-done((bf16[4,48,1920]{2,1,0:T(8,128)(2,1)S(1)}, bf16[4,48,1920]{2,1,0:T(8,128)(2,1)S(1)}, u32[]{:S(2)}, u32[]{:S(2)}) %collective-permute-start.9) | collective-permute-done | bytes 737312 | tf_op jit(solution)/shard_map/ppermute | solution.py:337
  54.6 1.1 %collective-permute-done.8.refs_5_ = bf16[4,48,1920]{2,1,0:T(8,128)(2,1)S(1)} collective-permute-done((bf16[4,48,1920]{2,1,0:T(8,128)(2,1)S(1)}, bf16[4,48,1920]{2,1,0:T(8,128)(2,1)S(1)}, u32[]{:S(2)}, u32[]{:S(2)}) %collective-permute-start.8) | collective-permute-done | bytes 737312 | tf_op jit(solution)/shard_map/ppermute | solution.py:337
  55.7 0.0 copy-done
  55.7 0.0 copy-done.2
  55.7 0.0 copy-done.3
  55.7 0.0 copy-done.4
  55.7 0.0 copy-done.5
  55.7 0.0 copy-done.6
  55.7 0.0 copy-done.7
  55.7 0.8 copy-done.8
  56.5 22.8 %layer.1 = (bf16[8,768]{1,0:T(8,128)(2,1)}, bf16[16,8,896]{2,1,0:T(8,128)(2,1)}, bf16[256,768]{1,0:T(8,128)(2,1)}) custom-call(s32[8]{0:T(128)} %len_ref.1, s32[8]{0:T(128)} %positive_ref.1, bf16[1024,768]{1,0:T(8,128)(2,1)} %bitcast.6, f32[1,768]{1,0:T(1,128)} %reshape.18.gain_ref, bf16[4,48,1920]{2,1,0:T(8,128)(2,1)} %copy-done, ...), custom_call_target="tpu_custom_call" | custom-call | tf_op jit(solution)/shard_map/layer/pallas_call | solution.py:231
  79.3 12.7 %all_to_all.5.near_ref = bf16[16,8,896]{2,1,0:T(8,128)(2,1)S(1)} all-to-all(bf16[16,8,896]{2,1,0:T(8,128)(2,1)} %get-tuple-element.12), channel_id=1, replica_groups={{0,2,4,6,8,10,12,14,16,18,20,22,24,26,28,30},{1,3,5,7,9,11,13,15,17,19,..., dimensions={0} | all-to-all | bytes 458752 | tf_op jit(solution)/shard_map/all_to_all | solution.py:351
  92.0 2.3 %collective-permute-start.11 = (bf16[16,8,896]{2,1,0:T(8,128)(2,1)S(1)}, bf16[16,8,896]{2,1,0:T(8,128)(2,1)S(1)}, u32[]{:S(2)}, u32[]{:S(2)}) collective-permute-start(bf16[16,8,896]{2,1,0:T(8,128)(2,1)S(1)} %all_to_all.5.near_ref), channel_id=1, source_target_pairs={{1,0},{0,1},{3,2},{2,3},{5,4},{4,5},{7,6},{6,7},{9,8},{8,9},{11,10... | collective-permute-start | bytes 688136 | tf_op jit(solution)/shard_map/ppermute | solution.py:337
  94.3 1.1 %collective-permute-done.11.far_ref = bf16[16,8,896]{2,1,0:T(8,128)(2,1)S(1)} collective-permute-done((bf16[16,8,896]{2,1,0:T(8,128)(2,1)S(1)}, bf16[16,8,896]{2,1,0:T(8,128)(2,1)S(1)}, u32[]{:S(2)}, u32[]{:S(2)}) %collective-permute-start.11) | collective-permute-done | bytes 229408 | tf_op jit(solution)/shard_map/ppermute | solution.py:337
  95.5 0.0 copy-done.1
  95.5 0.7 copy-done.9
  96.1 3.1 %contrast.1 = (f32[8,768]{1,0:T(8,128)}, f32[8,768]{1,0:T(8,128)}, f32[1,8]{1,0:T(1,128)}) custom-call(bf16[256,768]{1,0:T(8,128)(2,1)} %get-tuple-element.11.told_ref, bf16[16,8,896]{2,1,0:T(8,128)(2,1)} %copy-done.1, bf16[16,8,896]{2,1,0:T(8,128)(2,1)} %copy-done.9), custom_call_target="tpu_custom_call" | custom-call | tf_op jit(solution)/shard_map/contrast/pallas_call | solution.py:311
  (7 shorter events, 0.0 us)
Async XLA Ops:
  0.6 52.2 %copy-start.11 = (f32[768]{0:T(1024)S(1)}, f32[768]{0:T(1024)}, u32[]{:S(2)}) copy-start(f32[768]{0:T(1024)} %param.12) | copy-start | bytes 9220
  2.2 4.4 %collective-permute-start = (bf16[24,1920]{1,0:T(8,128)(2,1)}, bf16[24,1920]{1,0:T(8,128)(2,1)S(1)}, u32[]{:S(2)}, u32[]{:S(2)}) collective-permute-start(bf16[24,1920]{1,0:T(8,128)(2,1)} %give.1), channel_id=1, source_target_pairs={{1,0},{0,1},{3,2},{2,3},{5,4},{4,5},{7,6},{6,7},{9,8},{8,9},{11,10... | collective-permute-start | bytes 276488 | tf_op jit(solution)/shard_map/ppermute | solution.py:337
  6.6 0.6 copy-start.10
  9.0 10.3 %collective-permute-start.3 = (bf16[48,1920]{1,0:T(8,128)(2,1)}, bf16[48,1920]{1,0:T(8,128)(2,1)S(1)}, u32[]{:S(2)}, u32[]{:S(2)}) collective-permute-start(bf16[48,1920]{1,0:T(8,128)(2,1)} %chip.1), channel_id=1, source_target_pairs={{22,0},{23,1},{16,2},{17,3},{18,4},{19,5},{20,6},{21,7},{30,8},{31... | collective-permute-start | bytes 552968 | tf_op jit(solution)/shard_map/ppermute | solution.py:337
  11.3 14.9 %collective-permute-start.2 = (bf16[48,1920]{1,0:T(8,128)(2,1)}, bf16[48,1920]{1,0:T(8,128)(2,1)S(1)}, u32[]{:S(2)}, u32[]{:S(2)}) collective-permute-start(bf16[48,1920]{1,0:T(8,128)(2,1)} %chip.1), channel_id=1, source_target_pairs={{4,0},{5,1},{6,2},{7,3},{0,4},{1,5},{2,6},{3,7},{12,8},{13,9},{14,... | collective-permute-start | bytes 552968 | tf_op jit(solution)/shard_map/ppermute | solution.py:337
  14.3 11.9 %collective-permute-start.1 = (bf16[48,1920]{1,0:T(8,128)(2,1)}, bf16[48,1920]{1,0:T(8,128)(2,1)S(1)}, u32[]{:S(2)}, u32[]{:S(2)}) collective-permute-start(bf16[48,1920]{1,0:T(8,128)(2,1)} %chip.1), channel_id=1, source_target_pairs={{18,0},{19,1},{20,2},{21,3},{22,4},{23,5},{16,6},{17,7},{26,8},{27... | collective-permute-start | bytes 552968 | tf_op jit(solution)/shard_map/ppermute | solution.py:337
  27.2 28.4 %copy-start = (bf16[4,48,1920]{2,1,0:T(8,128)(2,1)}, bf16[4,48,1920]{2,1,0:T(8,128)(2,1)S(1)}, u32[]{:S(2)}) copy-start(bf16[4,48,1920]{2,1,0:T(8,128)(2,1)S(1)} %pad_maximum_fusion.refs_0_) | copy-start | bytes 2211844
  27.2 21.4 %collective-permute-start.6 = (bf16[4,48,1920]{2,1,0:T(8,128)(2,1)S(1)}, bf16[4,48,1920]{2,1,0:T(8,128)(2,1)S(1)}, u32[]{:S(2)}, u32[]{:S(2)}) collective-permute-start(bf16[4,48,1920]{2,1,0:T(8,128)(2,1)S(1)} %pad_maximum_fusion.refs_0_), channel_id=1, source_target_pairs={{2,0},{3,1},{4,2},{5,3},{6,4},{7,5},{0,6},{1,7},{10,8},{11,9},{12,... | collective-permute-start | bytes 2211848 | tf_op jit(solution)/shard_map/ppermute | solution.py:337
  32.7 17.7 %collective-permute-start.5 = (bf16[4,48,1920]{2,1,0:T(8,128)(2,1)S(1)}, bf16[4,48,1920]{2,1,0:T(8,128)(2,1)S(1)}, u32[]{:S(2)}, u32[]{:S(2)}) collective-permute-start(bf16[4,48,1920]{2,1,0:T(8,128)(2,1)S(1)} %pad_maximum_fusion.refs_0_), channel_id=1, source_target_pairs={{24,0},{25,1},{26,2},{27,3},{28,4},{29,5},{30,6},{31,7},{0,8},{1,9... | collective-permute-start | bytes 2211848 | tf_op jit(solution)/shard_map/ppermute | solution.py:337
  33.0 19.8 %collective-permute-start.4 = (bf16[4,48,1920]{2,1,0:T(8,128)(2,1)S(1)}, bf16[4,48,1920]{2,1,0:T(8,128)(2,1)S(1)}, u32[]{:S(2)}, u32[]{:S(2)}) collective-permute-start(bf16[4,48,1920]{2,1,0:T(8,128)(2,1)S(1)} %pad_maximum_fusion.refs_0_), channel_id=1, source_target_pairs={{8,0},{9,1},{10,2},{11,3},{12,4},{13,5},{14,6},{15,7},{16,8},{17,9... | collective-permute-start | bytes 2211848 | tf_op jit(solution)/shard_map/ppermute | solution.py:337
  35.3 18.3 %collective-permute-start.7 = (bf16[4,48,1920]{2,1,0:T(8,128)(2,1)S(1)}, bf16[4,48,1920]{2,1,0:T(8,128)(2,1)S(1)}, u32[]{:S(2)}, u32[]{:S(2)}) collective-permute-start(bf16[4,48,1920]{2,1,0:T(8,128)(2,1)S(1)} %pad_maximum_fusion.refs_0_), channel_id=1, source_target_pairs={{1,0},{0,1},{3,2},{2,3},{5,4},{4,5},{7,6},{6,7},{9,8},{8,9},{11,10... | collective-permute-start | bytes 2211848 | tf_op jit(solution)/shard_map/ppermute | solution.py:337
  48.7 7.0 %copy-start.2 = (bf16[4,48,1920]{2,1,0:T(8,128)(2,1)}, bf16[4,48,1920]{2,1,0:T(8,128)(2,1)S(1)}, u32[]{:S(2)}) copy-start(bf16[4,48,1920]{2,1,0:T(8,128)(2,1)S(1)} %collective-permute-done.6.refs_3_) | copy-start | bytes 2211844
  48.7 4.9 %collective-permute-start.10 = (bf16[4,48,1920]{2,1,0:T(8,128)(2,1)S(1)}, bf16[4,48,1920]{2,1,0:T(8,128)(2,1)S(1)}, u32[]{:S(2)}, u32[]{:S(2)}) collective-permute-start(bf16[4,48,1920]{2,1,0:T(8,128)(2,1)S(1)} %collective-permute-done.6.refs_3_), channel_id=1, source_target_pairs={{1,0},{0,1},{3,2},{2,3},{5,4},{4,5},{7,6},{6,7},{9,8},{8,9},{11,10... | collective-permute-start | bytes 2211848 | tf_op jit(solution)/shard_map/ppermute | solution.py:337
  50.4 5.3 %copy-start.3 = (bf16[4,48,1920]{2,1,0:T(8,128)(2,1)}, bf16[4,48,1920]{2,1,0:T(8,128)(2,1)S(1)}, u32[]{:S(2)}) copy-start(bf16[4,48,1920]{2,1,0:T(8,128)(2,1)S(1)} %collective-permute-done.5.refs_2_) | copy-start | bytes 2211844
  50.4 4.2 %collective-permute-start.9 = (bf16[4,48,1920]{2,1,0:T(8,128)(2,1)S(1)}, bf16[4,48,1920]{2,1,0:T(8,128)(2,1)S(1)}, u32[]{:S(2)}, u32[]{:S(2)}) collective-permute-start(bf16[4,48,1920]{2,1,0:T(8,128)(2,1)S(1)} %collective-permute-done.5.refs_2_), channel_id=1, source_target_pairs={{1,0},{0,1},{3,2},{2,3},{5,4},{4,5},{7,6},{6,7},{9,8},{8,9},{11,10... | collective-permute-start | bytes 2211848 | tf_op jit(solution)/shard_map/ppermute | solution.py:337
  52.8 2.9 %copy-start.4 = (bf16[4,48,1920]{2,1,0:T(8,128)(2,1)}, bf16[4,48,1920]{2,1,0:T(8,128)(2,1)S(1)}, u32[]{:S(2)}) copy-start(bf16[4,48,1920]{2,1,0:T(8,128)(2,1)S(1)} %collective-permute-done.4.refs_1_) | copy-start | bytes 2211844
  52.8 2.9 %collective-permute-start.8 = (bf16[4,48,1920]{2,1,0:T(8,128)(2,1)S(1)}, bf16[4,48,1920]{2,1,0:T(8,128)(2,1)S(1)}, u32[]{:S(2)}, u32[]{:S(2)}) collective-permute-start(bf16[4,48,1920]{2,1,0:T(8,128)(2,1)S(1)} %collective-permute-done.4.refs_1_), channel_id=1, source_target_pairs={{1,0},{0,1},{3,2},{2,3},{5,4},{4,5},{7,6},{6,7},{9,8},{8,9},{11,10... | collective-permute-start | bytes 2211848 | tf_op jit(solution)/shard_map/ppermute | solution.py:337
  53.6 2.1 %copy-start.5 = (bf16[4,48,1920]{2,1,0:T(8,128)(2,1)}, bf16[4,48,1920]{2,1,0:T(8,128)(2,1)S(1)}, u32[]{:S(2)}) copy-start(bf16[4,48,1920]{2,1,0:T(8,128)(2,1)S(1)} %collective-permute-done.7.refs_4_) | copy-start | bytes 2211844
  53.6 2.1 %copy-start.6 = (bf16[4,48,1920]{2,1,0:T(8,128)(2,1)}, bf16[4,48,1920]{2,1,0:T(8,128)(2,1)S(1)}, u32[]{:S(2)}) copy-start(bf16[4,48,1920]{2,1,0:T(8,128)(2,1)S(1)} %collective-permute-done.10.refs_7_) | copy-start | bytes 2211844
  54.6 1.1 %copy-start.7 = (bf16[4,48,1920]{2,1,0:T(8,128)(2,1)}, bf16[4,48,1920]{2,1,0:T(8,128)(2,1)S(1)}, u32[]{:S(2)}) copy-start(bf16[4,48,1920]{2,1,0:T(8,128)(2,1)S(1)} %collective-permute-done.9.refs_6_) | copy-start | bytes 2211844
  55.7 0.9 copy-start.8
  92.0 3.4 %copy-start.1 = (bf16[16,8,896]{2,1,0:T(8,128)(2,1)}, bf16[16,8,896]{2,1,0:T(8,128)(2,1)S(1)}, u32[]{:S(2)}) copy-start(bf16[16,8,896]{2,1,0:T(8,128)(2,1)S(1)} %all_to_all.5.near_ref) | copy-start | bytes 688132
  92.0 3.4 %collective-permute-start.11 = (bf16[16,8,896]{2,1,0:T(8,128)(2,1)S(1)}, bf16[16,8,896]{2,1,0:T(8,128)(2,1)S(1)}, u32[]{:S(2)}, u32[]{:S(2)}) collective-permute-start(bf16[16,8,896]{2,1,0:T(8,128)(2,1)S(1)} %all_to_all.5.near_ref), channel_id=1, source_target_pairs={{1,0},{0,1},{3,2},{2,3},{5,4},{4,5},{7,6},{6,7},{9,8},{8,9},{11,10... | collective-permute-start | bytes 688136 | tf_op jit(solution)/shard_map/ppermute | solution.py:337
  95.5 0.7 copy-start.9

commit v4 on v3

--- a/solution.py
+++ b/solution.py
@@ -14,7 +14,6 @@
 LOG2E = 1.4426950408889634
 F32 = jnp.float32
 BF16 = jnp.bfloat16
-VMEM_LIMIT = 56 * 2**20
 NT = (((1,), (1,)), ((), ()))
 
 
@@ -38,50 +37,59 @@
 LARGE = ((0, 0), (1, 0), (3, 0), (0, 1))
 
 
-def half_block(half, context_ref, query_ref, wqkv_ref, wout_ref):
-    hidden = query_ref.shape[1]
-    first = half == 0
-    parts = [wqkv_ref[:, b * hidden : (b + 1) * hidden].astype(F32) for b in range(3)] + [wout_ref[...].astype(F32)]
-    parts.append(jnp.concatenate([context_ref[...].astype(F32), query_ref[...].astype(F32)], axis=0))
-    parts = [jnp.where(first, p[:, :HALF], p[:, HALF:]) for p in parts]
-    return jnp.concatenate(parts, axis=1)
-
-
 def place_of_device():
     me = lax.axis_index("dev")
     return me >> 3, (me >> 1) & 3, me & 1
 
 
-def give_kernel(context_ref, query_ref, wqkv_ref, wout_ref, o_ref):
-    core = place_of_device()[2]
-    o_ref[...] = half_block(1 - core, context_ref, query_ref, wqkv_ref, wout_ref).astype(BF16)
-
-
-def chip_kernel(context_ref, query_ref, wqkv_ref, wout_ref, got_ref, o_ref):
-    core = place_of_device()[2]
-    own = half_block(core, context_ref, query_ref, wqkv_ref, wout_ref)
+def cut_kernel(raw_ref, keep_ref, give_ref):
+    first = place_of_device()[2] == 0
+    for b in range(5):
+        low = raw_ref[:, 2 * b * HALF : (2 * b + 1) * HALF].astype(F32)
+        high = raw_ref[:, (2 * b + 1) * HALF : (2 * b + 2) * HALF].astype(F32)
+        keep_ref[:, b * HALF : (b + 1) * HALF] = jnp.where(first, low, high).astype(BF16)
+        give_ref[:, b * HALF : (b + 1) * HALF] = jnp.where(first, high, low).astype(BF16)
+
+
+def cut(raw):
+    vmem = pl.BlockSpec(memory_space=pltpu.VMEM)
+    half = jax.ShapeDtypeStruct((raw.shape[0], BLOCK), BF16)
+    return pl.pallas_call(
+        cut_kernel,
+        out_shape=(half, half),
+        in_specs=[vmem],
+        out_specs=(vmem, vmem),
+        compiler_params=pltpu.CompilerParams(vmem_limit_bytes=4 * 2**20),
+        name="cut",
+    )(raw)
+
+
+def chip_kernel(keep_ref, got_ref, o_ref):
+    first = place_of_device()[2] == 0
+    own = keep_ref[...].astype(F32)
     got = got_ref[...].astype(F32)
-    low = jnp.where(core == 0, own, got)
-    high = jnp.where(core == 0, got, own)
+    low = jnp.where(first, own, got)
+    high = jnp.where(first, got, own)
     o_ref[:, :PROJECT] = jnp.concatenate([low[:, :PROJECT], high[:, :PROJECT]], axis=0).astype(BF16)
     rows = [low[:16, PROJECT:], high[:16, PROJECT:], low[16:, PROJECT:], high[16:, PROJECT:]]
     o_ref[:, PROJECT:] = jnp.concatenate(rows, axis=0).astype(BF16)
 
 
-def build(kernel, rows, name, *arrays):
+def chip(keep, got):
     vmem = pl.BlockSpec(memory_space=pltpu.VMEM)
     return pl.pallas_call(
-        kernel,
-        out_shape=jax.ShapeDtypeStruct((rows, BLOCK), BF16),
-        in_specs=[vmem] * len(arrays),
+        chip_kernel,
+        out_shape=jax.ShapeDtypeStruct((2 * keep.shape[0], BLOCK), BF16),
+        in_specs=[vmem, vmem],
         out_specs=vmem,
-        name=name,
-    )(*arrays)
+        compiler_params=pltpu.CompilerParams(vmem_limit_bytes=4 * 2**20),
+        name="chip",
+    )(keep, got)
 
 
 def layer_kernel(rows, unroll, len_ref, positive_ref, x_ref, gain_ref, *refs):
     pieces, refs = refs[:8], refs[8:]
-    o_ref, tell_ref, told_ref, w_s, wo_s, ctx_s, query_s, q_s, k_s, v_s, kc_s, vc_s, attn_s, sems = refs
+    o_ref, tell_ref, told_ref, w_s, wo_s, ctx_s, query_s, told_s, q_s, k_s, v_s, kc_s, vc_s, attn_s, bias_s, sems = refs
     tokens, hidden = x_ref.shape
     docs = o_ref.shape[0]
     seq = tokens // docs
@@ -90,7 +98,7 @@
     nctx = ctx_s.shape[1] * ctx_s.shape[2]
     scale = LOG2E / HEAD**0.5
     x, z, core = place_of_device()
-    weights, others, last = [], [], []
+    weights, others, last, asked = ([], []), [], [], []
     for side in range(2):
         for p, (ax, az) in enumerate(LARGE):
             piece = pieces[side * 4 + p]
@@ -100,7 +108,7 @@
                 at = pl.multiple_of(chip * 48, 48)
                 here = (core + side) & 1
                 lanes = pl.ds(pl.multiple_of(here * HALF, HALF), HALF)
-                weights.append(
+                weights[side].append(
                     pltpu.make_async_copy(
                         piece.at[k, :, pl.ds(0, WEIGHTS)], w_s.at[side, pl.ds(at, 48)], sems.at[0, n * 4 + k]
                     )
@@ -110,7 +118,7 @@
                         piece.at[k, :, pl.ds(WEIGHTS, HALF)], wo_s.at[pl.ds(at, 48), lanes], sems.at[1, n * 4 + k]
                     )
                 )
-                last.append(
+                asked.append(
                     pltpu.make_async_copy(
                         piece.at[k, pl.ds(32, 16), pl.ds(PROJECT, HALF)], query_s.at[side, chip], sems.at[2, n * 4 + k]
                     )
@@ -120,32 +128,40 @@
                     piece.at[:, pl.ds(0, 32), pl.ds(PROJECT, HALF)], ctx_s.at[side, pl.ds(4 * p, 4)], sems.at[3, n]
                 )
             )
-    for copy in weights + others + last:
+    for copy in weights[0] + others + weights[1] + asked:
         copy.start()
-    for copy in weights:
+
+    def project(side, i, _):
+        r = pl.ds(pl.multiple_of(i * rows, rows), rows)
+        t = jnp.dot(x_ref[r, :], w_s[side], preferred_element_type=F32)
+        q_s[r, side * HALF : (side + 1) * HALF] = (t[:, :HALF] * scale).astype(BF16)
+        for begin, out in ((HALF, k_s), (2 * HALF, v_s)):
+            for j in range(per):
+                even, odd = halves(t[:, begin + j * PAIR : begin + (j + 1) * PAIR])
+                for e in range(rows // seq):
+                    d = i * (rows // seq) + e
+                    out[side * per + j, d, :seq] = even[e * seq : (e + 1) * seq]
+                    out[side * per + j, d, seq:] = odd[e * seq : (e + 1) * seq]
+        return 0
+
+    for side in range(2):
+        for copy in weights[side]:
+            copy.wait()
+        lax.fori_loop(0, tokens // rows, functools.partial(project, side), 0)
+    for copy in last:
+        copy.start()
+    for copy in others + asked:
         copy.wait()
-
-    def project(i, _):
-        r = pl.ds(pl.multiple_of(i * rows, rows), rows)
-        states = x_ref[r, :]
-        for side in range(2):
-            t = jnp.dot(states, w_s[side], preferred_element_type=F32)
-            q_s[r, side * HALF : (side + 1) * HALF] = (t[:, :HALF] * scale).astype(BF16)
-            for begin, out in ((HALF, k_s), (2 * HALF, v_s)):
-                for j in range(per):
-                    even, odd = halves(t[:, begin + j * PAIR : begin + (j + 1) * PAIR])
-                    for e in range(rows // seq):
-                        d = i * (rows // seq) + e
-                        out[side * per + j, d, :seq] = even[e * seq : (e + 1) * seq]
-                        out[side * per + j, d, seq:] = odd[e * seq : (e + 1) * seq]
-        return 0
-
-    lax.fori_loop(0, tokens // rows, project, 0)
-    for copy in others:
-        copy.wait()
+    first = core == 0
+    count = told_ref.shape[0]
+    near = query_s[0].reshape(count, HALF)
+    far = query_s[1].reshape(count, HALF)
+    told_s[:, :HALF] = jnp.where(first, near, far)
+    told_s[:, HALF:] = jnp.where(first, far, near)
+    told_copy = pltpu.make_async_copy(told_s, told_ref, sems.at[3, 17])
+    told_copy.start()
     near = ctx_s[0].reshape(nctx, HALF)
     far = ctx_s[1].reshape(nctx, HALF)
-    first = core == 0
     ctx = jnp.concatenate([jnp.where(first, near, far), jnp.where(first, far, near)], axis=1)
     for side in range(2):
         t = jnp.dot(ctx, w_s[side, :, HALF:], preferred_element_type=F32)
@@ -156,16 +172,22 @@
                 out[side * per + j, nctx:] = odd
     ones_ctx = ones_beside(nctx)
     ones_own = ones_beside(seq)
+    column = lax.broadcasted_iota(jnp.int32, (docs, docs), 0) == lax.broadcasted_iota(jnp.int32, (docs, docs), 1)
+
+    def down(ref):
+        return jnp.sum(jnp.where(column, ref[...].reshape(1, docs).astype(F32), 0.0), axis=1, keepdims=True)
+
+    lengths = down(len_ref)
     slot = lax.broadcasted_iota(jnp.int32, (1, 2 * seq), 1)
-    slot = jnp.where(slot < seq, slot, slot - seq)
+    slot = jnp.where(slot < seq, slot, slot - seq).astype(F32)
+    bias_s[...] = jnp.where(slot < lengths, 0.0, -jnp.inf)
     for j in range(pairs):
 
         def doc(d, _):
             r = pl.ds(pl.multiple_of(d * seq, seq), seq)
             q = q_s[r, j * PAIR : (j + 1) * PAIR]
-            bias = jnp.where(slot < len_ref[d], 0.0, -jnp.inf).astype(F32)
             score_ctx = lax.dot_general(q, kc_s[j], NT, preferred_element_type=F32)
-            score_own = lax.dot_general(q, k_s[j, d], NT, preferred_element_type=F32) + bias
+            score_own = lax.dot_general(q, k_s[j, d], NT, preferred_element_type=F32) + bias_s[pl.ds(d, 1), :]
             p_ctx, p_own = [], []
             for e in range(2):
                 c = score_ctx[:, e * nctx : (e + 1) * nctx]
@@ -189,7 +211,7 @@
         lax.fori_loop(0, docs, doc, 0, unroll=unroll)
     for copy in last:
         copy.wait()
-    position = lax.broadcasted_iota(jnp.int32, (seq, 1), 0)
+    position = lax.broadcasted_iota(jnp.int32, (seq, 1), 0).astype(F32)
     pooled = []
     for g in range(0, docs, 2):
         both = slice(g * seq, (g + 2) * seq)
@@ -199,23 +221,16 @@
             center = jnp.mean(h, axis=1, keepdims=True)
             off = h - center
             spread = jnp.mean(off * off, axis=1, keepdims=True)
-            length = len_ref[d]
+            length = lengths[d : d + 1]
             weight = jnp.where(position < length, lax.rsqrt(spread + EPSILON), 0.0)
-            pooled.append(jnp.sum(off * weight, axis=0, keepdims=True) / length.astype(F32))
-    embed = jnp.concatenate(pooled, axis=0) * gain_ref[...]
+            pooled.append(jnp.sum(off * weight, axis=0, keepdims=True) / length)
+    embed = jnp.concatenate(pooled, axis=0) * gain_ref[...].reshape(1, hidden)
     o_ref[...] = embed.astype(BF16)
-    row = lax.broadcasted_iota(jnp.int32, (docs, 128), 0)
-    beside = jnp.zeros((docs, 128), F32)
-    for i in range(docs):
-        beside = jnp.where(row == i, positive_ref[i].astype(F32), beside)
+    beside = jnp.broadcast_to(down(positive_ref), (docs, 128))
     tell = jnp.concatenate([embed, beside], axis=1).astype(BF16)
     for i in range(tell_ref.shape[0]):
         tell_ref[i] = tell
-    count = told_ref.shape[0]
-    near = query_s[0].reshape(count, HALF)
-    far = query_s[1].reshape(count, HALF)
-    told_ref[:, :HALF] = jnp.where(first, near, far)
-    told_ref[:, HALF:] = jnp.where(first, far, near)
+    told_copy.wait()
 
 
 def layer(lengths, positive, x, gain, pieces, seq):
@@ -224,9 +239,8 @@
     pairs = hidden // PAIR
     chips = 16
     nctx = chips * 32
-    rows = 2 * seq
+    rows = 4 * seq
     vmem = pl.BlockSpec(memory_space=pltpu.VMEM)
-    smem = pl.BlockSpec(memory_space=pltpu.SMEM)
     hbm = pl.BlockSpec(memory_space=pl.ANY)
     return pl.pallas_call(
         functools.partial(layer_kernel, rows, docs),
@@ -235,24 +249,26 @@
             jax.ShapeDtypeStruct((chips, docs, hidden + 128), BF16),
             jax.ShapeDtypeStruct((chips * 16, hidden), BF16),
         ),
-        in_specs=[smem, smem, vmem, vmem] + [hbm] * 8,
-        out_specs=(vmem, vmem, vmem),
+        in_specs=[vmem, vmem, vmem, vmem] + [hbm] * 8,
+        out_specs=(vmem, vmem, hbm),
         scratch_shapes=[
             pltpu.VMEM((2, hidden, WEIGHTS), BF16),
             pltpu.VMEM((hidden, hidden), BF16),
             pltpu.VMEM((2, chips, 32, HALF), BF16),
             pltpu.VMEM((2, chips, 16, HALF), BF16),
+            pltpu.VMEM((chips * 16, hidden), BF16),
             pltpu.VMEM((tokens, hidden), BF16),
             pltpu.VMEM((pairs, docs, 2 * seq, PAIR), BF16),
             pltpu.VMEM((pairs, docs, 2 * seq, PAIR), BF16),
             pltpu.VMEM((pairs, 2 * nctx, PAIR), BF16),
             pltpu.VMEM((pairs, 2 * nctx, PAIR), BF16),
             pltpu.VMEM((tokens, hidden), BF16),
+            pltpu.VMEM((docs, 2 * seq), F32),
             pltpu.SemaphoreType.DMA((4, 32)),
         ],
-        compiler_params=pltpu.CompilerParams(vmem_limit_bytes=VMEM_LIMIT),
+        compiler_params=pltpu.CompilerParams(vmem_limit_bytes=32 * 2**20),
         name="layer",
-    )(lengths, positive, x, gain.reshape(1, hidden), *pieces)
+    )(lengths, positive, x, gain, *pieces)
 
 
 def exact_dot(a, b):
@@ -322,7 +338,7 @@
             pltpu.VMEM((16, docs), F32),
             pltpu.VMEM((docs, 128), F32),
         ],
-        compiler_params=pltpu.CompilerParams(vmem_limit_bytes=VMEM_LIMIT),
+        compiler_params=pltpu.CompilerParams(vmem_limit_bytes=8 * 2**20),
         name="contrast",
     )(told, near, far)
 
@@ -340,9 +356,9 @@
 def local(doc_states, context_embeds, w_qkv, w_out, ln_gain, queries, positive, lengths):
     docs, seq, hidden = doc_states.shape
     x = doc_states.reshape(docs * seq, hidden)
-    arrays = (context_embeds, queries, w_qkv, w_out)
-    got = fetch(build(give_kernel, 24, "give", *arrays), dcore=1)
-    block = build(chip_kernel, 48, "chip", *arrays, got)
+    rows = jnp.concatenate([context_embeds, queries], axis=0)
+    keep, give = cut(jnp.concatenate([w_qkv, w_out, rows], axis=1))
+    block = chip(keep, fetch(give, dcore=1))
     four = jnp.stack([block] + [fetch(block, dx, dz) for dx, dz in SMALL[1:]])
     near = [four] + [fetch(four, dx, dz) for dx, dz in LARGE[1:]]
     far = [fetch(piece, dcore=1) for piece in near]

time: 99.5 us -> 90.9 us (0.914)
  Pallas kernels: 29.2 us -> 23.2 us
  local copies, waits for them, and re-layouts: 2.86 us -> 0.02 us
    pallas_call x2, Pallas kernels: 3.32 us -> 0.1 us  [the longest x1 0.05 us: cut(): pl.pallas_call(cut_kernel, out_shape=(half, half), in_specs=[vmem], out_s...]
    unnamed x24 -> x8, local copies, waits for them, and re-layouts: 2.15 us -> 0.02 us
    pallas_call x1, Pallas kernels: 22.8 us -> 21.2 us  [layer(): pl.pallas_call(functools.partial(layer_kernel, rows, docs), out_shape=(ja...]
    pallas_call x1, Pallas kernels: 3.08 us -> 1.91 us  [contrast(): pl.pallas_call(contrast_kernel, out_shape=(jax.ShapeDtypeStruct((mine, hi...]
    concatenate x0 -> x1, other arithmetic: none -> 1.08 us  [local(): keep, give = cut(jnp.concatenate([w_qkv, w_out, rows], axis=1))]
  transfers between devices with their start and end apart: 12 -> 12, of which waited for: 8 -> 8; matrix products, arithmetic and copies ran while one was open for 1% -> 0% of each run, Pallas kernels for 0% -> 0%
where the time goes in v4:
time: 90.9 us; the launch traced here: 90.7 us
  waiting for transfers between devices  27.5 us (30%)
  starting transfers between devices  25.7 us (28%)
  Pallas kernels  23.2 us (26%)
  blocking collectives  12.4 us (14%)
  other arithmetic  1.2 us (1%)
    ppermute x12, waiting for transfers between devices, fetch(): return lax.ppermute(value, 'dev', moves)  27.5 us
    ppermute x12, starting transfers between devices, fetch(): return lax.ppermute(value, 'dev', moves)  25.7 us
    pallas_call x1, Pallas kernels, layer(): pl.pallas_call(functools.partial(layer_kernel, rows, docs), out_shape=(ja...  21.2 us
    all_to_all x1, blocking collectives, local(): near = lax.all_to_all(tell, 'dev', 0, 0, axis_index_groups=chips)  12.4 us
    pallas_call x1, Pallas kernels, contrast(): pl.pallas_call(contrast_kernel, out_shape=(jax.ShapeDtypeStruct((mine, hi...  1.91 us
  transfers between devices with their start and end apart: 12, of which 8 were waited for; matrix products, arithmetic and copies ran while one was open for 0% of the time, Pallas kernels for 0%

profile of v4, /device:TPU:1, one launch (start us, length us, event | category | flops | bytes accessed | tf_op | source)
XLA Modules:
  0.0 90.7 jit_solution(6599662437644079753)
XLA Ops:
  0.6 0.0 copy-start.2
  0.6 0.0 copy-start.3
  0.7 0.0 copy-start.1
  0.7 0.0 copy-start
  0.7 1.1 %maximum_maximum_fusion.raw_ref = bf16[24,3840]{1,0:T(8,128)(2,1)S(1)} fusion(bf16[8,768]{1,0:T(8,128)(2,1)} %param.13, bf16[16,768]{1,0:T(8,128)(2,1)} %param.9, bf16[24,768]{1,0:T(8,128)(2,1)} %param.11, bf16[24,2304]{1,0:T(8,128)(2,1)} %param.10), kind=kLoop, calls=%fused_computation.1 | loop fusion | flops 737280 | bytes 368640 | tf_op jit(solution)/shard_map/concatenate | solution.py:360
  1.8 0.1 cut.1
  1.8 3.3 %collective-permute-start = (bf16[24,1920]{1,0:T(8,128)(2,1)S(1)}, bf16[24,1920]{1,0:T(8,128)(2,1)S(1)}, u32[]{:S(2)}, u32[]{:S(2)}) collective-permute-start(bf16[24,1920]{1,0:T(8,128)(2,1)S(1)} %get-tuple-element.13), channel_id=1, source_target_pairs={{1,0},{0,1},{3,2},{2,3},{5,4},{4,5},{7,6},{6,7},{9,8},{8,9},{11,10... | collective-permute-start | bytes 276488 | tf_op jit(solution)/shard_map/ppermute | solution.py:353
  5.1 0.9 %collective-permute-done.got_ref = bf16[24,1920]{1,0:T(8,128)(2,1)S(1)} collective-permute-done((bf16[24,1920]{1,0:T(8,128)(2,1)S(1)}, bf16[24,1920]{1,0:T(8,128)(2,1)S(1)}, u32[]{:S(2)}, u32[]{:S(2)}) %collective-permute-start) | collective-permute-done | bytes 92192 | tf_op jit(solution)/shard_map/ppermute | solution.py:353
  6.1 2.4 %collective-permute-start.3 = (bf16[48,1920]{1,0:T(8,128)(2,1)S(1)}, bf16[48,1920]{1,0:T(8,128)(2,1)S(1)}, u32[]{:S(2)}, u32[]{:S(2)}) collective-permute-start(bf16[48,1920]{1,0:T(8,128)(2,1)S(1)} %chip.1), channel_id=1, source_target_pairs={{22,0},{23,1},{16,2},{17,3},{18,4},{19,5},{20,6},{21,7},{30,8},{31... | collective-permute-start | bytes 552968 | tf_op jit(solution)/shard_map/ppermute | solution.py:353
  8.6 3.0 %collective-permute-start.2 = (bf16[48,1920]{1,0:T(8,128)(2,1)S(1)}, bf16[48,1920]{1,0:T(8,128)(2,1)S(1)}, u32[]{:S(2)}, u32[]{:S(2)}) collective-permute-start(bf16[48,1920]{1,0:T(8,128)(2,1)S(1)} %chip.1), channel_id=1, source_target_pairs={{4,0},{5,1},{6,2},{7,3},{0,4},{1,5},{2,6},{3,7},{12,8},{13,9},{14,... | collective-permute-start | bytes 552968 | tf_op jit(solution)/shard_map/ppermute | solution.py:353
  11.6 0.7 collective-permute-start.1
  12.2 4.1 %collective-permute-done.3 = bf16[48,1920]{1,0:T(8,128)(2,1)S(1)} collective-permute-done((bf16[48,1920]{1,0:T(8,128)(2,1)S(1)}, bf16[48,1920]{1,0:T(8,128)(2,1)S(1)}, u32[]{:S(2)}, u32[]{:S(2)}) %collective-permute-start.3) | collective-permute-done | bytes 184352 | tf_op jit(solution)/shard_map/ppermute | solution.py:353
  16.3 6.9 %collective-permute-done.2 = bf16[48,1920]{1,0:T(8,128)(2,1)S(1)} collective-permute-done((bf16[48,1920]{1,0:T(8,128)(2,1)S(1)}, bf16[48,1920]{1,0:T(8,128)(2,1)S(1)}, u32[]{:S(2)}, u32[]{:S(2)}) %collective-permute-start.2) | collective-permute-done | bytes 184352 | tf_op jit(solution)/shard_map/ppermute | solution.py:353
  23.2 0.0 collective-permute-done.1
  23.2 0.1 pad_maximum_fusion.refs_0_
  23.3 5.4 %collective-permute-start.6 = (bf16[4,48,1920]{2,1,0:T(8,128)(2,1)S(1)}, bf16[4,48,1920]{2,1,0:T(8,128)(2,1)S(1)}, u32[]{:S(2)}, u32[]{:S(2)}) collective-permute-start(bf16[4,48,1920]{2,1,0:T(8,128)(2,1)S(1)} %pad_maximum_fusion.refs_0_), channel_id=1, source_target_pairs={{2,0},{3,1},{4,2},{5,3},{6,4},{7,5},{0,6},{1,7},{10,8},{11,9},{12,... | collective-permute-start | bytes 2211848 | tf_op jit(solution)/shard_map/ppermute | solution.py:353
  28.7 0.3 collective-permute-start.5
  29.1 2.4 %collective-permute-start.4 = (bf16[4,48,1920]{2,1,0:T(8,128)(2,1)S(1)}, bf16[4,48,1920]{2,1,0:T(8,128)(2,1)S(1)}, u32[]{:S(2)}, u32[]{:S(2)}) collective-permute-start(bf16[4,48,1920]{2,1,0:T(8,128)(2,1)S(1)} %pad_maximum_fusion.refs_0_), channel_id=1, source_target_pairs={{8,0},{9,1},{10,2},{11,3},{12,4},{13,5},{14,6},{15,7},{16,8},{17,9... | collective-permute-start | bytes 2211848 | tf_op jit(solution)/shard_map/ppermute | solution.py:353
  31.4 2.0 %collective-permute-start.7 = (bf16[4,48,1920]{2,1,0:T(8,128)(2,1)S(1)}, bf16[4,48,1920]{2,1,0:T(8,128)(2,1)S(1)}, u32[]{:S(2)}, u32[]{:S(2)}) collective-permute-start(bf16[4,48,1920]{2,1,0:T(8,128)(2,1)S(1)} %pad_maximum_fusion.refs_0_), channel_id=1, source_target_pairs={{1,0},{0,1},{3,2},{2,3},{5,4},{4,5},{7,6},{6,7},{9,8},{8,9},{11,10... | collective-permute-start | bytes 2211848 | tf_op jit(solution)/shard_map/ppermute | solution.py:353
  33.4 11.2 %collective-permute-done.6.refs_3_ = bf16[4,48,1920]{2,1,0:T(8,128)(2,1)S(1)} collective-permute-done((bf16[4,48,1920]{2,1,0:T(8,128)(2,1)S(1)}, bf16[4,48,1920]{2,1,0:T(8,128)(2,1)S(1)}, u32[]{:S(2)}, u32[]{:S(2)}) %collective-permute-start.6) | collective-permute-done | bytes 737312 | tf_op jit(solution)/shard_map/ppermute | solution.py:353
  44.7 1.4 %collective-permute-start.10 = (bf16[4,48,1920]{2,1,0:T(8,128)(2,1)S(1)}, bf16[4,48,1920]{2,1,0:T(8,128)(2,1)S(1)}, u32[]{:S(2)}, u32[]{:S(2)}) collective-permute-start(bf16[4,48,1920]{2,1,0:T(8,128)(2,1)S(1)} %collective-permute-done.6.refs_3_), channel_id=1, source_target_pairs={{1,0},{0,1},{3,2},{2,3},{5,4},{4,5},{7,6},{6,7},{9,8},{8,9},{11,10... | collective-permute-start | bytes 2211848 | tf_op jit(solution)/shard_map/ppermute | solution.py:353
  46.1 0.4 collective-permute-done.5.refs_2_
  46.5 2.4 %collective-permute-start.9 = (bf16[4,48,1920]{2,1,0:T(8,128)(2,1)S(1)}, bf16[4,48,1920]{2,1,0:T(8,128)(2,1)S(1)}, u32[]{:S(2)}, u32[]{:S(2)}) collective-permute-start(bf16[4,48,1920]{2,1,0:T(8,128)(2,1)S(1)} %collective-permute-done.5.refs_2_), channel_id=1, source_target_pairs={{1,0},{0,1},{3,2},{2,3},{5,4},{4,5},{7,6},{6,7},{9,8},{8,9},{11,10... | collective-permute-start | bytes 2211848 | tf_op jit(solution)/shard_map/ppermute | solution.py:353
  48.9 0.0 collective-permute-done.4.refs_1_
  48.9 0.0 collective-permute-start.8
  48.9 0.0 collective-permute-done.7.refs_4_
  48.9 0.0 collective-permute-done.10.refs_7_
  48.9 1.8 %collective-permute-done.9.refs_6_ = bf16[4,48,1920]{2,1,0:T(8,128)(2,1)S(1)} collective-permute-done((bf16[4,48,1920]{2,1,0:T(8,128)(2,1)S(1)}, bf16[4,48,1920]{2,1,0:T(8,128)(2,1)S(1)}, u32[]{:S(2)}, u32[]{:S(2)}) %collective-permute-start.9) | collective-permute-done | bytes 737312 | tf_op jit(solution)/shard_map/ppermute | solution.py:353
  50.7 1.1 %collective-permute-done.8.refs_5_ = bf16[4,48,1920]{2,1,0:T(8,128)(2,1)S(1)} collective-permute-done((bf16[4,48,1920]{2,1,0:T(8,128)(2,1)S(1)}, bf16[4,48,1920]{2,1,0:T(8,128)(2,1)S(1)}, u32[]{:S(2)}, u32[]{:S(2)}) %collective-permute-start.8) | collective-permute-done | bytes 737312 | tf_op jit(solution)/shard_map/ppermute | solution.py:353
  51.7 0.0 copy-done.2
  51.8 0.0 copy-done.3
  51.8 0.0 copy-done.1
  51.8 0.0 copy-done
  51.8 21.2 %layer.1 = (bf16[8,768]{1,0:T(8,128)(2,1)}, bf16[16,8,896]{2,1,0:T(8,128)(2,1)S(1)}, bf16[256,768]{1,0:T(8,128)(2,1)S(1)}) custom-call(s32[8]{0:T(128)S(1)} %copy-done.2, s32[8]{0:T(128)S(1)} %copy-done.3, bf16[1024,768]{1,0:T(8,128)(2,1)S(1)} %bitcast.6, f32[768]{0:T(1024)S(1)} %copy-done.1, bf16[4,48,1920]{2,1,0:T(8,128)(2,1)S(1)} %pad_maximum_fusion.refs_0_, ...), custom_call_target="tpu_custom_call" | custom-call | tf_op jit(solution)/shard_map/layer/pallas_call | solution.py:245
  73.0 12.4 %all_to_all.5.near_ref = bf16[16,8,896]{2,1,0:T(8,128)(2,1)S(1)} all-to-all(bf16[16,8,896]{2,1,0:T(8,128)(2,1)S(1)} %get-tuple-element.16), channel_id=1, replica_groups={{0,2,4,6,8,10,12,14,16,18,20,22,24,26,28,30},{1,3,5,7,9,11,13,15,17,19,..., dimensions={0} | all-to-all | bytes 458752 | tf_op jit(solution)/shard_map/all_to_all | solution.py:367
  85.4 2.3 %collective-permute-start.11 = (bf16[16,8,896]{2,1,0:T(8,128)(2,1)S(1)}, bf16[16,8,896]{2,1,0:T(8,128)(2,1)S(1)}, u32[]{:S(2)}, u32[]{:S(2)}) collective-permute-start(bf16[16,8,896]{2,1,0:T(8,128)(2,1)S(1)} %all_to_all.5.near_ref), channel_id=1, source_target_pairs={{1,0},{0,1},{3,2},{2,3},{5,4},{4,5},{7,6},{6,7},{9,8},{8,9},{11,10... | collective-permute-start | bytes 688136 | tf_op jit(solution)/shard_map/ppermute | solution.py:353
  87.7 1.1 %collective-permute-done.11.far_ref = bf16[16,8,896]{2,1,0:T(8,128)(2,1)S(1)} collective-permute-done((bf16[16,8,896]{2,1,0:T(8,128)(2,1)S(1)}, bf16[16,8,896]{2,1,0:T(8,128)(2,1)S(1)}, u32[]{:S(2)}, u32[]{:S(2)}) %collective-permute-start.11) | collective-permute-done | bytes 229408 | tf_op jit(solution)/shard_map/ppermute | solution.py:353
  88.8 1.9 %contrast.1 = (f32[8,768]{1,0:T(8,128)}, f32[8,768]{1,0:T(8,128)}, f32[1,8]{1,0:T(1,128)}) custom-call(bf16[256,768]{1,0:T(8,128)(2,1)S(1)} %get-tuple-element.15.told_ref, bf16[16,8,896]{2,1,0:T(8,128)(2,1)S(1)} %all_to_all.5.near_ref, bf16[16,8,896]{2,1,0:T(8,128)(2,1)S(1)} %collective-permute-done.11.far_ref), custom_call_target="tpu_custom_call" | custom-call | tf_op jit(solution)/shard_map/contrast/pallas_call | solution.py:327
  (1 shorter events, 0.0 us)
Async XLA Ops:
  0.6 51.1 %copy-start.2 = (s32[8]{0:T(128)S(1)}, s32[8]{0:T(128)}, u32[]{:S(2)}) copy-start(s32[8]{0:T(128)} %len_ref.1) | copy-start | bytes 100
  0.6 51.1 %copy-start.3 = (s32[8]{0:T(128)S(1)}, s32[8]{0:T(128)}, u32[]{:S(2)}) copy-start(s32[8]{0:T(128)} %positive_ref.1) | copy-start | bytes 100
  0.7 51.1 %copy-start.1 = (f32[768]{0:T(1024)S(1)}, f32[768]{0:T(1024)}, u32[]{:S(2)}) copy-start(f32[768]{0:T(1024)} %gain_ref.1) | copy-start | bytes 9220
  0.7 51.1 %copy-start = (bf16[8,128,768]{2,1,0:T(8,128)(2,1)S(1)}, bf16[8,128,768]{2,1,0:T(8,128)(2,1)}, u32[]{:S(2)}) copy-start(bf16[8,128,768]{2,1,0:T(8,128)(2,1)} %param.8) | copy-start | bytes 4718596
  1.8 4.3 %collective-permute-start = (bf16[24,1920]{1,0:T(8,128)(2,1)S(1)}, bf16[24,1920]{1,0:T(8,128)(2,1)S(1)}, u32[]{:S(2)}, u32[]{:S(2)}) collective-permute-start(bf16[24,1920]{1,0:T(8,128)(2,1)S(1)} %get-tuple-element.13), channel_id=1, source_target_pairs={{1,0},{0,1},{3,2},{2,3},{5,4},{4,5},{7,6},{6,7},{9,8},{8,9},{11,10... | collective-permute-start | bytes 276488 | tf_op jit(solution)/shard_map/ppermute | solution.py:353
  6.1 10.2 %collective-permute-start.3 = (bf16[48,1920]{1,0:T(8,128)(2,1)S(1)}, bf16[48,1920]{1,0:T(8,128)(2,1)S(1)}, u32[]{:S(2)}, u32[]{:S(2)}) collective-permute-start(bf16[48,1920]{1,0:T(8,128)(2,1)S(1)} %chip.1), channel_id=1, source_target_pairs={{22,0},{23,1},{16,2},{17,3},{18,4},{19,5},{20,6},{21,7},{30,8},{31... | collective-permute-start | bytes 552968 | tf_op jit(solution)/shard_map/ppermute | solution.py:353
  8.6 14.6 %collective-permute-start.2 = (bf16[48,1920]{1,0:T(8,128)(2,1)S(1)}, bf16[48,1920]{1,0:T(8,128)(2,1)S(1)}, u32[]{:S(2)}, u32[]{:S(2)}) collective-permute-start(bf16[48,1920]{1,0:T(8,128)(2,1)S(1)} %chip.1), channel_id=1, source_target_pairs={{4,0},{5,1},{6,2},{7,3},{0,4},{1,5},{2,6},{3,7},{12,8},{13,9},{14,... | collective-permute-start | bytes 552968 | tf_op jit(solution)/shard_map/ppermute | solution.py:353
  11.6 11.7 %collective-permute-start.1 = (bf16[48,1920]{1,0:T(8,128)(2,1)S(1)}, bf16[48,1920]{1,0:T(8,128)(2,1)S(1)}, u32[]{:S(2)}, u32[]{:S(2)}) collective-permute-start(bf16[48,1920]{1,0:T(8,128)(2,1)S(1)} %chip.1), channel_id=1, source_target_pairs={{18,0},{19,1},{20,2},{21,3},{22,4},{23,5},{16,6},{17,7},{26,8},{27... | collective-permute-start | bytes 552968 | tf_op jit(solution)/shard_map/ppermute | solution.py:353
  23.3 21.3 %collective-permute-start.6 = (bf16[4,48,1920]{2,1,0:T(8,128)(2,1)S(1)}, bf16[4,48,1920]{2,1,0:T(8,128)(2,1)S(1)}, u32[]{:S(2)}, u32[]{:S(2)}) collective-permute-start(bf16[4,48,1920]{2,1,0:T(8,128)(2,1)S(1)} %pad_maximum_fusion.refs_0_), channel_id=1, source_target_pairs={{2,0},{3,1},{4,2},{5,3},{6,4},{7,5},{0,6},{1,7},{10,8},{11,9},{12,... | collective-permute-start | bytes 2211848 | tf_op jit(solution)/shard_map/ppermute | solution.py:353
  28.7 17.7 %collective-permute-start.5 = (bf16[4,48,1920]{2,1,0:T(8,128)(2,1)S(1)}, bf16[4,48,1920]{2,1,0:T(8,128)(2,1)S(1)}, u32[]{:S(2)}, u32[]{:S(2)}) collective-permute-start(bf16[4,48,1920]{2,1,0:T(8,128)(2,1)S(1)} %pad_maximum_fusion.refs_0_), channel_id=1, source_target_pairs={{24,0},{25,1},{26,2},{27,3},{28,4},{29,5},{30,6},{31,7},{0,8},{1,9... | collective-permute-start | bytes 2211848 | tf_op jit(solution)/shard_map/ppermute | solution.py:353
  29.1 19.8 %collective-permute-start.4 = (bf16[4,48,1920]{2,1,0:T(8,128)(2,1)S(1)}, bf16[4,48,1920]{2,1,0:T(8,128)(2,1)S(1)}, u32[]{:S(2)}, u32[]{:S(2)}) collective-permute-start(bf16[4,48,1920]{2,1,0:T(8,128)(2,1)S(1)} %pad_maximum_fusion.refs_0_), channel_id=1, source_target_pairs={{8,0},{9,1},{10,2},{11,3},{12,4},{13,5},{14,6},{15,7},{16,8},{17,9... | collective-permute-start | bytes 2211848 | tf_op jit(solution)/shard_map/ppermute | solution.py:353
  31.4 17.4 %collective-permute-start.7 = (bf16[4,48,1920]{2,1,0:T(8,128)(2,1)S(1)}, bf16[4,48,1920]{2,1,0:T(8,128)(2,1)S(1)}, u32[]{:S(2)}, u32[]{:S(2)}) collective-permute-start(bf16[4,48,1920]{2,1,0:T(8,128)(2,1)S(1)} %pad_maximum_fusion.refs_0_), channel_id=1, source_target_pairs={{1,0},{0,1},{3,2},{2,3},{5,4},{4,5},{7,6},{6,7},{9,8},{8,9},{11,10... | collective-permute-start | bytes 2211848 | tf_op jit(solution)/shard_map/ppermute | solution.py:353
  44.7 4.2 %collective-permute-start.10 = (bf16[4,48,1920]{2,1,0:T(8,128)(2,1)S(1)}, bf16[4,48,1920]{2,1,0:T(8,128)(2,1)S(1)}, u32[]{:S(2)}, u32[]{:S(2)}) collective-permute-start(bf16[4,48,1920]{2,1,0:T(8,128)(2,1)S(1)} %collective-permute-done.6.refs_3_), channel_id=1, source_target_pairs={{1,0},{0,1},{3,2},{2,3},{5,4},{4,5},{7,6},{6,7},{9,8},{8,9},{11,10... | collective-permute-start | bytes 2211848 | tf_op jit(solution)/shard_map/ppermute | solution.py:353
  46.5 4.2 %collective-permute-start.9 = (bf16[4,48,1920]{2,1,0:T(8,128)(2,1)S(1)}, bf16[4,48,1920]{2,1,0:T(8,128)(2,1)S(1)}, u32[]{:S(2)}, u32[]{:S(2)}) collective-permute-start(bf16[4,48,1920]{2,1,0:T(8,128)(2,1)S(1)} %collective-permute-done.5.refs_2_), channel_id=1, source_target_pairs={{1,0},{0,1},{3,2},{2,3},{5,4},{4,5},{7,6},{6,7},{9,8},{8,9},{11,10... | collective-permute-start | bytes 2211848 | tf_op jit(solution)/shard_map/ppermute | solution.py:353
  48.9 2.9 %collective-permute-start.8 = (bf16[4,48,1920]{2,1,0:T(8,128)(2,1)S(1)}, bf16[4,48,1920]{2,1,0:T(8,128)(2,1)S(1)}, u32[]{:S(2)}, u32[]{:S(2)}) collective-permute-start(bf16[4,48,1920]{2,1,0:T(8,128)(2,1)S(1)} %collective-permute-done.4.refs_1_), channel_id=1, source_target_pairs={{1,0},{0,1},{3,2},{2,3},{5,4},{4,5},{7,6},{6,7},{9,8},{8,9},{11,10... | collective-permute-start | bytes 2211848 | tf_op jit(solution)/shard_map/ppermute | solution.py:353
  85.4 3.4 %collective-permute-start.11 = (bf16[16,8,896]{2,1,0:T(8,128)(2,1)S(1)}, bf16[16,8,896]{2,1,0:T(8,128)(2,1)S(1)}, u32[]{:S(2)}, u32[]{:S(2)}) collective-permute-start(bf16[16,8,896]{2,1,0:T(8,128)(2,1)S(1)} %all_to_all.5.near_ref), channel_id=1, source_target_pairs={{1,0},{0,1},{3,2},{2,3},{5,4},{4,5},{7,6},{6,7},{9,8},{8,9},{11,10... | collective-permute-start | bytes 688136 | tf_op jit(solution)/shard_map/ppermute | solution.py:353

commit v5 on v4

--- a/solution.py
+++ b/solution.py
@@ -104,7 +104,7 @@
             piece = pieces[side * 4 + p]
             n = side * 4 + p
             for k, (bx, bz) in enumerate(SMALL):
-                chip = ((x + ax + bx) & 3) * 4 + ((z + az + bz) & 3)
+                chip = ((x + ax + bx) & 3) * 4 + (((z ^ az) + bz) & 3)
                 at = pl.multiple_of(chip * 48, 48)
                 here = (core + side) & 1
                 lanes = pl.ds(pl.multiple_of(here * HALF, HALF), HALF)
@@ -343,9 +343,9 @@
     )(told, near, far)
 
 
-def fetch(value, dx=0, dz=0, dcore=0):
+def fetch(value, dx=0, dz=0, pair=0, dcore=0):
     moves = [
-        ((x + dx) % 4 * 8 + (z + dz) % 4 * 2 + (core ^ dcore), x * 8 + z * 2 + core)
+        ((x + dx) % 4 * 8 + ((z ^ pair) + dz) % 4 * 2 + (core ^ dcore), x * 8 + z * 2 + core)
         for x in range(4)
         for z in range(4)
         for core in range(2)
@@ -360,7 +360,7 @@
     keep, give = cut(jnp.concatenate([w_qkv, w_out, rows], axis=1))
     block = chip(keep, fetch(give, dcore=1))
     four = jnp.stack([block] + [fetch(block, dx, dz) for dx, dz in SMALL[1:]])
-    near = [four] + [fetch(four, dx, dz) for dx, dz in LARGE[1:]]
+    near = [four] + [fetch(four, dx, pair=dz) for dx, dz in LARGE[1:]]
     far = [fetch(piece, dcore=1) for piece in near]
     embed, tell, told = layer(lengths, positive, x, ln_gain, near + far, seq)
     chips = [[chip * 2 + core for chip in range(16)] for core in range(2)]

time: 90.9 us -> 90.1 us (level)
  no operation moved by 1% of the time
where the time goes in v5:
time: 90.1 us; the launch traced here: 90 us
  waiting for transfers between devices  28.2 us (31%)
  starting transfers between devices  24.9 us (28%)
  Pallas kernels  23.2 us (26%)
  blocking collectives  11.7 us (13%)
  other arithmetic  1.2 us (1%)
    ppermute x12, waiting for transfers between devices, fetch(): return lax.ppermute(value, 'dev', moves)  28.2 us
    ppermute x12, starting transfers between devices, fetch(): return lax.ppermute(value, 'dev', moves)  24.9 us
    pallas_call x1, Pallas kernels, layer(): pl.pallas_call(functools.partial(layer_kernel, rows, docs), out_shape=(ja...  21.2 us
    all_to_all x1, blocking collectives, local(): near = lax.all_to_all(tell, 'dev', 0, 0, axis_index_groups=chips)  11.7 us
    pallas_call x1, Pallas kernels, contrast(): pl.pallas_call(contrast_kernel, out_shape=(jax.ShapeDtypeStruct((mine, hi...  1.91 us
  transfers between devices with their start and end apart: 12, of which 8 were waited for; matrix products, arithmetic and copies ran while one was open for 0% of the time, Pallas kernels for 0%

profile of v5, /device:TPU:1, one launch (start us, length us, event | category | flops | bytes accessed | tf_op | source)
XLA Modules:
  0.0 90.0 jit_solution(17656191314590963186)
XLA Ops:
  0.6 0.0 copy-start.2
  0.6 0.0 copy-start.3
  0.7 0.0 copy-start.1
  0.7 0.0 copy-start
  0.7 1.1 %maximum_maximum_fusion.raw_ref = bf16[24,3840]{1,0:T(8,128)(2,1)S(1)} fusion(bf16[8,768]{1,0:T(8,128)(2,1)} %param.13, bf16[16,768]{1,0:T(8,128)(2,1)} %param.9, bf16[24,768]{1,0:T(8,128)(2,1)} %param.11, bf16[24,2304]{1,0:T(8,128)(2,1)} %param.10), kind=kLoop, calls=%fused_computation.1 | loop fusion | flops 737280 | bytes 368640 | tf_op jit(solution)/shard_map/concatenate | solution.py:360
  1.8 0.1 cut.1
  1.8 3.3 %collective-permute-start = (bf16[24,1920]{1,0:T(8,128)(2,1)S(1)}, bf16[24,1920]{1,0:T(8,128)(2,1)S(1)}, u32[]{:S(2)}, u32[]{:S(2)}) collective-permute-start(bf16[24,1920]{1,0:T(8,128)(2,1)S(1)} %get-tuple-element.13), channel_id=1, source_target_pairs={{1,0},{0,1},{3,2},{2,3},{5,4},{4,5},{7,6},{6,7},{9,8},{8,9},{11,10... | collective-permute-start | bytes 276488 | tf_op jit(solution)/shard_map/ppermute | solution.py:353
  5.1 0.9 %collective-permute-done.got_ref = bf16[24,1920]{1,0:T(8,128)(2,1)S(1)} collective-permute-done((bf16[24,1920]{1,0:T(8,128)(2,1)S(1)}, bf16[24,1920]{1,0:T(8,128)(2,1)S(1)}, u32[]{:S(2)}, u32[]{:S(2)}) %collective-permute-start) | collective-permute-done | bytes 92192 | tf_op jit(solution)/shard_map/ppermute | solution.py:353
  6.1 2.4 %collective-permute-start.3 = (bf16[48,1920]{1,0:T(8,128)(2,1)S(1)}, bf16[48,1920]{1,0:T(8,128)(2,1)S(1)}, u32[]{:S(2)}, u32[]{:S(2)}) collective-permute-start(bf16[48,1920]{1,0:T(8,128)(2,1)S(1)} %chip.1), channel_id=1, source_target_pairs={{22,0},{23,1},{16,2},{17,3},{18,4},{19,5},{20,6},{21,7},{30,8},{31... | collective-permute-start | bytes 552968 | tf_op jit(solution)/shard_map/ppermute | solution.py:353
  8.6 3.0 %collective-permute-start.2 = (bf16[48,1920]{1,0:T(8,128)(2,1)S(1)}, bf16[48,1920]{1,0:T(8,128)(2,1)S(1)}, u32[]{:S(2)}, u32[]{:S(2)}) collective-permute-start(bf16[48,1920]{1,0:T(8,128)(2,1)S(1)} %chip.1), channel_id=1, source_target_pairs={{4,0},{5,1},{6,2},{7,3},{0,4},{1,5},{2,6},{3,7},{12,8},{13,9},{14,... | collective-permute-start | bytes 552968 | tf_op jit(solution)/shard_map/ppermute | solution.py:353
  11.6 0.7 collective-permute-start.1
  12.2 4.1 %collective-permute-done.3 = bf16[48,1920]{1,0:T(8,128)(2,1)S(1)} collective-permute-done((bf16[48,1920]{1,0:T(8,128)(2,1)S(1)}, bf16[48,1920]{1,0:T(8,128)(2,1)S(1)}, u32[]{:S(2)}, u32[]{:S(2)}) %collective-permute-start.3) | collective-permute-done | bytes 184352 | tf_op jit(solution)/shard_map/ppermute | solution.py:353
  16.3 6.9 %collective-permute-done.2 = bf16[48,1920]{1,0:T(8,128)(2,1)S(1)} collective-permute-done((bf16[48,1920]{1,0:T(8,128)(2,1)S(1)}, bf16[48,1920]{1,0:T(8,128)(2,1)S(1)}, u32[]{:S(2)}, u32[]{:S(2)}) %collective-permute-start.2) | collective-permute-done | bytes 184352 | tf_op jit(solution)/shard_map/ppermute | solution.py:353
  23.2 0.0 collective-permute-done.1
  23.2 0.1 pad_maximum_fusion.refs_0_
  23.3 5.3 %collective-permute-start.6 = (bf16[4,48,1920]{2,1,0:T(8,128)(2,1)S(1)}, bf16[4,48,1920]{2,1,0:T(8,128)(2,1)S(1)}, u32[]{:S(2)}, u32[]{:S(2)}) collective-permute-start(bf16[4,48,1920]{2,1,0:T(8,128)(2,1)S(1)} %pad_maximum_fusion.refs_0_), channel_id=1, source_target_pairs={{2,0},{3,1},{0,2},{1,3},{6,4},{7,5},{4,6},{5,7},{10,8},{11,9},{8,1... | collective-permute-start | bytes 2211848 | tf_op jit(solution)/shard_map/ppermute | solution.py:353
  28.6 0.5 collective-permute-start.5
  29.1 2.2 %collective-permute-start.4 = (bf16[4,48,1920]{2,1,0:T(8,128)(2,1)S(1)}, bf16[4,48,1920]{2,1,0:T(8,128)(2,1)S(1)}, u32[]{:S(2)}, u32[]{:S(2)}) collective-permute-start(bf16[4,48,1920]{2,1,0:T(8,128)(2,1)S(1)} %pad_maximum_fusion.refs_0_), channel_id=1, source_target_pairs={{8,0},{9,1},{10,2},{11,3},{12,4},{13,5},{14,6},{15,7},{16,8},{17,9... | collective-permute-start | bytes 2211848 | tf_op jit(solution)/shard_map/ppermute | solution.py:353
  31.3 1.7 %collective-permute-start.7 = (bf16[4,48,1920]{2,1,0:T(8,128)(2,1)S(1)}, bf16[4,48,1920]{2,1,0:T(8,128)(2,1)S(1)}, u32[]{:S(2)}, u32[]{:S(2)}) collective-permute-start(bf16[4,48,1920]{2,1,0:T(8,128)(2,1)S(1)} %pad_maximum_fusion.refs_0_), channel_id=1, source_target_pairs={{1,0},{0,1},{3,2},{2,3},{5,4},{4,5},{7,6},{6,7},{9,8},{8,9},{11,10... | collective-permute-start | bytes 2211848 | tf_op jit(solution)/shard_map/ppermute | solution.py:353
  33.0 11.7 %collective-permute-done.6.refs_3_ = bf16[4,48,1920]{2,1,0:T(8,128)(2,1)S(1)} collective-permute-done((bf16[4,48,1920]{2,1,0:T(8,128)(2,1)S(1)}, bf16[4,48,1920]{2,1,0:T(8,128)(2,1)S(1)}, u32[]{:S(2)}, u32[]{:S(2)}) %collective-permute-start.6) | collective-permute-done | bytes 737312 | tf_op jit(solution)/shard_map/ppermute | solution.py:353
  44.7 1.4 %collective-permute-start.10 = (bf16[4,48,1920]{2,1,0:T(8,128)(2,1)S(1)}, bf16[4,48,1920]{2,1,0:T(8,128)(2,1)S(1)}, u32[]{:S(2)}, u32[]{:S(2)}) collective-permute-start(bf16[4,48,1920]{2,1,0:T(8,128)(2,1)S(1)} %collective-permute-done.6.refs_3_), channel_id=1, source_target_pairs={{1,0},{0,1},{3,2},{2,3},{5,4},{4,5},{7,6},{6,7},{9,8},{8,9},{11,10... | collective-permute-start | bytes 2211848 | tf_op jit(solution)/shard_map/ppermute | solution.py:353
  46.1 0.6 collective-permute-done.5.refs_2_
  46.7 2.0 %collective-permute-start.9 = (bf16[4,48,1920]{2,1,0:T(8,128)(2,1)S(1)}, bf16[4,48,1920]{2,1,0:T(8,128)(2,1)S(1)}, u32[]{:S(2)}, u32[]{:S(2)}) collective-permute-start(bf16[4,48,1920]{2,1,0:T(8,128)(2,1)S(1)} %collective-permute-done.5.refs_2_), channel_id=1, source_target_pairs={{1,0},{0,1},{3,2},{2,3},{5,4},{4,5},{7,6},{6,7},{9,8},{8,9},{11,10... | collective-permute-start | bytes 2211848 | tf_op jit(solution)/shard_map/ppermute | solution.py:353
  48.8 0.0 collective-permute-done.4.refs_1_
  48.8 0.0 collective-permute-start.8
  48.8 0.0 collective-permute-done.7.refs_4_
  48.8 0.0 collective-permute-done.10.refs_7_
  48.8 1.8 %collective-permute-done.9.refs_6_ = bf16[4,48,1920]{2,1,0:T(8,128)(2,1)S(1)} collective-permute-done((bf16[4,48,1920]{2,1,0:T(8,128)(2,1)S(1)}, bf16[4,48,1920]{2,1,0:T(8,128)(2,1)S(1)}, u32[]{:S(2)}, u32[]{:S(2)}) %collective-permute-start.9) | collective-permute-done | bytes 737312 | tf_op jit(solution)/shard_map/ppermute | solution.py:353
  50.6 1.1 %collective-permute-done.8.refs_5_ = bf16[4,48,1920]{2,1,0:T(8,128)(2,1)S(1)} collective-permute-done((bf16[4,48,1920]{2,1,0:T(8,128)(2,1)S(1)}, bf16[4,48,1920]{2,1,0:T(8,128)(2,1)S(1)}, u32[]{:S(2)}, u32[]{:S(2)}) %collective-permute-start.8) | collective-permute-done | bytes 737312 | tf_op jit(solution)/shard_map/ppermute | solution.py:353
  51.6 0.0 copy-done.2
  51.6 0.0 copy-done.3
  51.7 0.0 copy-done.1
  51.7 0.0 copy-done
  51.7 21.2 %layer.1 = (bf16[8,768]{1,0:T(8,128)(2,1)}, bf16[16,8,896]{2,1,0:T(8,128)(2,1)S(1)}, bf16[256,768]{1,0:T(8,128)(2,1)S(1)}) custom-call(s32[8]{0:T(128)S(1)} %copy-done.2, s32[8]{0:T(128)S(1)} %copy-done.3, bf16[1024,768]{1,0:T(8,128)(2,1)S(1)} %bitcast.6, f32[768]{0:T(1024)S(1)} %copy-done.1, bf16[4,48,1920]{2,1,0:T(8,128)(2,1)S(1)} %pad_maximum_fusion.refs_0_, ...), custom_call_target="tpu_custom_call" | custom-call | tf_op jit(solution)/shard_map/layer/pallas_call | solution.py:245
  72.9 11.7 %all_to_all.5.near_ref = bf16[16,8,896]{2,1,0:T(8,128)(2,1)S(1)} all-to-all(bf16[16,8,896]{2,1,0:T(8,128)(2,1)S(1)} %get-tuple-element.16), channel_id=1, replica_groups={{0,2,4,6,8,10,12,14,16,18,20,22,24,26,28,30},{1,3,5,7,9,11,13,15,17,19,..., dimensions={0} | all-to-all | bytes 458752 | tf_op jit(solution)/shard_map/all_to_all | solution.py:367
  84.6 2.3 %collective-permute-start.11 = (bf16[16,8,896]{2,1,0:T(8,128)(2,1)S(1)}, bf16[16,8,896]{2,1,0:T(8,128)(2,1)S(1)}, u32[]{:S(2)}, u32[]{:S(2)}) collective-permute-start(bf16[16,8,896]{2,1,0:T(8,128)(2,1)S(1)} %all_to_all.5.near_ref), channel_id=1, source_target_pairs={{1,0},{0,1},{3,2},{2,3},{5,4},{4,5},{7,6},{6,7},{9,8},{8,9},{11,10... | collective-permute-start | bytes 688136 | tf_op jit(solution)/shard_map/ppermute | solution.py:353
  86.9 1.1 %collective-permute-done.11.far_ref = bf16[16,8,896]{2,1,0:T(8,128)(2,1)S(1)} collective-permute-done((bf16[16,8,896]{2,1,0:T(8,128)(2,1)S(1)}, bf16[16,8,896]{2,1,0:T(8,128)(2,1)S(1)}, u32[]{:S(2)}, u32[]{:S(2)}) %collective-permute-start.11) | collective-permute-done | bytes 229408 | tf_op jit(solution)/shard_map/ppermute | solution.py:353
  88.1 1.9 %contrast.1 = (f32[8,768]{1,0:T(8,128)}, f32[8,768]{1,0:T(8,128)}, f32[1,8]{1,0:T(1,128)}) custom-call(bf16[256,768]{1,0:T(8,128)(2,1)S(1)} %get-tuple-element.15.told_ref, bf16[16,8,896]{2,1,0:T(8,128)(2,1)S(1)} %all_to_all.5.near_ref, bf16[16,8,896]{2,1,0:T(8,128)(2,1)S(1)} %collective-permute-done.11.far_ref), custom_call_target="tpu_custom_call" | custom-call | tf_op jit(solution)/shard_map/contrast/pallas_call | solution.py:327
  (1 shorter events, 0.0 us)
Async XLA Ops:
  0.6 51.0 %copy-start.2 = (s32[8]{0:T(128)S(1)}, s32[8]{0:T(128)}, u32[]{:S(2)}) copy-start(s32[8]{0:T(128)} %len_ref.1) | copy-start | bytes 100
  0.6 51.0 %copy-start.3 = (s32[8]{0:T(128)S(1)}, s32[8]{0:T(128)}, u32[]{:S(2)}) copy-start(s32[8]{0:T(128)} %positive_ref.1) | copy-start | bytes 100
  0.7 51.0 %copy-start.1 = (f32[768]{0:T(1024)S(1)}, f32[768]{0:T(1024)}, u32[]{:S(2)}) copy-start(f32[768]{0:T(1024)} %gain_ref.1) | copy-start | bytes 9220
  0.7 51.0 %copy-start = (bf16[8,128,768]{2,1,0:T(8,128)(2,1)S(1)}, bf16[8,128,768]{2,1,0:T(8,128)(2,1)}, u32[]{:S(2)}) copy-start(bf16[8,128,768]{2,1,0:T(8,128)(2,1)} %param.8) | copy-start | bytes 4718596
  1.8 4.3 %collective-permute-start = (bf16[24,1920]{1,0:T(8,128)(2,1)S(1)}, bf16[24,1920]{1,0:T(8,128)(2,1)S(1)}, u32[]{:S(2)}, u32[]{:S(2)}) collective-permute-start(bf16[24,1920]{1,0:T(8,128)(2,1)S(1)} %get-tuple-element.13), channel_id=1, source_target_pairs={{1,0},{0,1},{3,2},{2,3},{5,4},{4,5},{7,6},{6,7},{9,8},{8,9},{11,10... | collective-permute-start | bytes 276488 | tf_op jit(solution)/shard_map/ppermute | solution.py:353
  6.1 10.2 %collective-permute-start.3 = (bf16[48,1920]{1,0:T(8,128)(2,1)S(1)}, bf16[48,1920]{1,0:T(8,128)(2,1)S(1)}, u32[]{:S(2)}, u32[]{:S(2)}) collective-permute-start(bf16[48,1920]{1,0:T(8,128)(2,1)S(1)} %chip.1), channel_id=1, source_target_pairs={{22,0},{23,1},{16,2},{17,3},{18,4},{19,5},{20,6},{21,7},{30,8},{31... | collective-permute-start | bytes 552968 | tf_op jit(solution)/shard_map/ppermute | solution.py:353
  8.6 14.6 %collective-permute-start.2 = (bf16[48,1920]{1,0:T(8,128)(2,1)S(1)}, bf16[48,1920]{1,0:T(8,128)(2,1)S(1)}, u32[]{:S(2)}, u32[]{:S(2)}) collective-permute-start(bf16[48,1920]{1,0:T(8,128)(2,1)S(1)} %chip.1), channel_id=1, source_target_pairs={{4,0},{5,1},{6,2},{7,3},{0,4},{1,5},{2,6},{3,7},{12,8},{13,9},{14,... | collective-permute-start | bytes 552968 | tf_op jit(solution)/shard_map/ppermute | solution.py:353
  11.6 11.7 %collective-permute-start.1 = (bf16[48,1920]{1,0:T(8,128)(2,1)S(1)}, bf16[48,1920]{1,0:T(8,128)(2,1)S(1)}, u32[]{:S(2)}, u32[]{:S(2)}) collective-permute-start(bf16[48,1920]{1,0:T(8,128)(2,1)S(1)} %chip.1), channel_id=1, source_target_pairs={{18,0},{19,1},{20,2},{21,3},{22,4},{23,5},{16,6},{17,7},{26,8},{27... | collective-permute-start | bytes 552968 | tf_op jit(solution)/shard_map/ppermute | solution.py:353
  23.3 21.3 %collective-permute-start.6 = (bf16[4,48,1920]{2,1,0:T(8,128)(2,1)S(1)}, bf16[4,48,1920]{2,1,0:T(8,128)(2,1)S(1)}, u32[]{:S(2)}, u32[]{:S(2)}) collective-permute-start(bf16[4,48,1920]{2,1,0:T(8,128)(2,1)S(1)} %pad_maximum_fusion.refs_0_), channel_id=1, source_target_pairs={{2,0},{3,1},{0,2},{1,3},{6,4},{7,5},{4,6},{5,7},{10,8},{11,9},{8,1... | collective-permute-start | bytes 2211848 | tf_op jit(solution)/shard_map/ppermute | solution.py:353
  28.6 18.1 %collective-permute-start.5 = (bf16[4,48,1920]{2,1,0:T(8,128)(2,1)S(1)}, bf16[4,48,1920]{2,1,0:T(8,128)(2,1)S(1)}, u32[]{:S(2)}, u32[]{:S(2)}) collective-permute-start(bf16[4,48,1920]{2,1,0:T(8,128)(2,1)S(1)} %pad_maximum_fusion.refs_0_), channel_id=1, source_target_pairs={{24,0},{25,1},{26,2},{27,3},{28,4},{29,5},{30,6},{31,7},{0,8},{1,9... | collective-permute-start | bytes 2211848 | tf_op jit(solution)/shard_map/ppermute | solution.py:353
  29.1 19.7 %collective-permute-start.4 = (bf16[4,48,1920]{2,1,0:T(8,128)(2,1)S(1)}, bf16[4,48,1920]{2,1,0:T(8,128)(2,1)S(1)}, u32[]{:S(2)}, u32[]{:S(2)}) collective-permute-start(bf16[4,48,1920]{2,1,0:T(8,128)(2,1)S(1)} %pad_maximum_fusion.refs_0_), channel_id=1, source_target_pairs={{8,0},{9,1},{10,2},{11,3},{12,4},{13,5},{14,6},{15,7},{16,8},{17,9... | collective-permute-start | bytes 2211848 | tf_op jit(solution)/shard_map/ppermute | solution.py:353
  31.3 17.4 %collective-permute-start.7 = (bf16[4,48,1920]{2,1,0:T(8,128)(2,1)S(1)}, bf16[4,48,1920]{2,1,0:T(8,128)(2,1)S(1)}, u32[]{:S(2)}, u32[]{:S(2)}) collective-permute-start(bf16[4,48,1920]{2,1,0:T(8,128)(2,1)S(1)} %pad_maximum_fusion.refs_0_), channel_id=1, source_target_pairs={{1,0},{0,1},{3,2},{2,3},{5,4},{4,5},{7,6},{6,7},{9,8},{8,9},{11,10... | collective-permute-start | bytes 2211848 | tf_op jit(solution)/shard_map/ppermute | solution.py:353
  44.7 4.1 %collective-permute-start.10 = (bf16[4,48,1920]{2,1,0:T(8,128)(2,1)S(1)}, bf16[4,48,1920]{2,1,0:T(8,128)(2,1)S(1)}, u32[]{:S(2)}, u32[]{:S(2)}) collective-permute-start(bf16[4,48,1920]{2,1,0:T(8,128)(2,1)S(1)} %collective-permute-done.6.refs_3_), channel_id=1, source_target_pairs={{1,0},{0,1},{3,2},{2,3},{5,4},{4,5},{7,6},{6,7},{9,8},{8,9},{11,10... | collective-permute-start | bytes 2211848 | tf_op jit(solution)/shard_map/ppermute | solution.py:353
  46.7 3.9 %collective-permute-start.9 = (bf16[4,48,1920]{2,1,0:T(8,128)(2,1)S(1)}, bf16[4,48,1920]{2,1,0:T(8,128)(2,1)S(1)}, u32[]{:S(2)}, u32[]{:S(2)}) collective-permute-start(bf16[4,48,1920]{2,1,0:T(8,128)(2,1)S(1)} %collective-permute-done.5.refs_2_), channel_id=1, source_target_pairs={{1,0},{0,1},{3,2},{2,3},{5,4},{4,5},{7,6},{6,7},{9,8},{8,9},{11,10... | collective-permute-start | bytes 2211848 | tf_op jit(solution)/shard_map/ppermute | solution.py:353
  48.8 2.9 %collective-permute-start.8 = (bf16[4,48,1920]{2,1,0:T(8,128)(2,1)S(1)}, bf16[4,48,1920]{2,1,0:T(8,128)(2,1)S(1)}, u32[]{:S(2)}, u32[]{:S(2)}) collective-permute-start(bf16[4,48,1920]{2,1,0:T(8,128)(2,1)S(1)} %collective-permute-done.4.refs_1_), channel_id=1, source_target_pairs={{1,0},{0,1},{3,2},{2,3},{5,4},{4,5},{7,6},{6,7},{9,8},{8,9},{11,10... | collective-permute-start | bytes 2211848 | tf_op jit(solution)/shard_map/ppermute | solution.py:353
  84.6 3.4 %collective-permute-start.11 = (bf16[16,8,896]{2,1,0:T(8,128)(2,1)S(1)}, bf16[16,8,896]{2,1,0:T(8,128)(2,1)S(1)}, u32[]{:S(2)}, u32[]{:S(2)}) collective-permute-start(bf16[16,8,896]{2,1,0:T(8,128)(2,1)S(1)} %all_to_all.5.near_ref), channel_id=1, source_target_pairs={{1,0},{0,1},{3,2},{2,3},{5,4},{4,5},{7,6},{6,7},{9,8},{8,9},{11,10... | collective-permute-start | bytes 688136 | tf_op jit(solution)/shard_map/ppermute | solution.py:353

commit v6 on v5

--- a/solution.py
+++ b/solution.py
@@ -88,7 +88,7 @@
 
 
 def layer_kernel(rows, unroll, len_ref, positive_ref, x_ref, gain_ref, *refs):
-    pieces, refs = refs[:8], refs[8:]
+    pieces, rests, refs = refs[:8], refs[8:16], refs[16:]
     o_ref, tell_ref, told_ref, w_s, wo_s, ctx_s, query_s, told_s, q_s, k_s, v_s, kc_s, vc_s, attn_s, bias_s, sems = refs
     tokens, hidden = x_ref.shape
     docs = o_ref.shape[0]
@@ -101,7 +101,7 @@
     weights, others, last, asked = ([], []), [], [], []
     for side in range(2):
         for p, (ax, az) in enumerate(LARGE):
-            piece = pieces[side * 4 + p]
+            piece, rest = pieces[side * 4 + p], rests[side * 4 + p]
             n = side * 4 + p
             for k, (bx, bz) in enumerate(SMALL):
                 chip = ((x + ax + bx) & 3) * 4 + (((z ^ az) + bz) & 3)
@@ -115,17 +115,17 @@
                 )
                 last.append(
                     pltpu.make_async_copy(
-                        piece.at[k, :, pl.ds(WEIGHTS, HALF)], wo_s.at[pl.ds(at, 48), lanes], sems.at[1, n * 4 + k]
+                        rest.at[k, :, pl.ds(0, HALF)], wo_s.at[pl.ds(at, 48), lanes], sems.at[1, n * 4 + k]
                     )
                 )
                 asked.append(
                     pltpu.make_async_copy(
-                        piece.at[k, pl.ds(32, 16), pl.ds(PROJECT, HALF)], query_s.at[side, chip], sems.at[2, n * 4 + k]
+                        rest.at[k, pl.ds(32, 16), pl.ds(HALF, HALF)], query_s.at[side, chip], sems.at[2, n * 4 + k]
                     )
                 )
             others.append(
                 pltpu.make_async_copy(
-                    piece.at[:, pl.ds(0, 32), pl.ds(PROJECT, HALF)], ctx_s.at[side, pl.ds(4 * p, 4)], sems.at[3, n]
+                    rest.at[:, pl.ds(0, 32), pl.ds(HALF, HALF)], ctx_s.at[side, pl.ds(4 * p, 4)], sems.at[3, n]
                 )
             )
     for copy in weights[0] + others + weights[1] + asked:
@@ -249,7 +249,7 @@
             jax.ShapeDtypeStruct((chips, docs, hidden + 128), BF16),
             jax.ShapeDtypeStruct((chips * 16, hidden), BF16),
         ),
-        in_specs=[vmem, vmem, vmem, vmem] + [hbm] * 8,
+        in_specs=[vmem, vmem, vmem, vmem] + [hbm] * 16,
         out_specs=(vmem, vmem, hbm),
         scratch_shapes=[
             pltpu.VMEM((2, hidden, WEIGHTS), BF16),
@@ -360,9 +360,11 @@
     keep, give = cut(jnp.concatenate([w_qkv, w_out, rows], axis=1))
     block = chip(keep, fetch(give, dcore=1))
     four = jnp.stack([block] + [fetch(block, dx, dz) for dx, dz in SMALL[1:]])
-    near = [four] + [fetch(four, dx, pair=dz) for dx, dz in LARGE[1:]]
-    far = [fetch(piece, dcore=1) for piece in near]
-    embed, tell, told = layer(lengths, positive, x, ln_gain, near + far, seq)
+    gathered = []
+    for part in (four[:, :, :WEIGHTS], four[:, :, WEIGHTS:]):
+        near = [part] + [fetch(part, dx, pair=dz) for dx, dz in LARGE[1:]]
+        gathered += near + [fetch(piece, dcore=1) for piece in near]
+    embed, tell, told = layer(lengths, positive, x, ln_gain, gathered, seq)
     chips = [[chip * 2 + core for chip in range(16)] for core in range(2)]
     near = lax.all_to_all(tell, "dev", 0, 0, axis_index_groups=chips)
     far = fetch(near, dcore=1)

time: 90.1 us -> 96.2 us (1.068)
  Pallas kernels: 23.2 us -> 27.7 us
  starting transfers between devices: 24.9 us -> 26.5 us
  blocking collectives: 11.7 us -> 12.7 us
    pallas_call x1, Pallas kernels: 21.2 us -> 25.7 us  [layer(): pl.pallas_call(functools.partial(layer_kernel, rows, docs), out_shape=(ja...]
    ppermute x12 -> x19, starting transfers between devices: 24.9 us -> 26.5 us  [fetch(): return lax.ppermute(value, 'dev', moves)]
    all_to_all x1, blocking collectives: 11.7 us -> 12.7 us  [local(): near = lax.all_to_all(tell, 'dev', 0, 0, axis_index_groups=chips)]
    ppermute x12 -> x19, waiting for transfers between devices: 28.2 us -> 27.3 us  [fetch(): return lax.ppermute(value, 'dev', moves)]
  transfers between devices with their start and end apart: 12 -> 19, of which waited for: 8 -> 10; matrix products, arithmetic and copies ran while one was open for 0% -> 0% of each run, Pallas kernels for 0% -> 0%
where the time goes in v6:
time: 96.2 us; the launch traced here: 96 us
  Pallas kernels  27.7 us (29%)
  waiting for transfers between devices  27.3 us (28%)
  starting transfers between devices  26.5 us (28%)
  blocking collectives  12.7 us (13%)
  other arithmetic  1.11 us (1%)
    ppermute x19, waiting for transfers between devices, fetch(): return lax.ppermute(value, 'dev', moves)  27.3 us
    ppermute x19, starting transfers between devices, fetch(): return lax.ppermute(value, 'dev', moves)  26.5 us
    pallas_call x1, Pallas kernels, layer(): pl.pallas_call(functools.partial(layer_kernel, rows, docs), out_shape=(ja...  25.7 us
    all_to_all x1, blocking collectives, local(): near = lax.all_to_all(tell, 'dev', 0, 0, axis_index_groups=chips)  12.7 us
  transfers between devices with their start and end apart: 19, of which 10 were waited for; matrix products, arithmetic and copies ran while one was open for 0% of the time, Pallas kernels for 0%

profile of v6, /device:TPU:1, one launch (start us, length us, event | category | flops | bytes accessed | tf_op | source)
XLA Modules:
  0.0 96.0 jit_solution(14622602459022929791)
XLA Ops:
  0.6 1.0 %maximum_maximum_fusion.raw_ref = bf16[24,3840]{1,0:T(8,128)(2,1)S(1)} fusion(bf16[8,768]{1,0:T(8,128)(2,1)} %param.13, bf16[16,768]{1,0:T(8,128)(2,1)} %param.9, bf16[24,768]{1,0:T(8,128)(2,1)} %param.11, bf16[24,2304]{1,0:T(8,128)(2,1)} %param.10), kind=kLoop, calls=%fused_computation.2 | loop fusion | flops 737280 | bytes 368640 | tf_op jit(solution)/shard_map/concatenate | solution.py:360
  1.6 0.1 cut.1
  1.7 3.3 %collective-permute-start = (bf16[24,1920]{1,0:T(8,128)(2,1)S(1)}, bf16[24,1920]{1,0:T(8,128)(2,1)S(1)}, u32[]{:S(2)}, u32[]{:S(2)}) collective-permute-start(bf16[24,1920]{1,0:T(8,128)(2,1)S(1)} %get-tuple-element.13), channel_id=1, source_target_pairs={{1,0},{0,1},{3,2},{2,3},{5,4},{4,5},{7,6},{6,7},{9,8},{8,9},{11,10... | collective-permute-start | bytes 276488 | tf_op jit(solution)/shard_map/ppermute | solution.py:353
  5.0 0.9 collective-permute-done.got_ref
  6.0 2.4 %collective-permute-start.3 = (bf16[48,1920]{1,0:T(8,128)(2,1)S(1)}, bf16[48,1920]{1,0:T(8,128)(2,1)S(1)}, u32[]{:S(2)}, u32[]{:S(2)}) collective-permute-start(bf16[48,1920]{1,0:T(8,128)(2,1)S(1)} %chip.1), channel_id=1, source_target_pairs={{22,0},{23,1},{16,2},{17,3},{18,4},{19,5},{20,6},{21,7},{30,8},{31... | collective-permute-start | bytes 552968 | tf_op jit(solution)/shard_map/ppermute | solution.py:353
  8.4 3.0 %collective-permute-start.2 = (bf16[48,1920]{1,0:T(8,128)(2,1)S(1)}, bf16[48,1920]{1,0:T(8,128)(2,1)S(1)}, u32[]{:S(2)}, u32[]{:S(2)}) collective-permute-start(bf16[48,1920]{1,0:T(8,128)(2,1)S(1)} %chip.1), channel_id=1, source_target_pairs={{4,0},{5,1},{6,2},{7,3},{0,4},{1,5},{2,6},{3,7},{12,8},{13,9},{14,... | collective-permute-start | bytes 552968 | tf_op jit(solution)/shard_map/ppermute | solution.py:353
  11.4 0.7 collective-permute-start.1
  12.1 4.1 %collective-permute-done.3 = bf16[48,1920]{1,0:T(8,128)(2,1)S(1)} collective-permute-done((bf16[48,1920]{1,0:T(8,128)(2,1)S(1)}, bf16[48,1920]{1,0:T(8,128)(2,1)S(1)}, u32[]{:S(2)}, u32[]{:S(2)}) %collective-permute-start.3) | collective-permute-done | bytes 184352 | tf_op jit(solution)/shard_map/ppermute | solution.py:353
  16.2 6.9 %collective-permute-done.2 = bf16[48,1920]{1,0:T(8,128)(2,1)S(1)} collective-permute-done((bf16[48,1920]{1,0:T(8,128)(2,1)S(1)}, bf16[48,1920]{1,0:T(8,128)(2,1)S(1)}, u32[]{:S(2)}, u32[]{:S(2)}) %collective-permute-start.2) | collective-permute-done | bytes 184352 | tf_op jit(solution)/shard_map/ppermute | solution.py:353
  23.1 0.0 collective-permute-done.1
  23.1 0.0 copy-start.3
  23.1 1.6 %collective-permute-start.14 = (bf16[4,48,768]{2,1,0:T(8,128)(2,1)S(1)}, bf16[4,48,768]{2,1,0:T(8,128)(2,1)S(1)}, u32[]{:S(2)}, u32[]{:S(2)}) collective-permute-start(bf16[4,48,768]{2,1,0:T(8,128)(2,1)S(1)} %pad_maximum_fusion.1.refs_8_), channel_id=1, source_target_pairs={{1,0},{0,1},{3,2},{2,3},{5,4},{4,5},{7,6},{6,7},{9,8},{8,9},{11,10... | collective-permute-start | bytes 884744 | tf_op jit(solution)/shard_map/ppermute | solution.py:353
  24.8 4.5 %collective-permute-start.13 = (bf16[4,48,768]{2,1,0:T(8,128)(2,1)S(1)}, bf16[4,48,768]{2,1,0:T(8,128)(2,1)S(1)}, u32[]{:S(2)}, u32[]{:S(2)}) collective-permute-start(bf16[4,48,768]{2,1,0:T(8,128)(2,1)S(1)} %pad_maximum_fusion.1.refs_8_), channel_id=1, source_target_pairs={{2,0},{3,1},{0,2},{1,3},{6,4},{7,5},{4,6},{5,7},{10,8},{11,9},{8,1... | collective-permute-start | bytes 884744 | tf_op jit(solution)/shard_map/ppermute | solution.py:353
  29.3 0.1 collective-permute-start.12
  29.4 2.6 %collective-permute-start.11 = (bf16[4,48,768]{2,1,0:T(8,128)(2,1)S(1)}, bf16[4,48,768]{2,1,0:T(8,128)(2,1)S(1)}, u32[]{:S(2)}, u32[]{:S(2)}) collective-permute-start(bf16[4,48,768]{2,1,0:T(8,128)(2,1)S(1)} %pad_maximum_fusion.1.refs_8_), channel_id=1, source_target_pairs={{8,0},{9,1},{10,2},{11,3},{12,4},{13,5},{14,6},{15,7},{16,8},{17,9... | collective-permute-start | bytes 884744 | tf_op jit(solution)/shard_map/ppermute | solution.py:353
  31.9 0.1 pad_maximum_fusion
  32.1 0.1 collective-permute-start.6
  32.2 0.0 collective-permute-done.14.refs_12_
  32.2 0.1 collective-permute-start.5
  32.3 4.2 %collective-permute-done.13.refs_11_ = bf16[4,48,768]{2,1,0:T(8,128)(2,1)S(1)} collective-permute-done((bf16[4,48,768]{2,1,0:T(8,128)(2,1)S(1)}, bf16[4,48,768]{2,1,0:T(8,128)(2,1)S(1)}, u32[]{:S(2)}, u32[]{:S(2)}) %collective-permute-start.13) | collective-permute-done | bytes 294944 | tf_op jit(solution)/shard_map/ppermute | solution.py:353
  36.5 1.1 %collective-permute-start.4 = (bf16[4,48,1152]{2,1,0:T(8,128)(2,1)S(1)}, bf16[4,48,1152]{2,1,0:T(8,128)(2,1)S(1)}, u32[]{:S(2)}, u32[]{:S(2)}) collective-permute-start(bf16[4,48,1152]{2,1,0:T(8,128)(2,1)S(1)} %slice.8.refs_0_), channel_id=1, source_target_pairs={{8,0},{9,1},{10,2},{11,3},{12,4},{13,5},{14,6},{15,7},{16,8},{17,9... | collective-permute-start | bytes 1327112 | tf_op jit(solution)/shard_map/ppermute | solution.py:353
  37.6 1.1 %collective-permute-done.12.refs_10_ = bf16[4,48,768]{2,1,0:T(8,128)(2,1)S(1)} collective-permute-done((bf16[4,48,768]{2,1,0:T(8,128)(2,1)S(1)}, bf16[4,48,768]{2,1,0:T(8,128)(2,1)S(1)}, u32[]{:S(2)}, u32[]{:S(2)}) %collective-permute-start.12) | collective-permute-done | bytes 294944 | tf_op jit(solution)/shard_map/ppermute | solution.py:353
  38.7 2.0 %collective-permute-start.7 = (bf16[4,48,1152]{2,1,0:T(8,128)(2,1)S(1)}, bf16[4,48,1152]{2,1,0:T(8,128)(2,1)S(1)}, u32[]{:S(2)}, u32[]{:S(2)}) collective-permute-start(bf16[4,48,1152]{2,1,0:T(8,128)(2,1)S(1)} %slice.8.refs_0_), channel_id=1, source_target_pairs={{1,0},{0,1},{3,2},{2,3},{5,4},{4,5},{7,6},{6,7},{9,8},{8,9},{11,10... | collective-permute-start | bytes 1327112 | tf_op jit(solution)/shard_map/ppermute | solution.py:353
  40.7 0.0 collective-permute-done.11.refs_9_
  40.7 0.0 collective-permute-start.17
  40.7 5.3 %collective-permute-done.6.refs_3_ = bf16[4,48,1152]{2,1,0:T(8,128)(2,1)S(1)} collective-permute-done((bf16[4,48,1152]{2,1,0:T(8,128)(2,1)S(1)}, bf16[4,48,1152]{2,1,0:T(8,128)(2,1)S(1)}, u32[]{:S(2)}, u32[]{:S(2)}) %collective-permute-start.6) | collective-permute-done | bytes 442400 | tf_op jit(solution)/shard_map/ppermute | solution.py:353
  46.0 0.7 collective-permute-start.10
  46.7 1.5 %collective-permute-done.5.refs_2_ = bf16[4,48,1152]{2,1,0:T(8,128)(2,1)S(1)} collective-permute-done((bf16[4,48,1152]{2,1,0:T(8,128)(2,1)S(1)}, bf16[4,48,1152]{2,1,0:T(8,128)(2,1)S(1)}, u32[]{:S(2)}, u32[]{:S(2)}) %collective-permute-start.5) | collective-permute-done | bytes 442400 | tf_op jit(solution)/shard_map/ppermute | solution.py:353
  48.2 1.2 %collective-permute-start.9 = (bf16[4,48,1152]{2,1,0:T(8,128)(2,1)S(1)}, bf16[4,48,1152]{2,1,0:T(8,128)(2,1)S(1)}, u32[]{:S(2)}, u32[]{:S(2)}) collective-permute-start(bf16[4,48,1152]{2,1,0:T(8,128)(2,1)S(1)} %collective-permute-done.5.refs_2_), channel_id=1, source_target_pairs={{1,0},{0,1},{3,2},{2,3},{5,4},{4,5},{7,6},{6,7},{9,8},{8,9},{11,10... | collective-permute-start | bytes 1327112 | tf_op jit(solution)/shard_map/ppermute | solution.py:353
  49.4 0.0 collective-permute-done.4.refs_1_
  49.4 0.0 collective-permute-start.8
  49.4 0.0 collective-permute-done.7.refs_4_
  49.4 0.5 collective-permute-start.16
  49.9 0.0 collective-permute-done.17.refs_15_
  49.9 0.3 collective-permute-start.15
  50.2 1.7 %collective-permute-done.16.refs_14_ = bf16[4,48,768]{2,1,0:T(8,128)(2,1)S(1)} collective-permute-done((bf16[4,48,768]{2,1,0:T(8,128)(2,1)S(1)}, bf16[4,48,768]{2,1,0:T(8,128)(2,1)S(1)}, u32[]{:S(2)}, u32[]{:S(2)}) %collective-permute-start.16) | collective-permute-done | bytes 294944 | tf_op jit(solution)/shard_map/ppermute | solution.py:353
  51.9 0.4 collective-permute-done.15.refs_13_
  52.3 0.0 collective-permute-done.10.refs_7_
  52.3 0.0 collective-permute-done.9.refs_6_
  52.3 0.0 collective-permute-done.8.refs_5_
  52.3 0.0 copy-done
  52.3 0.0 copy-done.1
  52.3 0.0 copy-done.2
  52.3 25.7 %layer.1 = (bf16[8,768]{1,0:T(8,128)(2,1)}, bf16[16,8,896]{2,1,0:T(8,128)(2,1)S(1)}, bf16[256,768]{1,0:T(8,128)(2,1)S(1)}) custom-call(s32[8]{0:T(128)S(1)} %copy-done.2, s32[8]{0:T(128)S(1)} %copy-done.3, bf16[1024,768]{1,0:T(8,128)(2,1)S(1)} %bitcast.8, f32[768]{0:T(1024)S(1)} %copy-done.1, bf16[4,48,1152]{2,1,0:T(8,128)(2,1)S(1)} %slice.8.refs_0_, ...), custom_call_target="tpu_custom_call" | custom-call | tf_op jit(solution)/shard_map/layer/pallas_call | solution.py:245
  78.0 12.7 %all_to_all.5.near_ref = bf16[16,8,896]{2,1,0:T(8,128)(2,1)S(1)} all-to-all(bf16[16,8,896]{2,1,0:T(8,128)(2,1)S(1)} %get-tuple-element.16), channel_id=1, replica_groups={{0,2,4,6,8,10,12,14,16,18,20,22,24,26,28,30},{1,3,5,7,9,11,13,15,17,19,..., dimensions={0} | all-to-all | bytes 458752 | tf_op jit(solution)/shard_map/all_to_all | solution.py:369
  90.7 2.3 %collective-permute-start.18 = (bf16[16,8,896]{2,1,0:T(8,128)(2,1)S(1)}, bf16[16,8,896]{2,1,0:T(8,128)(2,1)S(1)}, u32[]{:S(2)}, u32[]{:S(2)}) collective-permute-start(bf16[16,8,896]{2,1,0:T(8,128)(2,1)S(1)} %all_to_all.5.near_ref), channel_id=1, source_target_pairs={{1,0},{0,1},{3,2},{2,3},{5,4},{4,5},{7,6},{6,7},{9,8},{8,9},{11,10... | collective-permute-start | bytes 688136 | tf_op jit(solution)/shard_map/ppermute | solution.py:353
  93.0 1.1 %collective-permute-done.18.far_ref = bf16[16,8,896]{2,1,0:T(8,128)(2,1)S(1)} collective-permute-done((bf16[16,8,896]{2,1,0:T(8,128)(2,1)S(1)}, bf16[16,8,896]{2,1,0:T(8,128)(2,1)S(1)}, u32[]{:S(2)}, u32[]{:S(2)}) %collective-permute-start.18) | collective-permute-done | bytes 229408 | tf_op jit(solution)/shard_map/ppermute | solution.py:353
  94.1 1.9 %contrast.1 = (f32[8,768]{1,0:T(8,128)}, f32[8,768]{1,0:T(8,128)}, f32[1,8]{1,0:T(1,128)}) custom-call(bf16[256,768]{1,0:T(8,128)(2,1)S(1)} %get-tuple-element.15.told_ref, bf16[16,8,896]{2,1,0:T(8,128)(2,1)S(1)} %all_to_all.5.near_ref, bf16[16,8,896]{2,1,0:T(8,128)(2,1)S(1)} %collective-permute-done.18.far_ref), custom_call_target="tpu_custom_call" | custom-call | tf_op jit(solution)/shard_map/contrast/pallas_call | solution.py:327
  (7 shorter events, 0.1 us)
Async XLA Ops:
  1.7 4.3 %collective-permute-start = (bf16[24,1920]{1,0:T(8,128)(2,1)S(1)}, bf16[24,1920]{1,0:T(8,128)(2,1)S(1)}, u32[]{:S(2)}, u32[]{:S(2)}) collective-permute-start(bf16[24,1920]{1,0:T(8,128)(2,1)S(1)} %get-tuple-element.13), channel_id=1, source_target_pairs={{1,0},{0,1},{3,2},{2,3},{5,4},{4,5},{7,6},{6,7},{9,8},{8,9},{11,10... | collective-permute-start | bytes 276488 | tf_op jit(solution)/shard_map/ppermute | solution.py:353
  6.0 10.2 %collective-permute-start.3 = (bf16[48,1920]{1,0:T(8,128)(2,1)S(1)}, bf16[48,1920]{1,0:T(8,128)(2,1)S(1)}, u32[]{:S(2)}, u32[]{:S(2)}) collective-permute-start(bf16[48,1920]{1,0:T(8,128)(2,1)S(1)} %chip.1), channel_id=1, source_target_pairs={{22,0},{23,1},{16,2},{17,3},{18,4},{19,5},{20,6},{21,7},{30,8},{31... | collective-permute-start | bytes 552968 | tf_op jit(solution)/shard_map/ppermute | solution.py:353
  8.4 14.6 %collective-permute-start.2 = (bf16[48,1920]{1,0:T(8,128)(2,1)S(1)}, bf16[48,1920]{1,0:T(8,128)(2,1)S(1)}, u32[]{:S(2)}, u32[]{:S(2)}) collective-permute-start(bf16[48,1920]{1,0:T(8,128)(2,1)S(1)} %chip.1), channel_id=1, source_target_pairs={{4,0},{5,1},{6,2},{7,3},{0,4},{1,5},{2,6},{3,7},{12,8},{13,9},{14,... | collective-permute-start | bytes 552968 | tf_op jit(solution)/shard_map/ppermute | solution.py:353
  11.4 11.7 %collective-permute-start.1 = (bf16[48,1920]{1,0:T(8,128)(2,1)S(1)}, bf16[48,1920]{1,0:T(8,128)(2,1)S(1)}, u32[]{:S(2)}, u32[]{:S(2)}) collective-permute-start(bf16[48,1920]{1,0:T(8,128)(2,1)S(1)} %chip.1), channel_id=1, source_target_pairs={{18,0},{19,1},{20,2},{21,3},{22,4},{23,5},{16,6},{17,7},{26,8},{27... | collective-permute-start | bytes 552968 | tf_op jit(solution)/shard_map/ppermute | solution.py:353
  23.1 29.2 %copy-start = (bf16[8,128,768]{2,1,0:T(8,128)(2,1)S(1)}, bf16[8,128,768]{2,1,0:T(8,128)(2,1)}, u32[]{:S(2)}) copy-start(bf16[8,128,768]{2,1,0:T(8,128)(2,1)} %param.8) | copy-start | bytes 4718596
  23.1 29.2 %copy-start.1 = (f32[768]{0:T(1024)S(1)}, f32[768]{0:T(1024)}, u32[]{:S(2)}) copy-start(f32[768]{0:T(1024)} %gain_ref.1) | copy-start | bytes 9220
  23.1 29.2 %copy-start.2 = (s32[8]{0:T(128)S(1)}, s32[8]{0:T(128)}, u32[]{:S(2)}) copy-start(s32[8]{0:T(128)} %len_ref.1) | copy-start | bytes 100
  23.1 29.2 %copy-start.3 = (s32[8]{0:T(128)S(1)}, s32[8]{0:T(128)}, u32[]{:S(2)}) copy-start(s32[8]{0:T(128)} %positive_ref.1) | copy-start | bytes 100
  23.1 9.1 %collective-permute-start.14 = (bf16[4,48,768]{2,1,0:T(8,128)(2,1)S(1)}, bf16[4,48,768]{2,1,0:T(8,128)(2,1)S(1)}, u32[]{:S(2)}, u32[]{:S(2)}) collective-permute-start(bf16[4,48,768]{2,1,0:T(8,128)(2,1)S(1)} %pad_maximum_fusion.1.refs_8_), channel_id=1, source_target_pairs={{1,0},{0,1},{3,2},{2,3},{5,4},{4,5},{7,6},{6,7},{9,8},{8,9},{11,10... | collective-permute-start | bytes 884744 | tf_op jit(solution)/shard_map/ppermute | solution.py:353
  24.8 11.8 %collective-permute-start.13 = (bf16[4,48,768]{2,1,0:T(8,128)(2,1)S(1)}, bf16[4,48,768]{2,1,0:T(8,128)(2,1)S(1)}, u32[]{:S(2)}, u32[]{:S(2)}) collective-permute-start(bf16[4,48,768]{2,1,0:T(8,128)(2,1)S(1)} %pad_maximum_fusion.1.refs_8_), channel_id=1, source_target_pairs={{2,0},{3,1},{0,2},{1,3},{6,4},{7,5},{4,6},{5,7},{10,8},{11,9},{8,1... | collective-permute-start | bytes 884744 | tf_op jit(solution)/shard_map/ppermute | solution.py:353
  29.3 9.4 %collective-permute-start.12 = (bf16[4,48,768]{2,1,0:T(8,128)(2,1)S(1)}, bf16[4,48,768]{2,1,0:T(8,128)(2,1)S(1)}, u32[]{:S(2)}, u32[]{:S(2)}) collective-permute-start(bf16[4,48,768]{2,1,0:T(8,128)(2,1)S(1)} %pad_maximum_fusion.1.refs_8_), channel_id=1, source_target_pairs={{24,0},{25,1},{26,2},{27,3},{28,4},{29,5},{30,6},{31,7},{0,8},{1,9... | collective-permute-start | bytes 884744 | tf_op jit(solution)/shard_map/ppermute | solution.py:353
  29.4 11.3 %collective-permute-start.11 = (bf16[4,48,768]{2,1,0:T(8,128)(2,1)S(1)}, bf16[4,48,768]{2,1,0:T(8,128)(2,1)S(1)}, u32[]{:S(2)}, u32[]{:S(2)}) collective-permute-start(bf16[4,48,768]{2,1,0:T(8,128)(2,1)S(1)} %pad_maximum_fusion.1.refs_8_), channel_id=1, source_target_pairs={{8,0},{9,1},{10,2},{11,3},{12,4},{13,5},{14,6},{15,7},{16,8},{17,9... | collective-permute-start | bytes 884744 | tf_op jit(solution)/shard_map/ppermute | solution.py:353
  32.1 13.9 %collective-permute-start.6 = (bf16[4,48,1152]{2,1,0:T(8,128)(2,1)S(1)}, bf16[4,48,1152]{2,1,0:T(8,128)(2,1)S(1)}, u32[]{:S(2)}, u32[]{:S(2)}) collective-permute-start(bf16[4,48,1152]{2,1,0:T(8,128)(2,1)S(1)} %slice.8.refs_0_), channel_id=1, source_target_pairs={{2,0},{3,1},{0,2},{1,3},{6,4},{7,5},{4,6},{5,7},{10,8},{11,9},{8,1... | collective-permute-start | bytes 1327112 | tf_op jit(solution)/shard_map/ppermute | solution.py:353
  32.2 16.0 %collective-permute-start.5 = (bf16[4,48,1152]{2,1,0:T(8,128)(2,1)S(1)}, bf16[4,48,1152]{2,1,0:T(8,128)(2,1)S(1)}, u32[]{:S(2)}, u32[]{:S(2)}) collective-permute-start(bf16[4,48,1152]{2,1,0:T(8,128)(2,1)S(1)} %slice.8.refs_0_), channel_id=1, source_target_pairs={{24,0},{25,1},{26,2},{27,3},{28,4},{29,5},{30,6},{31,7},{0,8},{1,9... | collective-permute-start | bytes 1327112 | tf_op jit(solution)/shard_map/ppermute | solution.py:353
  36.5 12.9 %collective-permute-start.4 = (bf16[4,48,1152]{2,1,0:T(8,128)(2,1)S(1)}, bf16[4,48,1152]{2,1,0:T(8,128)(2,1)S(1)}, u32[]{:S(2)}, u32[]{:S(2)}) collective-permute-start(bf16[4,48,1152]{2,1,0:T(8,128)(2,1)S(1)} %slice.8.refs_0_), channel_id=1, source_target_pairs={{8,0},{9,1},{10,2},{11,3},{12,4},{13,5},{14,6},{15,7},{16,8},{17,9... | collective-permute-start | bytes 1327112 | tf_op jit(solution)/shard_map/ppermute | solution.py:353
  38.7 10.7 %collective-permute-start.7 = (bf16[4,48,1152]{2,1,0:T(8,128)(2,1)S(1)}, bf16[4,48,1152]{2,1,0:T(8,128)(2,1)S(1)}, u32[]{:S(2)}, u32[]{:S(2)}) collective-permute-start(bf16[4,48,1152]{2,1,0:T(8,128)(2,1)S(1)} %slice.8.refs_0_), channel_id=1, source_target_pairs={{1,0},{0,1},{3,2},{2,3},{5,4},{4,5},{7,6},{6,7},{9,8},{8,9},{11,10... | collective-permute-start | bytes 1327112 | tf_op jit(solution)/shard_map/ppermute | solution.py:353
  40.7 9.2 %collective-permute-start.17 = (bf16[4,48,768]{2,1,0:T(8,128)(2,1)S(1)}, bf16[4,48,768]{2,1,0:T(8,128)(2,1)S(1)}, u32[]{:S(2)}, u32[]{:S(2)}) collective-permute-start(bf16[4,48,768]{2,1,0:T(8,128)(2,1)S(1)} %collective-permute-done.13.refs_11_), channel_id=1, source_target_pairs={{1,0},{0,1},{3,2},{2,3},{5,4},{4,5},{7,6},{6,7},{9,8},{8,9},{11,10... | collective-permute-start | bytes 884744 | tf_op jit(solution)/shard_map/ppermute | solution.py:353
  46.0 6.3 %collective-permute-start.10 = (bf16[4,48,1152]{2,1,0:T(8,128)(2,1)S(1)}, bf16[4,48,1152]{2,1,0:T(8,128)(2,1)S(1)}, u32[]{:S(2)}, u32[]{:S(2)}) collective-permute-start(bf16[4,48,1152]{2,1,0:T(8,128)(2,1)S(1)} %collective-permute-done.6.refs_3_), channel_id=1, source_target_pairs={{1,0},{0,1},{3,2},{2,3},{5,4},{4,5},{7,6},{6,7},{9,8},{8,9},{11,10... | collective-permute-start | bytes 1327112 | tf_op jit(solution)/shard_map/ppermute | solution.py:353
  48.2 4.1 %collective-permute-start.9 = (bf16[4,48,1152]{2,1,0:T(8,128)(2,1)S(1)}, bf16[4,48,1152]{2,1,0:T(8,128)(2,1)S(1)}, u32[]{:S(2)}, u32[]{:S(2)}) collective-permute-start(bf16[4,48,1152]{2,1,0:T(8,128)(2,1)S(1)} %collective-permute-done.5.refs_2_), channel_id=1, source_target_pairs={{1,0},{0,1},{3,2},{2,3},{5,4},{4,5},{7,6},{6,7},{9,8},{8,9},{11,10... | collective-permute-start | bytes 1327112 | tf_op jit(solution)/shard_map/ppermute | solution.py:353
  49.4 2.9 %collective-permute-start.8 = (bf16[4,48,1152]{2,1,0:T(8,128)(2,1)S(1)}, bf16[4,48,1152]{2,1,0:T(8,128)(2,1)S(1)}, u32[]{:S(2)}, u32[]{:S(2)}) collective-permute-start(bf16[4,48,1152]{2,1,0:T(8,128)(2,1)S(1)} %collective-permute-done.4.refs_1_), channel_id=1, source_target_pairs={{1,0},{0,1},{3,2},{2,3},{5,4},{4,5},{7,6},{6,7},{9,8},{8,9},{11,10... | collective-permute-start | bytes 1327112 | tf_op jit(solution)/shard_map/ppermute | solution.py:353
  49.4 2.5 %collective-permute-start.16 = (bf16[4,48,768]{2,1,0:T(8,128)(2,1)S(1)}, bf16[4,48,768]{2,1,0:T(8,128)(2,1)S(1)}, u32[]{:S(2)}, u32[]{:S(2)}) collective-permute-start(bf16[4,48,768]{2,1,0:T(8,128)(2,1)S(1)} %collective-permute-done.12.refs_10_), channel_id=1, source_target_pairs={{1,0},{0,1},{3,2},{2,3},{5,4},{4,5},{7,6},{6,7},{9,8},{8,9},{11,10... | collective-permute-start | bytes 884744 | tf_op jit(solution)/shard_map/ppermute | solution.py:353
  49.9 2.4 %collective-permute-start.15 = (bf16[4,48,768]{2,1,0:T(8,128)(2,1)S(1)}, bf16[4,48,768]{2,1,0:T(8,128)(2,1)S(1)}, u32[]{:S(2)}, u32[]{:S(2)}) collective-permute-start(bf16[4,48,768]{2,1,0:T(8,128)(2,1)S(1)} %collective-permute-done.11.refs_9_), channel_id=1, source_target_pairs={{1,0},{0,1},{3,2},{2,3},{5,4},{4,5},{7,6},{6,7},{9,8},{8,9},{11,10... | collective-permute-start | bytes 884744 | tf_op jit(solution)/shard_map/ppermute | solution.py:353
  90.7 3.4 %collective-permute-start.18 = (bf16[16,8,896]{2,1,0:T(8,128)(2,1)S(1)}, bf16[16,8,896]{2,1,0:T(8,128)(2,1)S(1)}, u32[]{:S(2)}, u32[]{:S(2)}) collective-permute-start(bf16[16,8,896]{2,1,0:T(8,128)(2,1)S(1)} %all_to_all.5.near_ref), channel_id=1, source_target_pairs={{1,0},{0,1},{3,2},{2,3},{5,4},{4,5},{7,6},{6,7},{9,8},{8,9},{11,10... | collective-permute-start | bytes 688136 | tf_op jit(solution)/shard_map/ppermute | solution.py:353
